TPU v7x, 32 devices: a whole 2x2x4 slice. The times are simulated.
32 devices in a mesh: dom: 4 (over z), sub: 8 (over y, x, core).
Axes of the slice: x: 2, y: 2, z: 4, core: 2. Of those that a mesh axis runs over, the one named last changes fastest.
Arguments:
- blocks: bfloat16 [7168, 128, 128], P(('dom', 'sub')), may hold values from -0.1875 to 0.1875
- vectors: bfloat16 [16, 131072], P(None, ('dom', 'sub')), may hold values from -205 to 205, as said below
- col_index: int32 [32, 224], P(('dom', 'sub')), may hold values from 0 to 47, as said below
- row_ptr: int32 [32, 33], P(('dom', 'sub')), may hold values from 0 to 224, as said below
- send_list: int32 [32, 8, 2], P(('dom', 'sub')), may hold values from 0 to 31
Outputs:
- new_basis: float32 [16, 131072], P(None, ('dom', 'sub'))
- upper_factor: float32 [16, 16], replicated
- gain: float32 [16], replicated
Inputs may be any that keep to these rules, and one draw needn't show every extreme that they name: `col_index`: every stored block row holds 5 or 9 blocks, half of each device's rows 9. Its first three columns are its own row, the next and the previous own row (cyclically within the device); the rest are distinct ghost slots, and every ghost slot of every device is used by some block. `row_ptr`: each device's row pointers start at 0, rise by 5 or 9, and end at 224. `vectors`: rows and columns have unlike scales.
All inputs are finite; a program needn't handle non-finite values.
Results may differ from a plain program's by a relative error of at most 0.0028.
Values may be sent and summed in bfloat16 or wider, within the bound.
No kernel may reach another device: no remote copies, remote signals or barrier semaphores. Data moves between devices by JAX's collectives and lax.ppermute only.
A program may use at most 64 MiB of HBM per device.

v0:
```python
import jax
import jax.numpy as jnp
from jax import lax
from jax.sharding import PartitionSpec as P

B = 128
K = 16


def shifted(array, axis, by):
    count = lax.axis_size(axis)
    return lax.ppermute(array, axis, [(i, (i + by) % count) for i in range(count)])


def local(blocks, vectors, col_index, row_ptr, send_list):
    row_blocks = vectors.shape[1] // B
    n_outer = lax.axis_size("dom")
    n_inner = lax.axis_size("sub")
    devices = n_outer * n_inner
    ghost_count = send_list.shape[2]
    neighbour_count = send_list.shape[1]
    slot_count = neighbour_count * ghost_count
    pairs = [
        (outer_step, inner_step)
        for outer_step in (-1, 0, 1)
        for inner_step in (-1, 0, 1)
        if outer_step != 0 or inner_step != 0
    ]
    local_rows = jnp.transpose(vectors.reshape(K, row_blocks, B), (1, 0, 2))
    send_rows = send_list[0].reshape(-1)
    outgoing = jnp.take(local_rows, send_rows, axis=0).reshape(neighbour_count, ghost_count, K, B)
    holding = {}
    for inner_step in (-1, 1):
        bundle = jnp.stack(
            [outgoing[pairs.index((outer_step, inner_step))] for outer_step in (-1, 0, 1)], axis=0
        )
        moved = shifted(bundle, ("dom", "sub"), inner_step)
        for position, outer_step in enumerate((-1, 0, 1)):
            holding[outer_step, inner_step] = moved[position]
    for outer_step in (-1, 1):
        bundle = jnp.stack(
            [
                holding[outer_step, -1],
                outgoing[pairs.index((outer_step, 0))],
                holding[outer_step, 1],
            ],
            axis=0,
        )
        moved = shifted(bundle, ("dom", "sub"), outer_step * n_inner)
        for position, inner_step in enumerate((-1, 0, 1)):
            holding[outer_step, inner_step] = moved[position]
    arrived = jnp.stack([holding[pair] for pair in pairs], axis=0)
    combined = jnp.concatenate([local_rows, arrived.reshape(slot_count, K, B)], axis=0)
    columns = col_index[0]
    stored = columns.shape[0]
    entries = jnp.arange(stored, dtype=jnp.int32)
    starts = row_ptr[0]
    row_of = jnp.sum((starts[1:-1][None, :] <= entries[:, None]).astype(jnp.int32), axis=1)
    picked = jnp.take(combined, columns, axis=0)
    products = jnp.einsum("nke,nce->nkc", picked, blocks, preferred_element_type=jnp.float32)
    image_sums = jax.ops.segment_sum(
        products, row_of, num_segments=row_blocks, indices_are_sorted=True
    )
    image_rows = lax.optimization_barrier(image_sums.astype(jnp.bfloat16))
    squares = jnp.sum(jnp.square(image_rows.astype(jnp.float32)), axis=(0, 2))
    gain_sums = lax.psum(squares, ("dom", "sub"))
    rows_here = jnp.take(image_rows, row_of, axis=0)
    partial_terms = jnp.einsum(
        "nkc,ncb->nkb", rows_here, blocks, preferred_element_type=jnp.float32
    )
    spread = jax.ops.segment_sum(partial_terms, columns, num_segments=row_blocks + slot_count)
    returns = spread[row_blocks:].reshape(neighbour_count, ghost_count, K, B)
    back_holding = {}
    for outer_step in (-1, 1):
        bundle = jnp.stack(
            [returns[pairs.index((outer_step, inner_step))] for inner_step in (-1, 0, 1)], axis=0
        )
        moved = shifted(bundle, ("dom", "sub"), -outer_step * n_inner)
        for position, inner_step in enumerate((-1, 0, 1)):
            back_holding[outer_step, inner_step] = moved[position]
    for inner_step in (-1, 1):
        bundle = jnp.stack(
            [
                back_holding[-1, inner_step],
                returns[pairs.index((0, inner_step))],
                back_holding[1, inner_step],
            ],
            axis=0,
        )
        moved = shifted(bundle, ("dom", "sub"), -inner_step)
        for position, outer_step in enumerate((-1, 0, 1)):
            back_holding[outer_step, inner_step] = moved[position]
    returned = jnp.stack([back_holding[pair] for pair in pairs], axis=0)
    owned = spread[:row_blocks] + jax.ops.segment_sum(
        returned.reshape(slot_count, K, B), send_rows, num_segments=row_blocks
    )
    adjoint = jnp.transpose(owned, (1, 0, 2)).reshape(K, row_blocks * B)
    gram_local = jnp.dot(adjoint, adjoint.T, precision=lax.Precision.HIGHEST)
    gram_total = lax.psum(gram_local, ("dom", "sub"))
    total_rows = row_blocks * B * devices
    lower_factor = jnp.linalg.cholesky(gram_total / total_rows)
    new_basis = lax.linalg.triangular_solve(lower_factor, adjoint, left_side=True, lower=True)
    return (new_basis, lower_factor.T, gain_sums / total_rows)


def solution(mesh):
    return jax.shard_map(
        local,
        mesh=mesh,
        in_specs=(
            P(("dom", "sub"), None, None),
            P(None, ("dom", "sub")),
            P(("dom", "sub"), None),
            P(("dom", "sub"), None),
            P(("dom", "sub"), None, None),
        ),
        out_specs=(P(None, ("dom", "sub")), P(), P()),
        check_vma=False,
    )
```

profile of v0, /device:TPU:0, one launch (start us, length us, event | category | flops | bytes accessed | tf_op | source)
XLA Modules:
  0.0 113.1 jit_solution(10295912849791566675)
XLA Ops:
  0.6 0.8 copy.30
  2.4 6.4 %collective-permute-start = (bf16[3,2,16,128]{3,2,1,0:T(8,128)(2,1)S(1)}, bf16[3,2,16,128]{3,2,1,0:T(8,128)(2,1)S(1)}, u32[]{:S(2)}, u32[]{:S(2)}) collective-permute-start(bf16[3,2,16,128]{3,2,1,0:T(8,128)(2,1)S(1)} %pad_maximum_fusion.6), channel_id=1, source_target_pairs={{0,31},{1,0},{2,1},{3,2},{4,3},{5,4},{6,5},{7,6},{8,7},{9,8},{10,9... | collective-permute-start | bytes 73736 | tf_op jit(solution)/shard_map/ppermute | solution.py:12
  8.8 0.7 slice_bitcast_fusion.16
  10.3 0.7 compare_and_fusion.1
  11.0 4.6 %collective-permute-done.1 = bf16[3,2,16,128]{3,2,1,0:T(8,128)(2,1)S(1)} collective-permute-done((bf16[3,2,16,128]{3,2,1,0:T(8,128)(2,1)S(1)}, bf16[3,2,16,128]{3,2,1,0:T(8,128)(2,1)S(1)}, u32[]{:S(2)}, u32[]{:S(2)}) %collective-permute-start.1) | collective-permute-done | bytes 24608 | tf_op jit(solution)/shard_map/ppermute | solution.py:12
  15.7 2.0 %collective-permute-start.3 = (bf16[3,2,16,128]{3,2,1,0:T(8,128)(2,1)S(1)}, bf16[3,2,16,128]{3,2,1,0:T(8,128)(2,1)S(1)}, u32[]{:S(2)}, u32[]{:S(2)}) collective-permute-start(bf16[3,2,16,128]{3,2,1,0:T(8,128)(2,1)S(1)} %pad_maximum_fusion.9), channel_id=1, source_target_pairs={{0,8},{1,9},{2,10},{3,11},{4,12},{5,13},{6,14},{7,15},{8,16},{9,17... | collective-permute-start | bytes 73736 | tf_op jit(solution)/shard_map/ppermute | solution.py:12
  17.7 1.8 %collective-permute-done.2 = bf16[3,2,16,128]{3,2,1,0:T(8,128)(2,1)S(1)} collective-permute-done((bf16[3,2,16,128]{3,2,1,0:T(8,128)(2,1)S(1)}, bf16[3,2,16,128]{3,2,1,0:T(8,128)(2,1)S(1)}, u32[]{:S(2)}, u32[]{:S(2)}) %collective-permute-start.2) | collective-permute-done | bytes 24608 | tf_op jit(solution)/shard_map/ppermute | solution.py:12
  19.5 1.9 %collective-permute-done.3 = bf16[3,2,16,128]{3,2,1,0:T(8,128)(2,1)S(1)} collective-permute-done((bf16[3,2,16,128]{3,2,1,0:T(8,128)(2,1)S(1)}, bf16[3,2,16,128]{3,2,1,0:T(8,128)(2,1)S(1)}, u32[]{:S(2)}, u32[]{:S(2)}) %collective-permute-start.3) | collective-permute-done | bytes 24608 | tf_op jit(solution)/shard_map/ppermute | solution.py:12
  21.5 0.8 gather_fusion.1
  22.3 6.2 %fusion.2 = f32[224,16,128]{2,1,0:T(8,128)S(1)} fusion(bf16[224,128,128]{2,1,0:T(8,128)(2,1)} %param.5, bf16[224,16,128]{2,1,0:T(8,128)(2,1)S(1)} %gather_fusion.1, pred[224]{0:T(512)(128)(4,1)S(1)} %compare_and_fusion.1), kind=kOutput, calls=%fused_computation.9 | convolution fusion | flops 117899264 | bytes 10092768 | tf_op jit(solution)/shard_map/nke,nce->nkc/dot_general | solution.py:60
  28.5 9.2 %scatter_fusion = f32[32,16,128]{2,1,0:T(8,128)S(1)} fusion(f32[32,16,128]{2,1,0:T(8,128)S(1)} %broadcast.135, s32[224]{0:T(256)S(1)} %convert_reduce_fusion, f32[224,16,128]{2,1,0:T(8,128)S(1)} %fusion.2), kind=kCustom, calls=%fused_computation.3 | custom fusion | flops 458752 | bytes 5505920 | tf_op jit(solution)/shard_map/scatter-add | solution.py:61
  37.7 0.8 gather_fusion.2
  38.6 4.3 %fusion = f32[224,16,128]{2,1,0:T(8,128)S(1)} fusion(bf16[224,128,128]{2,1,0:T(8,128)(2,1)} %param.5, bf16[224,16,128]{2,1,0:T(8,128)(2,1)S(1)} %gather_fusion.2, pred[224]{0:T(512)(128)(4,1)S(1)} %compare_and_fusion.2), kind=kOutput, calls=%fused_computation.7 | convolution fusion | flops 117899264 | bytes 10092768 | tf_op jit(solution)/shard_map/nkc,ncb->nkb/dot_general | solution.py:68
  42.9 8.7 %scatter_fusion.1 = f32[48,16,128]{2,1,0:T(8,128)S(1)} fusion(f32[48,16,128]{2,1,0:T(8,128)S(1)} %broadcast_in_dim.38, s32[224]{0:T(256)S(1)} %bitcast.79, f32[224,16,128]{2,1,0:T(8,128)S(1)} %fusion), kind=kCustom, calls=%fused_computation.4 | custom fusion | flops 458752 | bytes 5505920 | tf_op jit(solution)/shard_map/scatter-add | solution.py:71
  51.8 2.0 %collective-permute-start.4 = (f32[3,2,16,128]{3,2,1,0:T(8,128)S(1)}, f32[3,2,16,128]{3,2,1,0:T(8,128)S(1)}, u32[]{:S(2)}, u32[]{:S(2)}) collective-permute-start(f32[3,2,16,128]{3,2,1,0:T(8,128)S(1)} %pad_maximum_fusion.2), channel_id=1, source_target_pairs={{0,8},{1,9},{2,10},{3,11},{4,12},{5,13},{6,14},{7,15},{8,16},{9,17... | collective-permute-start | bytes 147464 | tf_op jit(solution)/shard_map/ppermute | solution.py:12
  53.8 2.1 %collective-permute-done.5 = f32[3,2,16,128]{3,2,1,0:T(8,128)S(1)} collective-permute-done((f32[3,2,16,128]{3,2,1,0:T(8,128)S(1)}, f32[3,2,16,128]{3,2,1,0:T(8,128)S(1)}, u32[]{:S(2)}, u32[]{:S(2)}) %collective-permute-start.5) | collective-permute-done | bytes 49184 | tf_op jit(solution)/shard_map/ppermute | solution.py:12
  55.8 1.9 %collective-permute-done.4 = f32[3,2,16,128]{3,2,1,0:T(8,128)S(1)} collective-permute-done((f32[3,2,16,128]{3,2,1,0:T(8,128)S(1)}, f32[3,2,16,128]{3,2,1,0:T(8,128)S(1)}, u32[]{:S(2)}, u32[]{:S(2)}) %collective-permute-start.4) | collective-permute-done | bytes 49184 | tf_op jit(solution)/shard_map/ppermute | solution.py:12
  57.8 7.1 %collective-permute-done.6 = f32[3,2,16,128]{3,2,1,0:T(8,128)S(1)} collective-permute-done((f32[3,2,16,128]{3,2,1,0:T(8,128)S(1)}, f32[3,2,16,128]{3,2,1,0:T(8,128)S(1)}, u32[]{:S(2)}, u32[]{:S(2)}) %collective-permute-start.6) | collective-permute-done | bytes 49184 | tf_op jit(solution)/shard_map/ppermute | solution.py:12
  65.1 1.6 %collective-permute-done.7 = f32[3,2,16,128]{3,2,1,0:T(8,128)S(1)} collective-permute-done((f32[3,2,16,128]{3,2,1,0:T(8,128)S(1)}, f32[3,2,16,128]{3,2,1,0:T(8,128)S(1)}, u32[]{:S(2)}, u32[]{:S(2)}) %collective-permute-start.7) | collective-permute-done | bytes 49184 | tf_op jit(solution)/shard_map/ppermute | solution.py:12
  66.7 1.1 scatter_fusion.2
  68.3 38.3 %all-reduce = (f32[16,16]{0,1:T(8,128)S(1)}, f32[16]{0:T(128)S(1)}) all-reduce(f32[16,16]{0,1:T(8,128)S(1)} %convolution_bitcast_fusion, f32[16]{0:T(128)S(1)} %multiply_reduce_fusion), channel_id=1, replica_groups=mesh['dom'=4,'sub'=8] {'dom','sub'}, use_global_device_ids=true, to_apply=%region_4.5 | all-reduce | flops 272 | bytes 2176 | tf_op jit(solution)/shard_map/psum | solution.py:99
  106.7 1.5 %cholesky.16 = f32[16,16]{1,0:T(8,128)S(1)} custom-call(f32[16,16]{1,0:T(8,128)S(1)} %fusion.13), custom_call_target="Cholesky" | custom-call | tf_op jit(solution)/shard_map/jit(cholesky)/cholesky | solution.py:101
  109.5 1.2 %custom-call.6 = f32[1,16,16]{1,2,0:T(8,128)S(1)} custom-call(f32[1,16,16]{2,1,0:T(8,128)S(1)} %get-tuple-element.44), custom_call_target="InvertDiagBlocksLowerTriangular" | custom-call | tf_op jit(solution)/shard_map/triangular_solve | solution.py:102
  110.8 1.1 %fusion.8 = f32[16,4096]{1,0:T(8,128)} fusion(f32[1,16,16]{1,2,0:T(8,128)S(1)} %custom-call.6, f32[32,16,128]{2,1,0:T(8,128)S(1)} %scatter_fusion.2), kind=kOutput, calls=%fused_computation.15 | convolution fusion | flops 12582912 | bytes 525312 | tf_op jit(solution)/shard_map/triangular_solve | solution.py:102
  (61 shorter events, 5.3 us)
Async XLA Ops:
  0.6 1.0 copy-start
  2.4 8.7 %collective-permute-start = (bf16[3,2,16,128]{3,2,1,0:T(8,128)(2,1)S(1)}, bf16[3,2,16,128]{3,2,1,0:T(8,128)(2,1)S(1)}, u32[]{:S(2)}, u32[]{:S(2)}) collective-permute-start(bf16[3,2,16,128]{3,2,1,0:T(8,128)(2,1)S(1)} %pad_maximum_fusion.6), channel_id=1, source_target_pairs={{0,31},{1,0},{2,1},{3,2},{4,3},{5,4},{6,5},{7,6},{8,7},{9,8},{10,9... | collective-permute-start | bytes 73736 | tf_op jit(solution)/shard_map/ppermute | solution.py:12
  8.8 6.8 %collective-permute-start.1 = (bf16[3,2,16,128]{3,2,1,0:T(8,128)(2,1)S(1)}, bf16[3,2,16,128]{3,2,1,0:T(8,128)(2,1)S(1)}, u32[]{:S(2)}, u32[]{:S(2)}) collective-permute-start(bf16[3,2,16,128]{3,2,1,0:T(8,128)(2,1)S(1)} %pad_maximum_fusion.7), channel_id=1, source_target_pairs={{0,1},{1,2},{2,3},{3,4},{4,5},{5,6},{6,7},{7,8},{8,9},{9,10},{10,1... | collective-permute-start | bytes 73736 | tf_op jit(solution)/shard_map/ppermute | solution.py:12
  15.7 3.9 %collective-permute-start.2 = (bf16[3,2,16,128]{3,2,1,0:T(8,128)(2,1)S(1)}, bf16[3,2,16,128]{3,2,1,0:T(8,128)(2,1)S(1)}, u32[]{:S(2)}, u32[]{:S(2)}) collective-permute-start(bf16[3,2,16,128]{3,2,1,0:T(8,128)(2,1)S(1)} %pad_maximum_fusion.8), channel_id=1, source_target_pairs={{0,24},{1,25},{2,26},{3,27},{4,28},{5,29},{6,30},{7,31},{8,0},{9,1... | collective-permute-start | bytes 73736 | tf_op jit(solution)/shard_map/ppermute | solution.py:12
  15.7 5.7 %collective-permute-start.3 = (bf16[3,2,16,128]{3,2,1,0:T(8,128)(2,1)S(1)}, bf16[3,2,16,128]{3,2,1,0:T(8,128)(2,1)S(1)}, u32[]{:S(2)}, u32[]{:S(2)}) collective-permute-start(bf16[3,2,16,128]{3,2,1,0:T(8,128)(2,1)S(1)} %pad_maximum_fusion.9), channel_id=1, source_target_pairs={{0,8},{1,9},{2,10},{3,11},{4,12},{5,13},{6,14},{7,15},{8,16},{9,17... | collective-permute-start | bytes 73736 | tf_op jit(solution)/shard_map/ppermute | solution.py:12
  38.6 4.4 %copy-start.1 = (s32[1,224]{1,0:T(1,128)S(1)}, s32[1,224]{1,0:T(1,128)}, u32[]{:S(2)}) copy-start(s32[1,224]{1,0:T(1,128)} %param.7) | copy-start | bytes 2692
  51.7 4.1 %collective-permute-start.5 = (f32[3,2,16,128]{3,2,1,0:T(8,128)S(1)}, f32[3,2,16,128]{3,2,1,0:T(8,128)S(1)}, u32[]{:S(2)}, u32[]{:S(2)}) collective-permute-start(f32[3,2,16,128]{3,2,1,0:T(8,128)S(1)} %pad_maximum_fusion.3), channel_id=1, source_target_pairs={{0,24},{1,25},{2,26},{3,27},{4,28},{5,29},{6,30},{7,31},{8,0},{9,1... | collective-permute-start | bytes 147464 | tf_op jit(solution)/shard_map/ppermute | solution.py:12
  51.8 5.9 %collective-permute-start.4 = (f32[3,2,16,128]{3,2,1,0:T(8,128)S(1)}, f32[3,2,16,128]{3,2,1,0:T(8,128)S(1)}, u32[]{:S(2)}, u32[]{:S(2)}) collective-permute-start(f32[3,2,16,128]{3,2,1,0:T(8,128)S(1)} %pad_maximum_fusion.2), channel_id=1, source_target_pairs={{0,8},{1,9},{2,10},{3,11},{4,12},{5,13},{6,14},{7,15},{8,16},{9,17... | collective-permute-start | bytes 147464 | tf_op jit(solution)/shard_map/ppermute | solution.py:12
  57.7 7.2 %collective-permute-start.6 = (f32[3,2,16,128]{3,2,1,0:T(8,128)S(1)}, f32[3,2,16,128]{3,2,1,0:T(8,128)S(1)}, u32[]{:S(2)}, u32[]{:S(2)}) collective-permute-start(f32[3,2,16,128]{3,2,1,0:T(8,128)S(1)} %pad_maximum_fusion.4), channel_id=1, source_target_pairs={{0,1},{1,2},{2,3},{3,4},{4,5},{5,6},{6,7},{7,8},{8,9},{9,10},{10,1... | collective-permute-start | bytes 147464 | tf_op jit(solution)/shard_map/ppermute | solution.py:12
  64.9 1.8 %collective-permute-start.7 = (f32[3,2,16,128]{3,2,1,0:T(8,128)S(1)}, f32[3,2,16,128]{3,2,1,0:T(8,128)S(1)}, u32[]{:S(2)}, u32[]{:S(2)}) collective-permute-start(f32[3,2,16,128]{3,2,1,0:T(8,128)S(1)} %pad_maximum_fusion.5), channel_id=1, source_target_pairs={{0,31},{1,0},{2,1},{3,2},{4,3},{5,4},{6,5},{7,6},{8,7},{9,8},{10,9... | collective-permute-start | bytes 147464 | tf_op jit(solution)/shard_map/ppermute | solution.py:12
where the time goes:
time: 114 us; the launch traced here: 113 us
  blocking collectives  38.3 us (34%)
  other arithmetic  25.4 us (22%)
  waiting for transfers between devices  20.9 us (18%)
  matrix products  12.1 us (11%)
  starting transfers between devices  10.7 us (9%)
  local copies, waits for them, and re-layouts  4.8 us (4%)
    psum x1, blocking collectives, local(): gram_total = lax.psum(gram_local, ('dom', 'sub'))  38.3 us
    ppermute x8, waiting for transfers between devices, shifted(): lax.ppermute(array, axis, [(i, (i + by) % count) for i in range(count)])  20.9 us
    ppermute x8, starting transfers between devices, shifted(): lax.ppermute(array, axis, [(i, (i + by) % count) for i in range(count)])  10.7 us
    scatter-add x1, other arithmetic, local(): jax.ops.segment_sum(products, row_of, num_segments=row_blocks, indices_ar...  9.2 us
    scatter-add x1, other arithmetic, local(): jax.ops.segment_sum(partial_terms, columns, num_segments=row_blocks + slo...  8.72 us
    dot_general x1, matrix products, local(): jnp.einsum('nke,nce->nkc', picked, blocks, preferred_element_type=jnp.flo...  6.17 us
    dot_general x1, matrix products, local(): jnp.einsum('nkc,ncb->nkb', rows_here, blocks, preferred_element_type=jnp....  4.33 us
  transfers between devices with their start and end apart: 8, of which 7 were waited for; matrix products, arithmetic and copies ran while one was open for 2% of the time, Pallas kernels for 0%

commit v1 on v0

v1 whole, which is shorter than its diff:
```python
import functools

import jax
import jax.numpy as jnp
from jax import lax
from jax.experimental import pallas as pl
from jax.experimental.pallas import tpu as pltpu
from jax.sharding import PartitionSpec as P

AXES = ("dom", "sub")
B = 128
SHORT = 5
LONG = 9
LOCAL = 3
F32 = jnp.float32
BF16 = jnp.bfloat16
BY_LAST = (((1,), (1,)), ((), ()))
BY_FIRST = (((1,), (0,)), ((), ()))
VMEM = pl.BlockSpec(memory_space=pltpu.VMEM)
SMEM = pl.BlockSpec(memory_space=pltpu.SMEM)
LIMIT = 40 * 2**20


def neighbour(a, b):
    place = (a + 1) * 3 + b + 1
    return place - (place > 4)


def outward():
    return 2 * lax.rem(lax.axis_index("sub"), 2) - 1


def columns(block_row):
    return pl.ds(pl.multiple_of(block_row * B, B), B)


def joined(ref, places, axis):
    return jnp.concatenate([ref[place] for place in places], axis=axis)


def sent(s):
    return (
        ((0, -s), (1, -s), (-1, -s)),
        ((0, s),),
        ((s, s),),
        ((-s, s),),
        ((1, 0),),
        ((-1, 0),),
    )


def received(s):
    return (
        ((0, s),),
        ((0, -s),),
        ((-s, -s),),
        ((s, -s),),
        ((1, 0), (1, s)),
        ((-1, 0), (-1, s)),
    )


def exchange(pair, side, outer, inner, up, down):
    n_inner = lax.axis_size("sub")
    devices = lax.axis_size("dom") * n_inner

    def move(array, odd, even):
        return lax.ppermute(
            array,
            AXES,
            [(d, (d + (odd if d % 2 else even)) % devices) for d in range(devices)],
        )

    pair = move(pair, -1, 1)
    side = move(side, 1, -1)
    outer = move(outer, n_inner + 1, -n_inner - 1)
    inner = move(inner, 1 - n_inner, n_inner - 1)
    up = move(jnp.concatenate([up, pair[1:2]], axis=0), n_inner, n_inner)
    down = move(jnp.concatenate([down, pair[2:3]], axis=0), -n_inner, -n_inner)
    return pair, side, outer, inner, up, down


def gather_kernel(send, vectors, *outgoing):
    for ref, offsets in zip(outgoing, sent(outward())):
        for i, (a, b) in enumerate(offsets):
            for g in range(send.shape[2]):
                ref[i, g] = vectors[:, columns(send[0, neighbour(a, b), g])]


def local_forward_kernel(ptr, vectors, blocks, image):
    rows = image.shape[0]
    for j in range(rows):
        e = ptr[0, j]
        near = [vectors[:, c * B : c * B + B] for c in (j, (j + 1) % rows, (j - 1) % rows)]
        image[j] = lax.dot_general(
            jnp.concatenate(near, axis=1),
            joined(blocks, [e + t for t in range(LOCAL)], 1),
            BY_LAST,
            preferred_element_type=F32,
        )


def ghost_kernel(ptr, col, blocks, partial_image, *refs):
    arrived, image, outgoing = refs[:6], refs[6], refs[7:13]
    ghosts, total, spread, long_rows = refs[13:]
    rows = image.shape[0]
    many = long_rows.shape[0] - 1
    s = outward()
    for ref, offsets in zip(arrived, received(s)):
        for i, (a, b) in enumerate(offsets):
            for g in range(ref.shape[1]):
                ghosts[neighbour(a, b) * ref.shape[1] + g] = ref[i, g]
    found = 0
    for j in range(rows):
        long_rows[jnp.minimum(found, many)] = j
        found = found + (ptr[0, j + 1] - ptr[0, j] > SHORT).astype(jnp.int32)

    def forward(e, first, last):
        return lax.dot_general(
            joined(ghosts, [col[0, e + t] - rows for t in range(first, last)], 1),
            joined(blocks, [e + t for t in range(first, last)], 1),
            BY_LAST,
            preferred_element_type=F32,
        )

    for j in range(rows):
        total[j] = partial_image[j] + forward(ptr[0, j], LOCAL, SHORT)
    for i in range(many):
        j = long_rows[i]
        total[j] += forward(ptr[0, j], SHORT, LONG)
    image[...] = total[...].astype(BF16)
    spread[...] = jnp.zeros_like(spread)
    banks = spread.shape[0]

    def backward(j, first, last):
        e = ptr[0, j]
        terms = lax.dot_general(
            image[j],
            joined(blocks, [e + t for t in range(first, last)], 1),
            BY_FIRST,
            preferred_element_type=F32,
        )
        for t in range(first, last):
            k = t - first
            spread[k % banks, col[0, e + t] - rows] += terms[:, k * B : k * B + B]

    for j in range(rows):
        backward(j, LOCAL, SHORT)
    for i in range(many):
        backward(long_rows[i], SHORT, LONG)
    for ref, offsets in zip(outgoing, sent(s)):
        for i, (a, b) in enumerate(offsets):
            for g in range(ref.shape[1]):
                slot = neighbour(-a, -b) * ref.shape[1] + g
                ref[i, g] = sum(spread[bank, slot] for bank in range(banks))


def local_backward_kernel(ptr, blocks, image, adjoint, squares):
    rows = image.shape[0]
    total = jnp.zeros(squares.shape, F32)
    for j in range(rows):
        before, after = (j - 1) % rows, (j + 1) % rows
        adjoint[:, j * B : j * B + B] = lax.dot_general(
            joined(image, [j, before, after], 1),
            joined(blocks, [ptr[0, j], ptr[0, before] + 1, ptr[0, after] + 2], 0),
            BY_FIRST,
            preferred_element_type=F32,
        )
        wide = image[j].astype(F32)
        total = total + wide * wide
    squares[...] = total


def group_masks(k):
    group = B // k
    row = lax.broadcasted_iota(jnp.int32, (k, B), 0)
    lane = lax.broadcasted_iota(jnp.int32, (k, B), 1)
    return lax.rem(row, group) == lax.div(lane, k), row, lane


def gram_kernel(send, partial_adjoint, squares, *refs):
    arrived, adjoint, packed = refs[:6], refs[6], refs[7]
    k = adjoint.shape[0]
    s = outward()
    adjoint[...] = partial_adjoint[...]
    for ref, offsets in zip(arrived, received(s)):
        for i, (a, b) in enumerate(offsets):
            for g in range(ref.shape[1]):
                place = columns(send[0, neighbour(-a, -b), g])
                adjoint[:, place] += ref[i, g]
    z = adjoint[...]
    gram = lax.dot_general(z, z, BY_LAST, precision=lax.Precision.HIGHEST, preferred_element_type=F32)
    own, row, lane = group_masks(k)
    tile = (lax.rem(lane, k) == row).astype(F32)
    tiled = lax.dot_general(gram, tile, BY_FIRST, precision=lax.Precision.HIGHEST, preferred_element_type=F32)
    tiled = jnp.where(own, tiled, 0.0)
    group = B // k
    lines = [jnp.sum(tiled[i : i + group], axis=0, keepdims=True) for i in range(0, k, group)]
    norms = jnp.sum(squares[...], axis=1, keepdims=True)
    lines.append(jnp.sum(jnp.where(lane == row, norms, 0.0), axis=0, keepdims=True))
    lines.append(jnp.zeros(((-len(lines)) % 4, B), F32))
    packed[...] = jnp.broadcast_to(jnp.concatenate(lines, axis=0)[None], packed.shape)


def solve_kernel(count, packed, adjoint, basis, factor, gain):
    k = adjoint.shape[0]
    group = B // k
    own, row, lane = group_masks(k)
    sums = jnp.sum(packed[...], axis=0) / count
    spread = jnp.concatenate(
        [jnp.broadcast_to(sums[i : i + 1], (group, B)) for i in range(k // group)], axis=0
    )
    line = lax.broadcasted_iota(jnp.int32, (B, B), 0)
    column = lax.broadcasted_iota(jnp.int32, (B, B), 1)
    fold = (lax.rem(line, k) == column).astype(F32)
    both = lax.dot_general(
        jnp.where(own, spread, 0.0), fold, BY_FIRST, precision=lax.Precision.HIGHEST, preferred_element_type=F32
    )
    both = both + (lane == row + k).astype(F32)
    for i in range(k):
        pivots = jnp.broadcast_to(both[:, i : i + 1], (k, B))
        scale = lax.rsqrt(pivots[i : i + 1])
        top = both[i : i + 1] * scale
        lower = both - pivots * scale * top
        both = jnp.where(row > i, lower, jnp.where(row == i, top, both))
    factor[...] = jnp.where(lane >= row, both, 0.0)[:, :k]
    gain[...] = sums[k // group : k // group + 1, :k]
    inverse = both[:, k : 2 * k]
    basis[...] = lax.dot_general(
        inverse, adjoint[...], BY_FIRST, precision=lax.Precision.HIGHEST, preferred_element_type=F32
    )


def call(kernel, name, shapes, in_specs, scratch=(), flops=0, bytes_accessed=0):
    return pl.pallas_call(
        kernel,
        name=name,
        out_shape=[jax.ShapeDtypeStruct(shape, dtype) for shape, dtype in shapes],
        in_specs=in_specs,
        out_specs=[VMEM] * len(shapes),
        scratch_shapes=scratch,
        compiler_params=pltpu.CompilerParams(vmem_limit_bytes=LIMIT),
        cost_estimate=pl.CostEstimate(flops=flops, bytes_accessed=bytes_accessed, transcendentals=0),
    )


def local(blocks, vectors, col_index, row_ptr, send_list):
    k, unknowns = vectors.shape
    rows = unknowns // B
    stored = blocks.shape[0]
    devices = lax.axis_size("dom") * lax.axis_size("sub")
    ghost = send_list.shape[2]
    slots = send_list.shape[1] * ghost
    many = (stored - SHORT * rows) // (LONG - SHORT)
    sizes = (3, 1, 1, 1, 1, 1)
    held = pltpu.with_memory_space_constraint(blocks, pltpu.VMEM)
    outgoing = call(
        gather_kernel,
        "gather",
        [((n, ghost, k, B), BF16) for n in sizes],
        [SMEM, VMEM],
    )(send_list, vectors)
    arrived = exchange(*outgoing)
    (partial_image,) = call(
        local_forward_kernel,
        "local_forward",
        [((rows, k, B), F32)],
        [SMEM, VMEM, VMEM],
        flops=2 * rows * LOCAL * B * B * k,
        bytes_accessed=2 * rows * LOCAL * B * B,
    )(row_ptr, vectors, held)
    image, *returns = call(
        ghost_kernel,
        "ghost",
        [((rows, k, B), BF16)] + [((n, ghost, k, B), F32) for n in sizes],
        [SMEM, SMEM] + [VMEM] * 8,
        scratch=[
            pltpu.VMEM((slots, k, B), BF16),
            pltpu.VMEM((rows, k, B), F32),
            pltpu.VMEM((4, slots, k, B), F32),
            pltpu.SMEM((many + 1,), jnp.int32),
        ],
        flops=4 * (stored - rows * LOCAL) * B * B * k,
        bytes_accessed=4 * (stored - rows * LOCAL) * B * B,
    )(row_ptr, col_index, held, partial_image, *arrived)
    returned = exchange(*returns)
    partial_adjoint, squares = call(
        local_backward_kernel,
        "local_backward",
        [((k, unknowns), F32), ((k, B), F32)],
        [SMEM, VMEM, VMEM],
        flops=2 * rows * LOCAL * B * B * k,
        bytes_accessed=2 * rows * LOCAL * B * B,
    )(row_ptr, held, image)
    adjoint, packed = call(
        gram_kernel,
        "gram",
        [((k, unknowns), F32), ((devices, 4, B), F32)],
        [SMEM] + [VMEM] * 8,
    )(send_list, partial_adjoint, squares, *returned)
    everywhere = lax.all_to_all(packed, AXES, 0, 0)
    basis, factor, gain = call(
        functools.partial(solve_kernel, unknowns * devices),
        "solve",
        [((k, unknowns), F32), ((k, k), F32), ((1, k), F32)],
        [VMEM, VMEM],
    )(everywhere, adjoint)
    return basis, factor, gain[0]


def solution(mesh):
    return jax.shard_map(
        local,
        mesh=mesh,
        in_specs=(
            P(AXES, None, None),
            P(None, AXES),
            P(AXES, None),
            P(AXES, None),
            P(AXES, None, None),
        ),
        out_specs=(P(None, AXES), P(), P()),
        check_vma=False,
    )
```

time: 114 us -> 53.2 us (0.47)
  blocking collectives: 38.3 us -> 11.8 us
  other arithmetic: 25.4 us -> 0.02 us
  waiting for transfers between devices: 20.9 us -> 3.82 us
  matrix products: 12.1 us -> 0 us
  Pallas kernels: 0 us -> 10.2 us
  starting transfers between devices: 10.7 us -> 18.7 us
  local copies, waits for them, and re-layouts: 4.8 us -> 7.6 us
    psum x1 -> x0, blocking collectives: 38.3 us -> none  [local(): gram_total = lax.psum(gram_local, ('dom', 'sub'))]
    scatter-add x3 -> x0, other arithmetic: 19 us -> none  [the longest x1 9.2 us: local(): jax.ops.segment_sum(products, row_of, num_segments=row_blocks, indices_ar...]
    ppermute x8 -> x12, waiting for transfers between devices: 20.9 us -> 3.82 us  [move(): lax.ppermute(array, AXES, [(d, (d + (odd if d % 2 else even)) % devices)...]
    all_to_all x0 -> x1, blocking collectives: none -> 11.8 us  [local(): everywhere = lax.all_to_all(packed, AXES, 0, 0)]
    dot_general x3 -> x0, matrix products: 10.9 us -> none  [the longest x1 6.17 us: local(): jnp.einsum('nke,nce->nkc', picked, blocks, preferred_element_type=jnp.flo...]
    pallas_call x0 -> x6, Pallas kernels: none -> 10.2 us  [the longest x1 2.81 us: local(): call(functools.partial(solve_kernel, unknowns * devices), 'solve', [((k,...]
    ppermute x8 -> x12, starting transfers between devices: 10.7 us -> 18.7 us  [move(): lax.ppermute(array, AXES, [(d, (d + (odd if d % 2 else even)) % devices)...]
    unnamed x12 -> x13, local copies, waits for them, and re-layouts: 1.49 us -> 7.6 us
  transfers between devices with their start and end apart: 8 -> 12, of which waited for: 7 -> 5; matrix products, arithmetic and copies ran while one was open for 2% -> 0% of each run, Pallas kernels for 0% -> 6%
where the time goes in v1:
time: 53.2 us; the launch traced here: 52.9 us
  starting transfers between devices  18.7 us (35%)
  blocking collectives  11.8 us (22%)
  Pallas kernels  10.2 us (19%)
  local copies, waits for them, and re-layouts  7.6 us (14%)
  waiting for transfers between devices  3.82 us (7%)
  between operations  0.72 us (1%)
    ppermute x12, starting transfers between devices, move(): lax.ppermute(array, AXES, [(d, (d + (odd if d % 2 else even)) % devices)...  18.7 us
    all_to_all x1, blocking collectives, local(): everywhere = lax.all_to_all(packed, AXES, 0, 0)  11.8 us
    unnamed x13, local copies, waits for them, and re-layouts  7.6 us
    ppermute x12, waiting for transfers between devices, move(): lax.ppermute(array, AXES, [(d, (d + (odd if d % 2 else even)) % devices)...  3.82 us
    pallas_call x1, Pallas kernels, local(): call(functools.partial(solve_kernel, unknowns * devices), 'solve', [((k,...  2.81 us
    pallas_call x1, Pallas kernels, local(): call(ghost_kernel, 'ghost', [((rows, k, B), BF16)] + [((n, ghost, k, B),...  2.54 us
    pallas_call x1, Pallas kernels, local(): call(local_forward_kernel, 'local_forward', [((rows, k, B), F32)], [SMEM,...  1.73 us
    pallas_call x1, Pallas kernels, local(): call(gram_kernel, 'gram', [((k, unknowns), F32), ((devices, 4, B), F32)],...  1.32 us
  transfers between devices with their start and end apart: 12, of which 5 were waited for; matrix products, arithmetic and copies ran while one was open for 0% of the time, Pallas kernels for 6%

profile of v1, /device:TPU:0, one launch (start us, length us, event | category | flops | bytes accessed | tf_op | source)
XLA Modules:
  0.0 52.9 jit_solution(18183101878284384215)
XLA Ops:
  0.6 0.8 %copy.9.send = s32[1,8,2]{2,1,0:T(8,128)S(1)} copy(s32[1,8,2]{1,2,0:T(2,128)} %param.9) | data formatting | bytes 128 | tf_op args[4]
  1.4 0.9 %copy-done.2 = bf16[16,4096]{1,0:T(8,128)(2,1)S(1)} copy-done((bf16[16,4096]{1,0:T(8,128)(2,1)S(1)}, bf16[16,4096]{1,0:T(8,128)(2,1)}, u32[]{:S(2)}) %copy-start.2) | copy-done | bytes 131096
  3.5 0.8 %collective-permute-done.refs_0_ = bf16[3,2,16,128]{3,2,1,0:T(8,128)(2,1)S(1)} collective-permute-done((bf16[3,2,16,128]{3,2,1,0:T(8,128)(2,1)S(1)}, bf16[3,2,16,128]{3,2,1,0:T(8,128)(2,1)S(1)}, u32[]{:S(2)}, u32[]{:S(2)}) %collective-permute-start) | collective-permute-done | bytes 24608 | tf_op jit(solution)/shard_map/ppermute | solution.py:68
  4.3 2.9 %collective-permute-start.4 = (bf16[2,2,16,128]{3,2,1,0:T(8,128)(2,1)S(1)}, bf16[2,2,16,128]{3,2,1,0:T(8,128)(2,1)S(1)}, u32[]{:S(2)}, u32[]{:S(2)}) collective-permute-start(bf16[2,2,16,128]{3,2,1,0:T(8,128)(2,1)S(1)} %pad_maximum_fusion.2), channel_id=1, source_target_pairs={{0,8},{1,9},{2,10},{3,11},{4,12},{5,13},{6,14},{7,15},{8,16},{9,17... | collective-permute-start | bytes 49160 | tf_op jit(solution)/shard_map/ppermute | solution.py:68
  7.3 2.1 %collective-permute-start.5 = (bf16[2,2,16,128]{3,2,1,0:T(8,128)(2,1)S(1)}, bf16[2,2,16,128]{3,2,1,0:T(8,128)(2,1)S(1)}, u32[]{:S(2)}, u32[]{:S(2)}) collective-permute-start(bf16[2,2,16,128]{3,2,1,0:T(8,128)(2,1)S(1)} %pad_maximum_fusion.3), channel_id=1, source_target_pairs={{0,24},{1,25},{2,26},{3,27},{4,28},{5,29},{6,30},{7,31},{8,0},{9,1... | collective-permute-start | bytes 49160 | tf_op jit(solution)/shard_map/ppermute | solution.py:68
  9.3 3.1 %collective-permute-start.1 = (bf16[1,2,16,128]{3,2,1,0:T(8,128)(2,1)S(1)}, bf16[1,2,16,128]{3,2,1,0:T(8,128)(2,1)S(1)}, u32[]{:S(2)}, u32[]{:S(2)}) collective-permute-start(bf16[1,2,16,128]{3,2,1,0:T(8,128)(2,1)S(1)} %get-tuple-element.24), channel_id=1, source_target_pairs={{0,31},{1,2},{2,1},{3,4},{4,3},{5,6},{6,5},{7,8},{8,7},{9,10},{10,... | collective-permute-start | bytes 24584 | tf_op jit(solution)/shard_map/ppermute | solution.py:68
  12.4 1.0 %collective-permute-start.2 = (bf16[1,2,16,128]{3,2,1,0:T(8,128)(2,1)S(1)}, bf16[1,2,16,128]{3,2,1,0:T(8,128)(2,1)S(1)}, u32[]{:S(2)}, u32[]{:S(2)}) collective-permute-start(bf16[1,2,16,128]{3,2,1,0:T(8,128)(2,1)S(1)} %get-tuple-element.25), channel_id=1, source_target_pairs={{0,23},{1,10},{2,25},{3,12},{4,27},{5,14},{6,29},{7,16},{8,31},{9,... | collective-permute-start | bytes 24584 | tf_op jit(solution)/shard_map/ppermute | solution.py:68
  13.9 3.1 %copy-done = bf16[224,128,128]{2,1,0:T(8,128)(2,1)S(1)} copy-done((bf16[224,128,128]{2,1,0:T(8,128)(2,1)S(1)}, bf16[224,128,128]{2,1,0:T(8,128)(2,1)}, u32[]{:S(2)}) %copy-start) | copy-done | bytes 7340056
  17.0 0.9 %copy-done.3 = bf16[16,4096]{1,0:T(8,128)(2,1)S(1)} copy-done((bf16[16,4096]{1,0:T(8,128)(2,1)S(1)}, bf16[16,4096]{1,0:T(8,128)(2,1)}, u32[]{:S(2)}) %copy-start.3) | copy-done | bytes 131096
  17.9 0.7 %copy-done.4 = s32[1,33]{1,0:T(1,128)S(1)} copy-done((s32[1,33]{1,0:T(1,128)S(1)}, s32[1,33]{1,0:T(1,128)}, u32[]{:S(2)}) %copy-start.4) | copy-done | bytes 156
  18.6 1.7 %local_forward.1.partial_image = f32[32,16,128]{2,1,0:T(8,128)S(1)} custom-call(s32[1,33]{1,0:T(1,128)S(1)} %copy-done.4, bf16[16,4096]{1,0:T(8,128)(2,1)S(1)} %copy-done.3, bf16[224,128,128]{2,1,0:T(8,128)(2,1)S(1)} %copy-done), custom_call_target="tpu_custom_call" | custom-call | flops 50331648 | bytes 3145728 | tf_op jit(solution)/shard_map/local_forward/pallas_call | solution.py:264
  20.4 1.3 %copy-done.1 = bf16[224,128,128]{2,1,0:T(8,128)(2,1)S(1)} copy-done((bf16[224,128,128]{2,1,0:T(8,128)(2,1)S(1)}, bf16[224,128,128]{2,1,0:T(8,128)(2,1)}, u32[]{:S(2)}) %copy-start.1) | copy-done | bytes 7340056
  21.6 2.5 %ghost.1 = (bf16[32,16,128]{2,1,0:T(8,128)(2,1)S(1)}, f32[3,2,16,128]{3,2,1,0:T(8,128)S(1)}, f32[1,2,16,128]{3,2,1,0:T(8,128)S(1)}, f32[1,2,16,128]{3,2,1,0:T(8,...) custom-call(s32[1,33]{1,0:T(1,128)S(1)} %copy-done.4, ...), custom_call_target="tpu_custom_call" | custom-call | flops 134217728 | bytes 8388608 | tf_op jit(solution)/shard_map/ghost/pallas_call | solution.py:272
  24.3 1.2 %collective-permute-done.6.refs_0_ = f32[3,2,16,128]{3,2,1,0:T(8,128)S(1)} collective-permute-done((f32[3,2,16,128]{3,2,1,0:T(8,128)S(1)}, f32[3,2,16,128]{3,2,1,0:T(8,128)S(1)}, u32[]{:S(2)}, u32[]{:S(2)}) %collective-permute-start.6) | collective-permute-done | bytes 49184 | tf_op jit(solution)/shard_map/ppermute | solution.py:68
  25.5 1.6 %collective-permute-start.10 = (f32[2,2,16,128]{3,2,1,0:T(8,128)S(1)}, f32[2,2,16,128]{3,2,1,0:T(8,128)S(1)}, u32[]{:S(2)}, u32[]{:S(2)}) collective-permute-start(f32[2,2,16,128]{3,2,1,0:T(8,128)S(1)} %pad_maximum_fusion), channel_id=1, source_target_pairs={{0,8},{1,9},{2,10},{3,11},{4,12},{5,13},{6,14},{7,15},{8,16},{9,17... | collective-permute-start | bytes 98312 | tf_op jit(solution)/shard_map/ppermute | solution.py:68
  27.1 2.2 %collective-permute-start.11 = (f32[2,2,16,128]{3,2,1,0:T(8,128)S(1)}, f32[2,2,16,128]{3,2,1,0:T(8,128)S(1)}, u32[]{:S(2)}, u32[]{:S(2)}) collective-permute-start(f32[2,2,16,128]{3,2,1,0:T(8,128)S(1)} %pad_maximum_fusion.1), channel_id=1, source_target_pairs={{0,24},{1,25},{2,26},{3,27},{4,28},{5,29},{6,30},{7,31},{8,0},{9,1... | collective-permute-start | bytes 98312 | tf_op jit(solution)/shard_map/ppermute | solution.py:68
  29.4 1.3 %collective-permute-start.7 = (f32[1,2,16,128]{3,2,1,0:T(8,128)S(1)}, f32[1,2,16,128]{3,2,1,0:T(8,128)S(1)}, u32[]{:S(2)}, u32[]{:S(2)}) collective-permute-start(f32[1,2,16,128]{3,2,1,0:T(8,128)S(1)} %get-tuple-element.33), channel_id=1, source_target_pairs={{0,31},{1,2},{2,1},{3,4},{4,3},{5,6},{6,5},{7,8},{8,7},{9,10},{10,... | collective-permute-start | bytes 49160 | tf_op jit(solution)/shard_map/ppermute | solution.py:68
  30.7 2.2 %collective-permute-start.8 = (f32[1,2,16,128]{3,2,1,0:T(8,128)S(1)}, f32[1,2,16,128]{3,2,1,0:T(8,128)S(1)}, u32[]{:S(2)}, u32[]{:S(2)}) collective-permute-start(f32[1,2,16,128]{3,2,1,0:T(8,128)S(1)} %get-tuple-element.34), channel_id=1, source_target_pairs={{0,23},{1,10},{2,25},{3,12},{4,27},{5,14},{6,29},{7,16},{8,31},{9,... | collective-permute-start | bytes 49160 | tf_op jit(solution)/shard_map/ppermute | solution.py:68
  32.9 1.1 %collective-permute-start.9 = (f32[1,2,16,128]{3,2,1,0:T(8,128)S(1)}, f32[1,2,16,128]{3,2,1,0:T(8,128)S(1)}, u32[]{:S(2)}, u32[]{:S(2)}) collective-permute-start(f32[1,2,16,128]{3,2,1,0:T(8,128)S(1)} %get-tuple-element.35), channel_id=1, source_target_pairs={{0,7},{1,26},{2,9},{3,28},{4,11},{5,30},{6,13},{7,0},{8,15},{9,2},... | collective-permute-start | bytes 49160 | tf_op jit(solution)/shard_map/ppermute | solution.py:68
  34.0 1.2 %local_backward.1 = (f32[16,4096]{1,0:T(8,128)S(1)}, f32[16,128]{1,0:T(8,128)S(1)}) custom-call(s32[1,33]{1,0:T(1,128)S(1)} %copy-done.4, bf16[224,128,128]{2,1,0:T(8,128)(2,1)S(1)} %copy-done.1, bf16[32,16,128]{2,1,0:T(8,128)(2,1)S(1)} %get-tuple-element.29.image), custom_call_target="tpu_custom_call" | custom-call | flops 50331648 | bytes 3145728 | tf_op jit(solution)/shard_map/local_backward/pallas_call | solution.py:287
  35.2 0.9 %collective-permute-done.7.refs_1_ = f32[1,2,16,128]{3,2,1,0:T(8,128)S(1)} collective-permute-done((f32[1,2,16,128]{3,2,1,0:T(8,128)S(1)}, f32[1,2,16,128]{3,2,1,0:T(8,128)S(1)}, u32[]{:S(2)}, u32[]{:S(2)}) %collective-permute-start.7) | collective-permute-done | bytes 16416 | tf_op jit(solution)/shard_map/ppermute | solution.py:68
  37.0 1.3 %gram.1 = (f32[16,4096]{1,0:T(8,128)S(1)}, f32[32,4,128]{2,1,0:T(4,128)S(1)}) custom-call(s32[1,8,2]{2,1,0:T(8,128)S(1)} %copy.9.send, f32[16,4096]{1,0:T(8,128)S(1)} %get-tuple-element.30.partial_adjoint, f32[16,128]{1,0:T(8,128)S(1)} %get-tuple-element.31.squares, f32[3,2,16,128]{3,2,1,0:T(8,128)S(1)} %collective-permute-done.6.refs_0_, ...), custom_call_target="tpu_custom_call" | custom-call | tf_op jit(solution)/shard_map/gram/pallas_call | solution.py:295
  38.3 11.8 %all_to_all.5.packed = f32[32,4,128]{2,1,0:T(4,128)S(1)} all-to-all(f32[32,4,128]{2,1,0:T(4,128)S(1)} %get-tuple-element.38), channel_id=1, replica_groups=mesh['dom'=4,'sub'=8] {'dom','sub'}, dimensions={0} | all-to-all | bytes 131072 | tf_op jit(solution)/shard_map/all_to_all | solution.py:301
  50.1 2.8 %solve.1 = (f32[16,4096]{1,0:T(8,128)}, f32[16,16]{1,0:T(8,128)}, f32[1,16]{1,0:T(1,128)}) custom-call(f32[32,4,128]{2,1,0:T(4,128)S(1)} %all_to_all.5.packed, f32[16,4096]{1,0:T(8,128)S(1)} %get-tuple-element.39.adjoint), custom_call_target="tpu_custom_call" | custom-call | tf_op jit(solution)/shard_map/solve/pallas_call | solution.py:302
  (26 shorter events, 2.7 us)
Async XLA Ops:
  0.6 19.7 %copy-start.5 = (s32[1,224]{1,0:T(1,128)S(1)}, s32[1,224]{1,0:T(1,128)}, u32[]{:S(2)}) copy-start(s32[1,224]{1,0:T(1,128)} %col.1) | copy-start | bytes 2692
  1.4 0.9 %copy-start.2 = (bf16[16,4096]{1,0:T(8,128)(2,1)S(1)}, bf16[16,4096]{1,0:T(8,128)(2,1)}, u32[]{:S(2)}) copy-start(bf16[16,4096]{1,0:T(8,128)(2,1)} %vectors.3) | copy-start | bytes 393220
  3.0 1.4 %collective-permute-start = (bf16[3,2,16,128]{3,2,1,0:T(8,128)(2,1)S(1)}, bf16[3,2,16,128]{3,2,1,0:T(8,128)(2,1)S(1)}, u32[]{:S(2)}, u32[]{:S(2)}) collective-permute-start(bf16[3,2,16,128]{3,2,1,0:T(8,128)(2,1)S(1)} %get-tuple-element.23), channel_id=1, source_target_pairs={{0,1},{1,0},{2,3},{3,2},{4,5},{5,4},{6,7},{7,6},{8,9},{9,8},{10,11... | collective-permute-start | bytes 73736 | tf_op jit(solution)/shard_map/ppermute | solution.py:68
  4.3 16.0 %collective-permute-start.4 = (bf16[2,2,16,128]{3,2,1,0:T(8,128)(2,1)S(1)}, bf16[2,2,16,128]{3,2,1,0:T(8,128)(2,1)S(1)}, u32[]{:S(2)}, u32[]{:S(2)}) collective-permute-start(bf16[2,2,16,128]{3,2,1,0:T(8,128)(2,1)S(1)} %pad_maximum_fusion.2), channel_id=1, source_target_pairs={{0,8},{1,9},{2,10},{3,11},{4,12},{5,13},{6,14},{7,15},{8,16},{9,17... | collective-permute-start | bytes 49160 | tf_op jit(solution)/shard_map/ppermute | solution.py:68
  7.3 13.1 %collective-permute-start.5 = (bf16[2,2,16,128]{3,2,1,0:T(8,128)(2,1)S(1)}, bf16[2,2,16,128]{3,2,1,0:T(8,128)(2,1)S(1)}, u32[]{:S(2)}, u32[]{:S(2)}) collective-permute-start(bf16[2,2,16,128]{3,2,1,0:T(8,128)(2,1)S(1)} %pad_maximum_fusion.3), channel_id=1, source_target_pairs={{0,24},{1,25},{2,26},{3,27},{4,28},{5,29},{6,30},{7,31},{8,0},{9,1... | collective-permute-start | bytes 49160 | tf_op jit(solution)/shard_map/ppermute | solution.py:68
  9.3 11.0 %collective-permute-start.1 = (bf16[1,2,16,128]{3,2,1,0:T(8,128)(2,1)S(1)}, bf16[1,2,16,128]{3,2,1,0:T(8,128)(2,1)S(1)}, u32[]{:S(2)}, u32[]{:S(2)}) collective-permute-start(bf16[1,2,16,128]{3,2,1,0:T(8,128)(2,1)S(1)} %get-tuple-element.24), channel_id=1, source_target_pairs={{0,31},{1,2},{2,1},{3,4},{4,3},{5,6},{6,5},{7,8},{8,7},{9,10},{10,... | collective-permute-start | bytes 24584 | tf_op jit(solution)/shard_map/ppermute | solution.py:68
  12.4 7.9 %collective-permute-start.2 = (bf16[1,2,16,128]{3,2,1,0:T(8,128)(2,1)S(1)}, bf16[1,2,16,128]{3,2,1,0:T(8,128)(2,1)S(1)}, u32[]{:S(2)}, u32[]{:S(2)}) collective-permute-start(bf16[1,2,16,128]{3,2,1,0:T(8,128)(2,1)S(1)} %get-tuple-element.25), channel_id=1, source_target_pairs={{0,23},{1,10},{2,25},{3,12},{4,27},{5,14},{6,29},{7,16},{8,31},{9,... | collective-permute-start | bytes 24584 | tf_op jit(solution)/shard_map/ppermute | solution.py:68
  13.4 6.9 %collective-permute-start.3 = (bf16[1,2,16,128]{3,2,1,0:T(8,128)(2,1)S(1)}, bf16[1,2,16,128]{3,2,1,0:T(8,128)(2,1)S(1)}, u32[]{:S(2)}, u32[]{:S(2)}) collective-permute-start(bf16[1,2,16,128]{3,2,1,0:T(8,128)(2,1)S(1)} %get-tuple-element.26), channel_id=1, source_target_pairs={{0,7},{1,26},{2,9},{3,28},{4,11},{5,30},{6,13},{7,0},{8,15},{9,2},... | collective-permute-start | bytes 24584 | tf_op jit(solution)/shard_map/ppermute | solution.py:68
  13.9 3.1 %copy-start = (bf16[224,128,128]{2,1,0:T(8,128)(2,1)S(1)}, bf16[224,128,128]{2,1,0:T(8,128)(2,1)}, u32[]{:S(2)}) copy-start(bf16[224,128,128]{2,1,0:T(8,128)(2,1)} %blocks.5) | copy-start | bytes 22020100
  17.0 0.9 %copy-start.3 = (bf16[16,4096]{1,0:T(8,128)(2,1)S(1)}, bf16[16,4096]{1,0:T(8,128)(2,1)}, u32[]{:S(2)}) copy-start(bf16[16,4096]{1,0:T(8,128)(2,1)} %vectors.3) | copy-start | bytes 393220
  17.9 0.7 %copy-start.4 = (s32[1,33]{1,0:T(1,128)S(1)}, s32[1,33]{1,0:T(1,128)}, u32[]{:S(2)}) copy-start(s32[1,33]{1,0:T(1,128)} %ptr.5) | copy-start | bytes 400
  18.6 3.1 %copy-start.1 = (bf16[224,128,128]{2,1,0:T(8,128)(2,1)S(1)}, bf16[224,128,128]{2,1,0:T(8,128)(2,1)}, u32[]{:S(2)}) copy-start(bf16[224,128,128]{2,1,0:T(8,128)(2,1)} %blocks.5) | copy-start | bytes 22020100
  24.2 1.3 %collective-permute-start.6 = (f32[3,2,16,128]{3,2,1,0:T(8,128)S(1)}, f32[3,2,16,128]{3,2,1,0:T(8,128)S(1)}, u32[]{:S(2)}, u32[]{:S(2)}) collective-permute-start(f32[3,2,16,128]{3,2,1,0:T(8,128)S(1)} %get-tuple-element.32), channel_id=1, source_target_pairs={{0,1},{1,0},{2,3},{3,2},{4,5},{5,4},{6,7},{7,6},{8,9},{9,8},{10,11... | collective-permute-start | bytes 147464 | tf_op jit(solution)/shard_map/ppermute | solution.py:68
  25.5 11.5 %collective-permute-start.10 = (f32[2,2,16,128]{3,2,1,0:T(8,128)S(1)}, f32[2,2,16,128]{3,2,1,0:T(8,128)S(1)}, u32[]{:S(2)}, u32[]{:S(2)}) collective-permute-start(f32[2,2,16,128]{3,2,1,0:T(8,128)S(1)} %pad_maximum_fusion), channel_id=1, source_target_pairs={{0,8},{1,9},{2,10},{3,11},{4,12},{5,13},{6,14},{7,15},{8,16},{9,17... | collective-permute-start | bytes 98312 | tf_op jit(solution)/shard_map/ppermute | solution.py:68
  27.1 9.9 %collective-permute-start.11 = (f32[2,2,16,128]{3,2,1,0:T(8,128)S(1)}, f32[2,2,16,128]{3,2,1,0:T(8,128)S(1)}, u32[]{:S(2)}, u32[]{:S(2)}) collective-permute-start(f32[2,2,16,128]{3,2,1,0:T(8,128)S(1)} %pad_maximum_fusion.1), channel_id=1, source_target_pairs={{0,24},{1,25},{2,26},{3,27},{4,28},{5,29},{6,30},{7,31},{8,0},{9,1... | collective-permute-start | bytes 98312 | tf_op jit(solution)/shard_map/ppermute | solution.py:68
  29.4 6.8 %collective-permute-start.7 = (f32[1,2,16,128]{3,2,1,0:T(8,128)S(1)}, f32[1,2,16,128]{3,2,1,0:T(8,128)S(1)}, u32[]{:S(2)}, u32[]{:S(2)}) collective-permute-start(f32[1,2,16,128]{3,2,1,0:T(8,128)S(1)} %get-tuple-element.33), channel_id=1, source_target_pairs={{0,31},{1,2},{2,1},{3,4},{4,3},{5,6},{6,5},{7,8},{8,7},{9,10},{10,... | collective-permute-start | bytes 49160 | tf_op jit(solution)/shard_map/ppermute | solution.py:68
  30.7 5.9 %collective-permute-start.8 = (f32[1,2,16,128]{3,2,1,0:T(8,128)S(1)}, f32[1,2,16,128]{3,2,1,0:T(8,128)S(1)}, u32[]{:S(2)}, u32[]{:S(2)}) collective-permute-start(f32[1,2,16,128]{3,2,1,0:T(8,128)S(1)} %get-tuple-element.34), channel_id=1, source_target_pairs={{0,23},{1,10},{2,25},{3,12},{4,27},{5,14},{6,29},{7,16},{8,31},{9,... | collective-permute-start | bytes 49160 | tf_op jit(solution)/shard_map/ppermute | solution.py:68
  32.9 4.1 %collective-permute-start.9 = (f32[1,2,16,128]{3,2,1,0:T(8,128)S(1)}, f32[1,2,16,128]{3,2,1,0:T(8,128)S(1)}, u32[]{:S(2)}, u32[]{:S(2)}) collective-permute-start(f32[1,2,16,128]{3,2,1,0:T(8,128)S(1)} %get-tuple-element.35), channel_id=1, source_target_pairs={{0,7},{1,26},{2,9},{3,28},{4,11},{5,30},{6,13},{7,0},{8,15},{9,2},... | collective-permute-start | bytes 49160 | tf_op jit(solution)/shard_map/ppermute | solution.py:68

commit v2 on v1

--- a/solution.py
+++ b/solution.py
@@ -18,7 +18,8 @@
 BY_FIRST = (((1,), (0,)), ((), ()))
 VMEM = pl.BlockSpec(memory_space=pltpu.VMEM)
 SMEM = pl.BlockSpec(memory_space=pltpu.SMEM)
-LIMIT = 40 * 2**20
+HBM = pl.BlockSpec(memory_space=pltpu.HBM)
+LIMIT = 8 * 2**20
 
 
 def neighbour(a, b):
@@ -80,17 +81,48 @@
     return pair, side, outer, inner, up, down
 
 
-def gather_kernel(send, vectors, *outgoing):
+def gather_kernel(send_hbm, vectors_hbm, ptr_hbm, col_hbm, vectors, ptr, col, send_out, *refs):
+    outgoing, (send, sems) = refs[:6], refs[6:]
+    copies = [
+        pltpu.make_async_copy(source, target, sems.at[i])
+        for i, (source, target) in enumerate(
+            (
+                (send_hbm, send),
+                (vectors_hbm, vectors),
+                (ptr_hbm, ptr),
+                (col_hbm, col),
+                (send_hbm, send_out),
+            )
+        )
+    ]
+    for copy in copies:
+        copy.start()
+    for copy in copies:
+        copy.wait()
     for ref, offsets in zip(outgoing, sent(outward())):
         for i, (a, b) in enumerate(offsets):
-            for g in range(send.shape[2]):
-                ref[i, g] = vectors[:, columns(send[0, neighbour(a, b), g])]
-
-
-def local_forward_kernel(ptr, vectors, blocks, image):
+            for g in range(ref.shape[1]):
+                ref[i, g] = vectors[:, columns(send[0, g, neighbour(a, b)])]
+
+
+def local_forward_kernel(ptr, vectors, blocks_hbm, blocks, image, sems):
     rows = image.shape[0]
+    parts = sems.shape[0]
+    stored = blocks.shape[0]
+    edges = [stored * i // parts for i in range(parts + 1)]
+    copies = [
+        pltpu.make_async_copy(blocks_hbm.at[a:b], blocks.at[a:b], sems.at[i])
+        for i, (a, b) in enumerate(zip(edges[:-1], edges[1:]))
+    ]
+    for copy in copies:
+        copy.start()
+    waited = 0
     for j in range(rows):
         e = ptr[0, j]
+        furthest = min(LONG * j, stored - SHORT * (rows - j)) + LOCAL
+        while waited < parts and (j == rows - 1 or edges[waited] < furthest):
+            copies[waited].wait()
+            waited += 1
         near = [vectors[:, c * B : c * B + B] for c in (j, (j + 1) % rows, (j - 1) % rows)]
         image[j] = lax.dot_general(
             jnp.concatenate(near, axis=1),
@@ -186,7 +218,7 @@
     for ref, offsets in zip(arrived, received(s)):
         for i, (a, b) in enumerate(offsets):
             for g in range(ref.shape[1]):
-                place = columns(send[0, neighbour(-a, -b), g])
+                place = columns(send[0, g, neighbour(-a, -b)])
                 adjoint[:, place] += ref[i, g]
     z = adjoint[...]
     gram = lax.dot_general(z, z, BY_LAST, precision=lax.Precision.HIGHEST, preferred_element_type=F32)
@@ -235,7 +267,7 @@
     return pl.pallas_call(
         kernel,
         name=name,
-        out_shape=[jax.ShapeDtypeStruct(shape, dtype) for shape, dtype in shapes],
+        out_shape=[jax.ShapeDtypeStruct(*s) if isinstance(s, tuple) else s for s in shapes],
         in_specs=in_specs,
         out_specs=[VMEM] * len(shapes),
         scratch_shapes=scratch,
@@ -253,22 +285,27 @@
     slots = send_list.shape[1] * ghost
     many = (stored - SHORT * rows) // (LONG - SHORT)
     sizes = (3, 1, 1, 1, 1, 1)
-    held = pltpu.with_memory_space_constraint(blocks, pltpu.VMEM)
-    outgoing = call(
+    send_lines = jnp.transpose(send_list, (0, 2, 1))
+    here, ptr, col, send, *outgoing = call(
         gather_kernel,
         "gather",
-        [((n, ghost, k, B), BF16) for n in sizes],
-        [SMEM, VMEM],
-    )(send_list, vectors)
+        [(vectors.shape, BF16)]
+        + [(a.shape, jnp.int32) for a in (row_ptr, col_index, send_lines)]
+        + [((n, ghost, k, B), BF16) for n in sizes],
+        [HBM] * 4,
+        scratch=[pltpu.SMEM(send_lines.shape, jnp.int32), pltpu.SemaphoreType.DMA((5,))],
+        bytes_accessed=0,
+    )(*[pltpu.with_memory_space_constraint(a, pltpu.HBM) for a in (send_lines, vectors, row_ptr, col_index)])
     arrived = exchange(*outgoing)
-    (partial_image,) = call(
+    held, partial_image = call(
         local_forward_kernel,
         "local_forward",
-        [((rows, k, B), F32)],
-        [SMEM, VMEM, VMEM],
+        [pltpu.VMEM(blocks.shape, BF16), ((rows, k, B), F32)],
+        [SMEM, VMEM, HBM],
+        scratch=[pltpu.SemaphoreType.DMA((8,))],
         flops=2 * rows * LOCAL * B * B * k,
         bytes_accessed=2 * rows * LOCAL * B * B,
-    )(row_ptr, vectors, held)
+    )(ptr, here, pltpu.with_memory_space_constraint(blocks, pltpu.HBM))
     image, *returns = call(
         ghost_kernel,
         "ghost",
@@ -282,7 +319,7 @@
         ],
         flops=4 * (stored - rows * LOCAL) * B * B * k,
         bytes_accessed=4 * (stored - rows * LOCAL) * B * B,
-    )(row_ptr, col_index, held, partial_image, *arrived)
+    )(ptr, col, held, partial_image, *arrived)
     returned = exchange(*returns)
     partial_adjoint, squares = call(
         local_backward_kernel,
@@ -291,13 +328,13 @@
         [SMEM, VMEM, VMEM],
         flops=2 * rows * LOCAL * B * B * k,
         bytes_accessed=2 * rows * LOCAL * B * B,
-    )(row_ptr, held, image)
+    )(ptr, held, image)
     adjoint, packed = call(
         gram_kernel,
         "gram",
         [((k, unknowns), F32), ((devices, 4, B), F32)],
         [SMEM] + [VMEM] * 8,
-    )(send_list, partial_adjoint, squares, *returned)
+    )(send, partial_adjoint, squares, *returned)
     everywhere = lax.all_to_all(packed, AXES, 0, 0)
     basis, factor, gain = call(
         functools.partial(solve_kernel, unknowns * devices),

time: 53.2 us -> 48.2 us (0.906)
  local copies, waits for them, and re-layouts: 7.6 us -> 0.01 us
  Pallas kernels: 10.2 us -> 13 us
    unnamed x13 -> x0, local copies, waits for them, and re-layouts: 7.6 us -> none
    pallas_call x2, Pallas kernels: 2.37 us -> 5.13 us  [the longest x1 4.14 us: local(): call(local_forward_kernel, 'local_forward', [pltpu.VMEM(blocks.shape, BF1...]
  transfers between devices with their start and end apart: 12 -> 12, of which waited for: 5 -> 6; matrix products, arithmetic and copies ran while one was open for 0% -> 0% of each run, Pallas kernels for 6% -> 11%
where the time goes in v2:
time: 48.2 us; the launch traced here: 48.1 us
  starting transfers between devices  18.6 us (39%)
  Pallas kernels  13 us (27%)
  blocking collectives  11.8 us (24%)
  waiting for transfers between devices  3.96 us (8%)
  between operations  0.69 us (1%)
    ppermute x12, starting transfers between devices, move(): lax.ppermute(array, AXES, [(d, (d + (odd if d % 2 else even)) % devices)...  18.6 us
    all_to_all x1, blocking collectives, local(): everywhere = lax.all_to_all(packed, AXES, 0, 0)  11.8 us
    pallas_call x1, Pallas kernels, local(): call(local_forward_kernel, 'local_forward', [pltpu.VMEM(blocks.shape, BF1...  4.14 us
    ppermute x12, waiting for transfers between devices, move(): lax.ppermute(array, AXES, [(d, (d + (odd if d % 2 else even)) % devices)...  3.96 us
    pallas_call x1, Pallas kernels, local(): call(functools.partial(solve_kernel, unknowns * devices), 'solve', [((k,...  2.81 us
    pallas_call x1, Pallas kernels, local(): call(ghost_kernel, 'ghost', [((rows, k, B), BF16)] + [((n, ghost, k, B),...  2.56 us
    pallas_call x1, Pallas kernels, local(): call(gram_kernel, 'gram', [((k, unknowns), F32), ((devices, 4, B), F32)],...  1.27 us
    pallas_call x1, Pallas kernels, local(): call(local_backward_kernel, 'local_backward', [((k, unknowns), F32), ((k,...  1.19 us
  transfers between devices with their start and end apart: 12, of which 6 were waited for; matrix products, arithmetic and copies ran while one was open for 0% of the time, Pallas kernels for 11%

profile of v2, /device:TPU:0, one launch (start us, length us, event | category | flops | bytes accessed | tf_op | source)
XLA Modules:
  0.0 48.1 jit_solution(545326799992164073)
XLA Ops:
  0.6 1.0 %gather.1 = (bf16[16,4096]{1,0:T(8,128)(2,1)S(1)}, s32[1,33]{1,0:T(1,128)S(1)}, s32[1,224]{1,0:T(1,128)S(1)}, s32[1,2,8]{2,1,0:T(2,128)S(1)}, bf16[3,2,16,128]{3...) custom-call(s32[1,2,8]{2,1,0:T(2,128)} %bitcast.2, ...), custom_call_target="tpu_custom_call" | custom-call | tf_op jit(solution)/shard_map/gather/pallas_call | solution.py:289
  1.6 0.5 %collective-permute-start = (bf16[3,2,16,128]{3,2,1,0:T(8,128)(2,1)S(1)}, bf16[3,2,16,128]{3,2,1,0:T(8,128)(2,1)S(1)}, u32[]{:S(2)}, u32[]{:S(2)}) collective-permute-start(bf16[3,2,16,128]{3,2,1,0:T(8,128)(2,1)S(1)} %get-tuple-element.35), channel_id=1, source_target_pairs={{0,1},{1,0},{2,3},{3,2},{4,5},{5,4},{6,7},{7,6},{8,9},{9,8},{10,11... | collective-permute-start | bytes 73736 | tf_op jit(solution)/shard_map/ppermute | solution.py:69
  2.1 0.8 %collective-permute-done.refs_0_ = bf16[3,2,16,128]{3,2,1,0:T(8,128)(2,1)S(1)} collective-permute-done((bf16[3,2,16,128]{3,2,1,0:T(8,128)(2,1)S(1)}, bf16[3,2,16,128]{3,2,1,0:T(8,128)(2,1)S(1)}, u32[]{:S(2)}, u32[]{:S(2)}) %collective-permute-start) | collective-permute-done | bytes 24608 | tf_op jit(solution)/shard_map/ppermute | solution.py:69
  3.0 2.9 %collective-permute-start.4 = (bf16[2,2,16,128]{3,2,1,0:T(8,128)(2,1)S(1)}, bf16[2,2,16,128]{3,2,1,0:T(8,128)(2,1)S(1)}, u32[]{:S(2)}, u32[]{:S(2)}) collective-permute-start(bf16[2,2,16,128]{3,2,1,0:T(8,128)(2,1)S(1)} %pad_maximum_fusion.2), channel_id=1, source_target_pairs={{0,8},{1,9},{2,10},{3,11},{4,12},{5,13},{6,14},{7,15},{8,16},{9,17... | collective-permute-start | bytes 49160 | tf_op jit(solution)/shard_map/ppermute | solution.py:69
  5.9 2.1 %collective-permute-start.5 = (bf16[2,2,16,128]{3,2,1,0:T(8,128)(2,1)S(1)}, bf16[2,2,16,128]{3,2,1,0:T(8,128)(2,1)S(1)}, u32[]{:S(2)}, u32[]{:S(2)}) collective-permute-start(bf16[2,2,16,128]{3,2,1,0:T(8,128)(2,1)S(1)} %pad_maximum_fusion.3), channel_id=1, source_target_pairs={{0,24},{1,25},{2,26},{3,27},{4,28},{5,29},{6,30},{7,31},{8,0},{9,1... | collective-permute-start | bytes 49160 | tf_op jit(solution)/shard_map/ppermute | solution.py:69
  8.0 3.1 %collective-permute-start.1 = (bf16[1,2,16,128]{3,2,1,0:T(8,128)(2,1)S(1)}, bf16[1,2,16,128]{3,2,1,0:T(8,128)(2,1)S(1)}, u32[]{:S(2)}, u32[]{:S(2)}) collective-permute-start(bf16[1,2,16,128]{3,2,1,0:T(8,128)(2,1)S(1)} %get-tuple-element.36), channel_id=1, source_target_pairs={{0,31},{1,2},{2,1},{3,4},{4,3},{5,6},{6,5},{7,8},{8,7},{9,10},{10,... | collective-permute-start | bytes 24584 | tf_op jit(solution)/shard_map/ppermute | solution.py:69
  11.1 1.0 %collective-permute-start.2 = (bf16[1,2,16,128]{3,2,1,0:T(8,128)(2,1)S(1)}, bf16[1,2,16,128]{3,2,1,0:T(8,128)(2,1)S(1)}, u32[]{:S(2)}, u32[]{:S(2)}) collective-permute-start(bf16[1,2,16,128]{3,2,1,0:T(8,128)(2,1)S(1)} %get-tuple-element.37), channel_id=1, source_target_pairs={{0,23},{1,10},{2,25},{3,12},{4,27},{5,14},{6,29},{7,16},{8,31},{9,... | collective-permute-start | bytes 24584 | tf_op jit(solution)/shard_map/ppermute | solution.py:69
  12.1 0.5 %collective-permute-start.3 = (bf16[1,2,16,128]{3,2,1,0:T(8,128)(2,1)S(1)}, bf16[1,2,16,128]{3,2,1,0:T(8,128)(2,1)S(1)}, u32[]{:S(2)}, u32[]{:S(2)}) collective-permute-start(bf16[1,2,16,128]{3,2,1,0:T(8,128)(2,1)S(1)} %get-tuple-element.38), channel_id=1, source_target_pairs={{0,7},{1,26},{2,9},{3,28},{4,11},{5,30},{6,13},{7,0},{8,15},{9,2},... | collective-permute-start | bytes 24584 | tf_op jit(solution)/shard_map/ppermute | solution.py:69
  12.6 4.1 %local_forward.1 = (bf16[224,128,128]{2,1,0:T(8,128)(2,1)S(1)}, f32[32,16,128]{2,1,0:T(8,128)S(1)}) custom-call(s32[1,33]{1,0:T(1,128)S(1)} %get-tuple-element.30.ptr, bf16[16,4096]{1,0:T(8,128)(2,1)S(1)} %get-tuple-element.31.vectors, bf16[224,128,128]{2,1,0:T(8,128)(2,1)} %blocks_hbm.1), custom_call_target="tpu_custom_call" | custom-call | flops 50331648 | bytes 3145728 | tf_op jit(solution)/shard_map/local_forward/pallas_call | solution.py:300
  16.7 0.1 collective-permute-done.2.refs_2_
  16.9 2.6 %ghost.1 = (bf16[32,16,128]{2,1,0:T(8,128)(2,1)S(1)}, f32[3,2,16,128]{3,2,1,0:T(8,128)S(1)}, f32[1,2,16,128]{3,2,1,0:T(8,128)S(1)}, f32[1,2,16,128]{3,2,1,0:T(8,...) custom-call(s32[1,33]{1,0:T(1,128)S(1)} %get-tuple-element.30.ptr, ...), custom_call_target="tpu_custom_call" | custom-call | flops 134217728 | bytes 8388608 | tf_op jit(solution)/shard_map/ghost/pallas_call | solution.py:309
  19.5 1.2 %collective-permute-done.6.refs_0_ = f32[3,2,16,128]{3,2,1,0:T(8,128)S(1)} collective-permute-done((f32[3,2,16,128]{3,2,1,0:T(8,128)S(1)}, f32[3,2,16,128]{3,2,1,0:T(8,128)S(1)}, u32[]{:S(2)}, u32[]{:S(2)}) %collective-permute-start.6) | collective-permute-done | bytes 49184 | tf_op jit(solution)/shard_map/ppermute | solution.py:69
  20.7 1.6 %collective-permute-start.10 = (f32[2,2,16,128]{3,2,1,0:T(8,128)S(1)}, f32[2,2,16,128]{3,2,1,0:T(8,128)S(1)}, u32[]{:S(2)}, u32[]{:S(2)}) collective-permute-start(f32[2,2,16,128]{3,2,1,0:T(8,128)S(1)} %pad_maximum_fusion), channel_id=1, source_target_pairs={{0,8},{1,9},{2,10},{3,11},{4,12},{5,13},{6,14},{7,15},{8,16},{9,17... | collective-permute-start | bytes 98312 | tf_op jit(solution)/shard_map/ppermute | solution.py:69
  22.3 2.3 %collective-permute-start.11 = (f32[2,2,16,128]{3,2,1,0:T(8,128)S(1)}, f32[2,2,16,128]{3,2,1,0:T(8,128)S(1)}, u32[]{:S(2)}, u32[]{:S(2)}) collective-permute-start(f32[2,2,16,128]{3,2,1,0:T(8,128)S(1)} %pad_maximum_fusion.1), channel_id=1, source_target_pairs={{0,24},{1,25},{2,26},{3,27},{4,28},{5,29},{6,30},{7,31},{8,0},{9,1... | collective-permute-start | bytes 98312 | tf_op jit(solution)/shard_map/ppermute | solution.py:69
  24.6 1.2 %collective-permute-start.7 = (f32[1,2,16,128]{3,2,1,0:T(8,128)S(1)}, f32[1,2,16,128]{3,2,1,0:T(8,128)S(1)}, u32[]{:S(2)}, u32[]{:S(2)}) collective-permute-start(f32[1,2,16,128]{3,2,1,0:T(8,128)S(1)} %get-tuple-element.45), channel_id=1, source_target_pairs={{0,31},{1,2},{2,1},{3,4},{4,3},{5,6},{6,5},{7,8},{8,7},{9,10},{10,... | collective-permute-start | bytes 49160 | tf_op jit(solution)/shard_map/ppermute | solution.py:69
  25.8 2.2 %collective-permute-start.8 = (f32[1,2,16,128]{3,2,1,0:T(8,128)S(1)}, f32[1,2,16,128]{3,2,1,0:T(8,128)S(1)}, u32[]{:S(2)}, u32[]{:S(2)}) collective-permute-start(f32[1,2,16,128]{3,2,1,0:T(8,128)S(1)} %get-tuple-element.46), channel_id=1, source_target_pairs={{0,23},{1,10},{2,25},{3,12},{4,27},{5,14},{6,29},{7,16},{8,31},{9,... | collective-permute-start | bytes 49160 | tf_op jit(solution)/shard_map/ppermute | solution.py:69
  28.1 1.1 %collective-permute-start.9 = (f32[1,2,16,128]{3,2,1,0:T(8,128)S(1)}, f32[1,2,16,128]{3,2,1,0:T(8,128)S(1)}, u32[]{:S(2)}, u32[]{:S(2)}) collective-permute-start(f32[1,2,16,128]{3,2,1,0:T(8,128)S(1)} %get-tuple-element.47), channel_id=1, source_target_pairs={{0,7},{1,26},{2,9},{3,28},{4,11},{5,30},{6,13},{7,0},{8,15},{9,2},... | collective-permute-start | bytes 49160 | tf_op jit(solution)/shard_map/ppermute | solution.py:69
  29.2 1.2 %local_backward.1 = (f32[16,4096]{1,0:T(8,128)S(1)}, f32[16,128]{1,0:T(8,128)S(1)}) custom-call(s32[1,33]{1,0:T(1,128)S(1)} %get-tuple-element.30.ptr, bf16[224,128,128]{2,1,0:T(8,128)(2,1)S(1)} %get-tuple-element.32.blocks, bf16[32,16,128]{2,1,0:T(8,128)(2,1)S(1)} %get-tuple-element.41.image), custom_call_target="tpu_custom_call" | custom-call | flops 50331648 | bytes 3145728 | tf_op jit(solution)/shard_map/local_backward/pallas_call | solution.py:324
  30.4 1.0 %collective-permute-done.7.refs_1_ = f32[1,2,16,128]{3,2,1,0:T(8,128)S(1)} collective-permute-done((f32[1,2,16,128]{3,2,1,0:T(8,128)S(1)}, f32[1,2,16,128]{3,2,1,0:T(8,128)S(1)}, u32[]{:S(2)}, u32[]{:S(2)}) %collective-permute-start.7) | collective-permute-done | bytes 16416 | tf_op jit(solution)/shard_map/ppermute | solution.py:69
  31.4 0.3 collective-permute-done.8.refs_2_
  31.7 0.4 collective-permute-done.9.refs_3_
  32.2 1.3 %gram.1 = (f32[16,4096]{1,0:T(8,128)S(1)}, f32[32,4,128]{2,1,0:T(4,128)S(1)}) custom-call(s32[1,2,8]{2,1,0:T(2,128)S(1)} %get-tuple-element.29.send, f32[16,4096]{1,0:T(8,128)S(1)} %get-tuple-element.42.partial_adjoint, f32[16,128]{1,0:T(8,128)S(1)} %get-tuple-element.43.squares, f32[3,2,16,128]{3,2,1,0:T(8,128)S(1)} %collective-permute-done.6.refs_0_, ...), custom_call_target="tpu_custom_call" | custom-call | tf_op jit(solution)/shard_map/gram/pallas_call | solution.py:332
  33.4 11.8 %all_to_all.5.packed = f32[32,4,128]{2,1,0:T(4,128)S(1)} all-to-all(f32[32,4,128]{2,1,0:T(4,128)S(1)} %get-tuple-element.50), channel_id=1, replica_groups=mesh['dom'=4,'sub'=8] {'dom','sub'}, dimensions={0} | all-to-all | bytes 131072 | tf_op jit(solution)/shard_map/all_to_all | solution.py:338
  45.2 2.8 %solve.1 = (f32[16,4096]{1,0:T(8,128)}, f32[16,16]{1,0:T(8,128)}, f32[1,16]{1,0:T(1,128)}) custom-call(f32[32,4,128]{2,1,0:T(4,128)S(1)} %all_to_all.5.packed, f32[16,4096]{1,0:T(8,128)S(1)} %get-tuple-element.51.adjoint), custom_call_target="tpu_custom_call" | custom-call | tf_op jit(solution)/shard_map/solve/pallas_call | solution.py:339
  (13 shorter events, 0.1 us)
Async XLA Ops:
  1.6 1.4 %collective-permute-start = (bf16[3,2,16,128]{3,2,1,0:T(8,128)(2,1)S(1)}, bf16[3,2,16,128]{3,2,1,0:T(8,128)(2,1)S(1)}, u32[]{:S(2)}, u32[]{:S(2)}) collective-permute-start(bf16[3,2,16,128]{3,2,1,0:T(8,128)(2,1)S(1)} %get-tuple-element.35), channel_id=1, source_target_pairs={{0,1},{1,0},{2,3},{3,2},{4,5},{5,4},{6,7},{7,6},{8,9},{9,8},{10,11... | collective-permute-start | bytes 73736 | tf_op jit(solution)/shard_map/ppermute | solution.py:69
  3.0 13.8 %collective-permute-start.4 = (bf16[2,2,16,128]{3,2,1,0:T(8,128)(2,1)S(1)}, bf16[2,2,16,128]{3,2,1,0:T(8,128)(2,1)S(1)}, u32[]{:S(2)}, u32[]{:S(2)}) collective-permute-start(bf16[2,2,16,128]{3,2,1,0:T(8,128)(2,1)S(1)} %pad_maximum_fusion.2), channel_id=1, source_target_pairs={{0,8},{1,9},{2,10},{3,11},{4,12},{5,13},{6,14},{7,15},{8,16},{9,17... | collective-permute-start | bytes 49160 | tf_op jit(solution)/shard_map/ppermute | solution.py:69
  5.9 10.9 %collective-permute-start.5 = (bf16[2,2,16,128]{3,2,1,0:T(8,128)(2,1)S(1)}, bf16[2,2,16,128]{3,2,1,0:T(8,128)(2,1)S(1)}, u32[]{:S(2)}, u32[]{:S(2)}) collective-permute-start(bf16[2,2,16,128]{3,2,1,0:T(8,128)(2,1)S(1)} %pad_maximum_fusion.3), channel_id=1, source_target_pairs={{0,24},{1,25},{2,26},{3,27},{4,28},{5,29},{6,30},{7,31},{8,0},{9,1... | collective-permute-start | bytes 49160 | tf_op jit(solution)/shard_map/ppermute | solution.py:69
  8.0 8.7 %collective-permute-start.1 = (bf16[1,2,16,128]{3,2,1,0:T(8,128)(2,1)S(1)}, bf16[1,2,16,128]{3,2,1,0:T(8,128)(2,1)S(1)}, u32[]{:S(2)}, u32[]{:S(2)}) collective-permute-start(bf16[1,2,16,128]{3,2,1,0:T(8,128)(2,1)S(1)} %get-tuple-element.36), channel_id=1, source_target_pairs={{0,31},{1,2},{2,1},{3,4},{4,3},{5,6},{6,5},{7,8},{8,7},{9,10},{10,... | collective-permute-start | bytes 24584 | tf_op jit(solution)/shard_map/ppermute | solution.py:69
  11.1 5.8 %collective-permute-start.2 = (bf16[1,2,16,128]{3,2,1,0:T(8,128)(2,1)S(1)}, bf16[1,2,16,128]{3,2,1,0:T(8,128)(2,1)S(1)}, u32[]{:S(2)}, u32[]{:S(2)}) collective-permute-start(bf16[1,2,16,128]{3,2,1,0:T(8,128)(2,1)S(1)} %get-tuple-element.37), channel_id=1, source_target_pairs={{0,23},{1,10},{2,25},{3,12},{4,27},{5,14},{6,29},{7,16},{8,31},{9,... | collective-permute-start | bytes 24584 | tf_op jit(solution)/shard_map/ppermute | solution.py:69
  12.1 4.8 %collective-permute-start.3 = (bf16[1,2,16,128]{3,2,1,0:T(8,128)(2,1)S(1)}, bf16[1,2,16,128]{3,2,1,0:T(8,128)(2,1)S(1)}, u32[]{:S(2)}, u32[]{:S(2)}) collective-permute-start(bf16[1,2,16,128]{3,2,1,0:T(8,128)(2,1)S(1)} %get-tuple-element.38), channel_id=1, source_target_pairs={{0,7},{1,26},{2,9},{3,28},{4,11},{5,30},{6,13},{7,0},{8,15},{9,2},... | collective-permute-start | bytes 24584 | tf_op jit(solution)/shard_map/ppermute | solution.py:69
  19.4 1.3 %collective-permute-start.6 = (f32[3,2,16,128]{3,2,1,0:T(8,128)S(1)}, f32[3,2,16,128]{3,2,1,0:T(8,128)S(1)}, u32[]{:S(2)}, u32[]{:S(2)}) collective-permute-start(f32[3,2,16,128]{3,2,1,0:T(8,128)S(1)} %get-tuple-element.44), channel_id=1, source_target_pairs={{0,1},{1,0},{2,3},{3,2},{4,5},{5,4},{6,7},{7,6},{8,9},{9,8},{10,11... | collective-permute-start | bytes 147464 | tf_op jit(solution)/shard_map/ppermute | solution.py:69
  20.7 11.4 %collective-permute-start.10 = (f32[2,2,16,128]{3,2,1,0:T(8,128)S(1)}, f32[2,2,16,128]{3,2,1,0:T(8,128)S(1)}, u32[]{:S(2)}, u32[]{:S(2)}) collective-permute-start(f32[2,2,16,128]{3,2,1,0:T(8,128)S(1)} %pad_maximum_fusion), channel_id=1, source_target_pairs={{0,8},{1,9},{2,10},{3,11},{4,12},{5,13},{6,14},{7,15},{8,16},{9,17... | collective-permute-start | bytes 98312 | tf_op jit(solution)/shard_map/ppermute | solution.py:69
  22.3 9.9 %collective-permute-start.11 = (f32[2,2,16,128]{3,2,1,0:T(8,128)S(1)}, f32[2,2,16,128]{3,2,1,0:T(8,128)S(1)}, u32[]{:S(2)}, u32[]{:S(2)}) collective-permute-start(f32[2,2,16,128]{3,2,1,0:T(8,128)S(1)} %pad_maximum_fusion.1), channel_id=1, source_target_pairs={{0,24},{1,25},{2,26},{3,27},{4,28},{5,29},{6,30},{7,31},{8,0},{9,1... | collective-permute-start | bytes 98312 | tf_op jit(solution)/shard_map/ppermute | solution.py:69
  24.6 6.8 %collective-permute-start.7 = (f32[1,2,16,128]{3,2,1,0:T(8,128)S(1)}, f32[1,2,16,128]{3,2,1,0:T(8,128)S(1)}, u32[]{:S(2)}, u32[]{:S(2)}) collective-permute-start(f32[1,2,16,128]{3,2,1,0:T(8,128)S(1)} %get-tuple-element.45), channel_id=1, source_target_pairs={{0,31},{1,2},{2,1},{3,4},{4,3},{5,6},{6,5},{7,8},{8,7},{9,10},{10,... | collective-permute-start | bytes 49160 | tf_op jit(solution)/shard_map/ppermute | solution.py:69
  25.8 5.9 %collective-permute-start.8 = (f32[1,2,16,128]{3,2,1,0:T(8,128)S(1)}, f32[1,2,16,128]{3,2,1,0:T(8,128)S(1)}, u32[]{:S(2)}, u32[]{:S(2)}) collective-permute-start(f32[1,2,16,128]{3,2,1,0:T(8,128)S(1)} %get-tuple-element.46), channel_id=1, source_target_pairs={{0,23},{1,10},{2,25},{3,12},{4,27},{5,14},{6,29},{7,16},{8,31},{9,... | collective-permute-start | bytes 49160 | tf_op jit(solution)/shard_map/ppermute | solution.py:69
  28.1 4.1 %collective-permute-start.9 = (f32[1,2,16,128]{3,2,1,0:T(8,128)S(1)}, f32[1,2,16,128]{3,2,1,0:T(8,128)S(1)}, u32[]{:S(2)}, u32[]{:S(2)}) collective-permute-start(f32[1,2,16,128]{3,2,1,0:T(8,128)S(1)} %get-tuple-element.47), channel_id=1, source_target_pairs={{0,7},{1,26},{2,9},{3,28},{4,11},{5,30},{6,13},{7,0},{8,15},{9,2},... | collective-permute-start | bytes 49160 | tf_op jit(solution)/shard_map/ppermute | solution.py:69

commit v3 on v2

--- a/solution.py
+++ b/solution.py
@@ -18,6 +18,7 @@
 BY_FIRST = (((1,), (0,)), ((), ()))
 VMEM = pl.BlockSpec(memory_space=pltpu.VMEM)
 SMEM = pl.BlockSpec(memory_space=pltpu.SMEM)
+ANY = pl.BlockSpec(memory_space=pl.ANY)
 HBM = pl.BlockSpec(memory_space=pltpu.HBM)
 LIMIT = 8 * 2**20
 
@@ -81,7 +82,7 @@
     return pair, side, outer, inner, up, down
 
 
-def gather_kernel(send_hbm, vectors_hbm, ptr_hbm, col_hbm, vectors, ptr, col, send_out, *refs):
+def gather_kernel(send_hbm, vectors_hbm, ptr_hbm, col_hbm, blocks_hbm, vectors, ptr, col, send_out, *refs):
     outgoing, (send, sems) = refs[:6], refs[6:]
     copies = [
         pltpu.make_async_copy(source, target, sems.at[i])
@@ -103,26 +104,15 @@
         for i, (a, b) in enumerate(offsets):
             for g in range(ref.shape[1]):
                 ref[i, g] = vectors[:, columns(send[0, g, neighbour(a, b)])]
-
-
-def local_forward_kernel(ptr, vectors, blocks_hbm, blocks, image, sems):
+        for i in range(len(offsets), ref.shape[0]):
+            ref[i] = ref[0]
+
+
+def local_forward_kernel(ptr, vectors, blocks, *refs):
+    image = refs[-1]
     rows = image.shape[0]
-    parts = sems.shape[0]
-    stored = blocks.shape[0]
-    edges = [stored * i // parts for i in range(parts + 1)]
-    copies = [
-        pltpu.make_async_copy(blocks_hbm.at[a:b], blocks.at[a:b], sems.at[i])
-        for i, (a, b) in enumerate(zip(edges[:-1], edges[1:]))
-    ]
-    for copy in copies:
-        copy.start()
-    waited = 0
     for j in range(rows):
         e = ptr[0, j]
-        furthest = min(LONG * j, stored - SHORT * (rows - j)) + LOCAL
-        while waited < parts and (j == rows - 1 or edges[waited] < furthest):
-            copies[waited].wait()
-            waited += 1
         near = [vectors[:, c * B : c * B + B] for c in (j, (j + 1) % rows, (j - 1) % rows)]
         image[j] = lax.dot_general(
             jnp.concatenate(near, axis=1),
@@ -185,6 +175,8 @@
             for g in range(ref.shape[1]):
                 slot = neighbour(-a, -b) * ref.shape[1] + g
                 ref[i, g] = sum(spread[bank, slot] for bank in range(banks))
+        for i in range(len(offsets), ref.shape[0]):
+            ref[i] = ref[0]
 
 
 def local_backward_kernel(ptr, blocks, image, adjoint, squares):
@@ -284,7 +276,7 @@
     ghost = send_list.shape[2]
     slots = send_list.shape[1] * ghost
     many = (stored - SHORT * rows) // (LONG - SHORT)
-    sizes = (3, 1, 1, 1, 1, 1)
+    sizes = (3, 2, 2, 2, 1, 1)
     send_lines = jnp.transpose(send_list, (0, 2, 1))
     here, ptr, col, send, *outgoing = call(
         gather_kernel,
@@ -292,20 +284,19 @@
         [(vectors.shape, BF16)]
         + [(a.shape, jnp.int32) for a in (row_ptr, col_index, send_lines)]
         + [((n, ghost, k, B), BF16) for n in sizes],
-        [HBM] * 4,
+        [HBM] * 5,
         scratch=[pltpu.SMEM(send_lines.shape, jnp.int32), pltpu.SemaphoreType.DMA((5,))],
         bytes_accessed=0,
-    )(*[pltpu.with_memory_space_constraint(a, pltpu.HBM) for a in (send_lines, vectors, row_ptr, col_index)])
+    )(*[pltpu.with_memory_space_constraint(a, pltpu.HBM) for a in (send_lines, vectors, row_ptr, col_index, blocks)])
     arrived = exchange(*outgoing)
-    held, partial_image = call(
+    (partial_image,) = call(
         local_forward_kernel,
         "local_forward",
-        [pltpu.VMEM(blocks.shape, BF16), ((rows, k, B), F32)],
-        [SMEM, VMEM, HBM],
-        scratch=[pltpu.SemaphoreType.DMA((8,))],
+        [((rows, k, B), F32)],
+        [SMEM, VMEM, VMEM] + [ANY] * len(arrived[:0]),
         flops=2 * rows * LOCAL * B * B * k,
         bytes_accessed=2 * rows * LOCAL * B * B,
-    )(ptr, here, pltpu.with_memory_space_constraint(blocks, pltpu.HBM))
+    )(ptr, here, blocks, *arrived[:0])
     image, *returns = call(
         ghost_kernel,
         "ghost",
@@ -319,7 +310,7 @@
         ],
         flops=4 * (stored - rows * LOCAL) * B * B * k,
         bytes_accessed=4 * (stored - rows * LOCAL) * B * B,
-    )(ptr, col, held, partial_image, *arrived)
+    )(ptr, col, blocks, partial_image, *arrived)
     returned = exchange(*returns)
     partial_adjoint, squares = call(
         local_backward_kernel,
@@ -328,7 +319,7 @@
         [SMEM, VMEM, VMEM],
         flops=2 * rows * LOCAL * B * B * k,
         bytes_accessed=2 * rows * LOCAL * B * B,
-    )(ptr, held, image)
+    )(ptr, blocks, image)
     adjoint, packed = call(
         gram_kernel,
         "gram",

time: 48.2 us -> 46.7 us (0.969)
  starting transfers between devices: 18.6 us -> 22.2 us
  waiting for transfers between devices: 3.96 us -> 0.86 us
  Pallas kernels: 13 us -> 10.7 us
    ppermute x12, starting transfers between devices: 18.6 us -> 22.2 us  [move(): lax.ppermute(array, AXES, [(d, (d + (odd if d % 2 else even)) % devices)...]
    ppermute x12, waiting for transfers between devices: 3.96 us -> 0.86 us  [move(): lax.ppermute(array, AXES, [(d, (d + (odd if d % 2 else even)) % devices)...]
    pallas_call x1, Pallas kernels: 4.14 us -> 1.73 us  [local(): call(local_forward_kernel, 'local_forward', [((rows, k, B), F32)], [SMEM,...]
  transfers between devices with their start and end apart: 12 -> 12, of which waited for: 6 -> 2; matrix products, arithmetic and copies ran while one was open for 0% -> 0% of each run, Pallas kernels for 11% -> 6%
where the time goes in v3:
time: 46.7 us; the launch traced here: 46.6 us
  starting transfers between devices  22.2 us (48%)
  blocking collectives  12 us (26%)
  Pallas kernels  10.7 us (23%)
  waiting for transfers between devices  0.86 us (2%)
  between operations  0.74 us (2%)
    ppermute x12, starting transfers between devices, move(): lax.ppermute(array, AXES, [(d, (d + (odd if d % 2 else even)) % devices)...  22.2 us
    all_to_all x1, blocking collectives, local(): everywhere = lax.all_to_all(packed, AXES, 0, 0)  12 us
    pallas_call x1, Pallas kernels, local(): call(functools.partial(solve_kernel, unknowns * devices), 'solve', [((k,...  2.81 us
    pallas_call x1, Pallas kernels, local(): call(ghost_kernel, 'ghost', [((rows, k, B), BF16)] + [((n, ghost, k, B),...  2.55 us
    pallas_call x1, Pallas kernels, local(): call(local_forward_kernel, 'local_forward', [((rows, k, B), F32)], [SMEM,...  1.73 us
    pallas_call x1, Pallas kernels, local(): call(gram_kernel, 'gram', [((k, unknowns), F32), ((devices, 4, B), F32)],...  1.28 us
    pallas_call x1, Pallas kernels, local(): call(local_backward_kernel, 'local_backward', [((k, unknowns), F32), ((k,...  1.19 us
    pallas_call x1, Pallas kernels, local(): call(gather_kernel, 'gather', [(vectors.shape, BF16)] + [(a.shape, jnp.in...  1.15 us
  transfers between devices with their start and end apart: 12, of which 2 were waited for; matrix products, arithmetic and copies ran while one was open for 0% of the time, Pallas kernels for 6%

profile of v3, /device:TPU:0, one launch (start us, length us, event | category | flops | bytes accessed | tf_op | source)
XLA Modules:
  0.0 46.6 jit_solution(2176512123641180668)
XLA Ops:
  0.6 1.1 %gather.1 = (bf16[16,4096]{1,0:T(8,128)(2,1)S(1)}, s32[1,33]{1,0:T(1,128)S(1)}, s32[1,224]{1,0:T(1,128)S(1)}, s32[1,2,8]{2,1,0:T(2,128)S(1)}, bf16[3,2,16,128]{3...) custom-call(s32[1,2,8]{2,1,0:T(2,128)} %bitcast.2, ...), custom_call_target="tpu_custom_call" | custom-call | tf_op jit(solution)/shard_map/gather/pallas_call | solution.py:281
  1.8 0.5 %collective-permute-start = (bf16[3,2,16,128]{3,2,1,0:T(8,128)(2,1)S(1)}, bf16[3,2,16,128]{3,2,1,0:T(8,128)(2,1)S(1)}, u32[]{:S(2)}, u32[]{:S(2)}) collective-permute-start(bf16[3,2,16,128]{3,2,1,0:T(8,128)(2,1)S(1)} %get-tuple-element.31), channel_id=1, source_target_pairs={{0,1},{1,0},{2,3},{3,2},{4,5},{5,4},{6,7},{7,6},{8,9},{9,8},{10,11... | collective-permute-start | bytes 73736 | tf_op jit(solution)/shard_map/ppermute | solution.py:70
  2.3 6.6 %collective-permute-start.1 = (bf16[2,2,16,128]{3,2,1,0:T(8,128)(2,1)S(1)}, bf16[2,2,16,128]{3,2,1,0:T(8,128)(2,1)S(1)}, u32[]{:S(2)}, u32[]{:S(2)}) collective-permute-start(bf16[2,2,16,128]{3,2,1,0:T(8,128)(2,1)S(1)} %get-tuple-element.32), channel_id=1, source_target_pairs={{0,31},{1,2},{2,1},{3,4},{4,3},{5,6},{6,5},{7,8},{8,7},{9,10},{10,... | collective-permute-start | bytes 49160 | tf_op jit(solution)/shard_map/ppermute | solution.py:70
  8.9 0.2 collective-permute-start.2
  9.1 1.4 %collective-permute-start.3 = (bf16[2,2,16,128]{3,2,1,0:T(8,128)(2,1)S(1)}, bf16[2,2,16,128]{3,2,1,0:T(8,128)(2,1)S(1)}, u32[]{:S(2)}, u32[]{:S(2)}) collective-permute-start(bf16[2,2,16,128]{3,2,1,0:T(8,128)(2,1)S(1)} %get-tuple-element.34), channel_id=1, source_target_pairs={{0,7},{1,26},{2,9},{3,28},{4,11},{5,30},{6,13},{7,0},{8,15},{9,2},... | collective-permute-start | bytes 49160 | tf_op jit(solution)/shard_map/ppermute | solution.py:70
  10.4 0.0 collective-permute-done.refs_0_
  10.4 1.6 %collective-permute-start.4 = (bf16[2,2,16,128]{3,2,1,0:T(8,128)(2,1)S(1)}, bf16[2,2,16,128]{3,2,1,0:T(8,128)(2,1)S(1)}, u32[]{:S(2)}, u32[]{:S(2)}) collective-permute-start(bf16[2,2,16,128]{3,2,1,0:T(8,128)(2,1)S(1)} %pad_maximum_fusion.2), channel_id=1, source_target_pairs={{0,8},{1,9},{2,10},{3,11},{4,12},{5,13},{6,14},{7,15},{8,16},{9,17... | collective-permute-start | bytes 49160 | tf_op jit(solution)/shard_map/ppermute | solution.py:70
  12.1 2.2 %collective-permute-start.5 = (bf16[2,2,16,128]{3,2,1,0:T(8,128)(2,1)S(1)}, bf16[2,2,16,128]{3,2,1,0:T(8,128)(2,1)S(1)}, u32[]{:S(2)}, u32[]{:S(2)}) collective-permute-start(bf16[2,2,16,128]{3,2,1,0:T(8,128)(2,1)S(1)} %pad_maximum_fusion.3), channel_id=1, source_target_pairs={{0,24},{1,25},{2,26},{3,27},{4,28},{5,29},{6,30},{7,31},{8,0},{9,1... | collective-permute-start | bytes 49160 | tf_op jit(solution)/shard_map/ppermute | solution.py:70
  14.3 1.7 %local_forward.1.partial_image = f32[32,16,128]{2,1,0:T(8,128)S(1)} custom-call(s32[1,33]{1,0:T(1,128)S(1)} %get-tuple-element.28.ptr, bf16[16,4096]{1,0:T(8,128)(2,1)S(1)} %get-tuple-element.30.vectors, bf16[224,128,128]{2,1,0:T(8,128)(2,1)S(1)} %copy-done), custom_call_target="tpu_custom_call" | custom-call | flops 50331648 | bytes 3145728 | tf_op jit(solution)/shard_map/local_forward/pallas_call | solution.py:292
  16.1 0.0 collective-permute-done.3.refs_3_
  16.1 0.0 collective-permute-done.4.refs_4_
  16.1 0.2 collective-permute-done.5.refs_5_
  16.3 2.5 %ghost.1 = (bf16[32,16,128]{2,1,0:T(8,128)(2,1)S(1)}, f32[3,2,16,128]{3,2,1,0:T(8,128)S(1)}, f32[2,2,16,128]{3,2,1,0:T(8,128)S(1)}, f32[2,2,16,128]{3,2,1,0:T(8,...) custom-call(s32[1,33]{1,0:T(1,128)S(1)} %get-tuple-element.28.ptr, ...), custom_call_target="tpu_custom_call" | custom-call | flops 134217728 | bytes 8388608 | tf_op jit(solution)/shard_map/ghost/pallas_call | solution.py:300
  18.8 0.1 collective-permute-start.6
  18.9 3.3 %collective-permute-start.7 = (f32[2,2,16,128]{3,2,1,0:T(8,128)S(1)}, f32[2,2,16,128]{3,2,1,0:T(8,128)S(1)}, u32[]{:S(2)}, u32[]{:S(2)}) collective-permute-start(f32[2,2,16,128]{3,2,1,0:T(8,128)S(1)} %get-tuple-element.41), channel_id=1, source_target_pairs={{0,31},{1,2},{2,1},{3,4},{4,3},{5,6},{6,5},{7,8},{8,7},{9,10},{10,... | collective-permute-start | bytes 98312 | tf_op jit(solution)/shard_map/ppermute | solution.py:70
  22.2 2.4 %collective-permute-start.8 = (f32[2,2,16,128]{3,2,1,0:T(8,128)S(1)}, f32[2,2,16,128]{3,2,1,0:T(8,128)S(1)}, u32[]{:S(2)}, u32[]{:S(2)}) collective-permute-start(f32[2,2,16,128]{3,2,1,0:T(8,128)S(1)} %get-tuple-element.42), channel_id=1, source_target_pairs={{0,23},{1,10},{2,25},{3,12},{4,27},{5,14},{6,29},{7,16},{8,31},{9,... | collective-permute-start | bytes 98312 | tf_op jit(solution)/shard_map/ppermute | solution.py:70
  24.7 0.7 %collective-permute-start.10 = (f32[2,2,16,128]{3,2,1,0:T(8,128)S(1)}, f32[2,2,16,128]{3,2,1,0:T(8,128)S(1)}, u32[]{:S(2)}, u32[]{:S(2)}) collective-permute-start(f32[2,2,16,128]{3,2,1,0:T(8,128)S(1)} %pad_maximum_fusion), channel_id=1, source_target_pairs={{0,8},{1,9},{2,10},{3,11},{4,12},{5,13},{6,14},{7,15},{8,16},{9,17... | collective-permute-start | bytes 98312 | tf_op jit(solution)/shard_map/ppermute | solution.py:70
  25.4 3.2 %collective-permute-start.11 = (f32[2,2,16,128]{3,2,1,0:T(8,128)S(1)}, f32[2,2,16,128]{3,2,1,0:T(8,128)S(1)}, u32[]{:S(2)}, u32[]{:S(2)}) collective-permute-start(f32[2,2,16,128]{3,2,1,0:T(8,128)S(1)} %pad_maximum_fusion.1), channel_id=1, source_target_pairs={{0,24},{1,25},{2,26},{3,27},{4,28},{5,29},{6,30},{7,31},{8,0},{9,1... | collective-permute-start | bytes 98312 | tf_op jit(solution)/shard_map/ppermute | solution.py:70
  28.5 1.2 %local_backward.1 = (f32[16,4096]{1,0:T(8,128)S(1)}, f32[16,128]{1,0:T(8,128)S(1)}) custom-call(s32[1,33]{1,0:T(1,128)S(1)} %get-tuple-element.28.ptr, bf16[224,128,128]{2,1,0:T(8,128)(2,1)S(1)} %copy-done, bf16[32,16,128]{2,1,0:T(8,128)(2,1)S(1)} %get-tuple-element.37.image), custom_call_target="tpu_custom_call" | custom-call | flops 50331648 | bytes 3145728 | tf_op jit(solution)/shard_map/local_backward/pallas_call | solution.py:315
  29.7 0.0 collective-permute-done.8.refs_2_
  29.8 0.7 %collective-permute-done.10.refs_4_ = f32[2,2,16,128]{3,2,1,0:T(8,128)S(1)} collective-permute-done((f32[2,2,16,128]{3,2,1,0:T(8,128)S(1)}, f32[2,2,16,128]{3,2,1,0:T(8,128)S(1)}, u32[]{:S(2)}, u32[]{:S(2)}) %collective-permute-start.10) | collective-permute-done | bytes 32800 | tf_op jit(solution)/shard_map/ppermute | solution.py:70
  30.4 1.3 %gram.1 = (f32[16,4096]{1,0:T(8,128)S(1)}, f32[32,4,128]{2,1,0:T(4,128)S(1)}) custom-call(s32[1,2,8]{2,1,0:T(2,128)S(1)} %get-tuple-element.27.send, f32[16,4096]{1,0:T(8,128)S(1)} %get-tuple-element.38.partial_adjoint, f32[16,128]{1,0:T(8,128)S(1)} %get-tuple-element.39.squares, f32[3,2,16,128]{3,2,1,0:T(8,128)S(1)} %collective-permute-done.6.refs_0_, ...), custom_call_target="tpu_custom_call" | custom-call | tf_op jit(solution)/shard_map/gram/pallas_call | solution.py:323
  31.7 12.0 %all_to_all.5.packed = f32[32,4,128]{2,1,0:T(4,128)S(1)} all-to-all(f32[32,4,128]{2,1,0:T(4,128)S(1)} %get-tuple-element.46), channel_id=1, replica_groups=mesh['dom'=4,'sub'=8] {'dom','sub'}, dimensions={0} | all-to-all | bytes 131072 | tf_op jit(solution)/shard_map/all_to_all | solution.py:329
  43.8 2.8 %solve.1 = (f32[16,4096]{1,0:T(8,128)}, f32[16,16]{1,0:T(8,128)}, f32[1,16]{1,0:T(1,128)}) custom-call(f32[32,4,128]{2,1,0:T(4,128)S(1)} %all_to_all.5.packed, f32[16,4096]{1,0:T(8,128)S(1)} %get-tuple-element.47.adjoint), custom_call_target="tpu_custom_call" | custom-call | tf_op jit(solution)/shard_map/solve/pallas_call | solution.py:330
  (15 shorter events, 0.0 us)
Async XLA Ops:
  0.6 13.7 %copy-start = (bf16[224,128,128]{2,1,0:T(8,128)(2,1)S(1)}, bf16[224,128,128]{2,1,0:T(8,128)(2,1)}, u32[]{:S(2)}) copy-start(bf16[224,128,128]{2,1,0:T(8,128)(2,1)} %blocks.5) | copy-start | bytes 22020100
  1.8 8.6 %collective-permute-start = (bf16[3,2,16,128]{3,2,1,0:T(8,128)(2,1)S(1)}, bf16[3,2,16,128]{3,2,1,0:T(8,128)(2,1)S(1)}, u32[]{:S(2)}, u32[]{:S(2)}) collective-permute-start(bf16[3,2,16,128]{3,2,1,0:T(8,128)(2,1)S(1)} %get-tuple-element.31), channel_id=1, source_target_pairs={{0,1},{1,0},{2,3},{3,2},{4,5},{5,4},{6,7},{7,6},{8,9},{9,8},{10,11... | collective-permute-start | bytes 73736 | tf_op jit(solution)/shard_map/ppermute | solution.py:70
  2.3 13.7 %collective-permute-start.1 = (bf16[2,2,16,128]{3,2,1,0:T(8,128)(2,1)S(1)}, bf16[2,2,16,128]{3,2,1,0:T(8,128)(2,1)S(1)}, u32[]{:S(2)}, u32[]{:S(2)}) collective-permute-start(bf16[2,2,16,128]{3,2,1,0:T(8,128)(2,1)S(1)} %get-tuple-element.32), channel_id=1, source_target_pairs={{0,31},{1,2},{2,1},{3,4},{4,3},{5,6},{6,5},{7,8},{8,7},{9,10},{10,... | collective-permute-start | bytes 49160 | tf_op jit(solution)/shard_map/ppermute | solution.py:70
  8.9 7.2 %collective-permute-start.2 = (bf16[2,2,16,128]{3,2,1,0:T(8,128)(2,1)S(1)}, bf16[2,2,16,128]{3,2,1,0:T(8,128)(2,1)S(1)}, u32[]{:S(2)}, u32[]{:S(2)}) collective-permute-start(bf16[2,2,16,128]{3,2,1,0:T(8,128)(2,1)S(1)} %get-tuple-element.33), channel_id=1, source_target_pairs={{0,23},{1,10},{2,25},{3,12},{4,27},{5,14},{6,29},{7,16},{8,31},{9,... | collective-permute-start | bytes 49160 | tf_op jit(solution)/shard_map/ppermute | solution.py:70
  9.1 7.0 %collective-permute-start.3 = (bf16[2,2,16,128]{3,2,1,0:T(8,128)(2,1)S(1)}, bf16[2,2,16,128]{3,2,1,0:T(8,128)(2,1)S(1)}, u32[]{:S(2)}, u32[]{:S(2)}) collective-permute-start(bf16[2,2,16,128]{3,2,1,0:T(8,128)(2,1)S(1)} %get-tuple-element.34), channel_id=1, source_target_pairs={{0,7},{1,26},{2,9},{3,28},{4,11},{5,30},{6,13},{7,0},{8,15},{9,2},... | collective-permute-start | bytes 49160 | tf_op jit(solution)/shard_map/ppermute | solution.py:70
  10.4 5.6 %collective-permute-start.4 = (bf16[2,2,16,128]{3,2,1,0:T(8,128)(2,1)S(1)}, bf16[2,2,16,128]{3,2,1,0:T(8,128)(2,1)S(1)}, u32[]{:S(2)}, u32[]{:S(2)}) collective-permute-start(bf16[2,2,16,128]{3,2,1,0:T(8,128)(2,1)S(1)} %pad_maximum_fusion.2), channel_id=1, source_target_pairs={{0,8},{1,9},{2,10},{3,11},{4,12},{5,13},{6,14},{7,15},{8,16},{9,17... | collective-permute-start | bytes 49160 | tf_op jit(solution)/shard_map/ppermute | solution.py:70
  12.1 4.2 %collective-permute-start.5 = (bf16[2,2,16,128]{3,2,1,0:T(8,128)(2,1)S(1)}, bf16[2,2,16,128]{3,2,1,0:T(8,128)(2,1)S(1)}, u32[]{:S(2)}, u32[]{:S(2)}) collective-permute-start(bf16[2,2,16,128]{3,2,1,0:T(8,128)(2,1)S(1)} %pad_maximum_fusion.3), channel_id=1, source_target_pairs={{0,24},{1,25},{2,26},{3,27},{4,28},{5,29},{6,30},{7,31},{8,0},{9,1... | collective-permute-start | bytes 49160 | tf_op jit(solution)/shard_map/ppermute | solution.py:70
  18.8 5.8 %collective-permute-start.6 = (f32[3,2,16,128]{3,2,1,0:T(8,128)S(1)}, f32[3,2,16,128]{3,2,1,0:T(8,128)S(1)}, u32[]{:S(2)}, u32[]{:S(2)}) collective-permute-start(f32[3,2,16,128]{3,2,1,0:T(8,128)S(1)} %get-tuple-element.40), channel_id=1, source_target_pairs={{0,1},{1,0},{2,3},{3,2},{4,5},{5,4},{6,7},{7,6},{8,9},{9,8},{10,11... | collective-permute-start | bytes 147464 | tf_op jit(solution)/shard_map/ppermute | solution.py:70
  18.9 10.8 %collective-permute-start.7 = (f32[2,2,16,128]{3,2,1,0:T(8,128)S(1)}, f32[2,2,16,128]{3,2,1,0:T(8,128)S(1)}, u32[]{:S(2)}, u32[]{:S(2)}) collective-permute-start(f32[2,2,16,128]{3,2,1,0:T(8,128)S(1)} %get-tuple-element.41), channel_id=1, source_target_pairs={{0,31},{1,2},{2,1},{3,4},{4,3},{5,6},{6,5},{7,8},{8,7},{9,10},{10,... | collective-permute-start | bytes 98312 | tf_op jit(solution)/shard_map/ppermute | solution.py:70
  22.2 7.5 %collective-permute-start.8 = (f32[2,2,16,128]{3,2,1,0:T(8,128)S(1)}, f32[2,2,16,128]{3,2,1,0:T(8,128)S(1)}, u32[]{:S(2)}, u32[]{:S(2)}) collective-permute-start(f32[2,2,16,128]{3,2,1,0:T(8,128)S(1)} %get-tuple-element.42), channel_id=1, source_target_pairs={{0,23},{1,10},{2,25},{3,12},{4,27},{5,14},{6,29},{7,16},{8,31},{9,... | collective-permute-start | bytes 98312 | tf_op jit(solution)/shard_map/ppermute | solution.py:70
  24.6 5.1 %collective-permute-start.9 = (f32[2,2,16,128]{3,2,1,0:T(8,128)S(1)}, f32[2,2,16,128]{3,2,1,0:T(8,128)S(1)}, u32[]{:S(2)}, u32[]{:S(2)}) collective-permute-start(f32[2,2,16,128]{3,2,1,0:T(8,128)S(1)} %get-tuple-element.43), channel_id=1, source_target_pairs={{0,7},{1,26},{2,9},{3,28},{4,11},{5,30},{6,13},{7,0},{8,15},{9,2},... | collective-permute-start | bytes 98312 | tf_op jit(solution)/shard_map/ppermute | solution.py:70
  24.7 5.8 %collective-permute-start.10 = (f32[2,2,16,128]{3,2,1,0:T(8,128)S(1)}, f32[2,2,16,128]{3,2,1,0:T(8,128)S(1)}, u32[]{:S(2)}, u32[]{:S(2)}) collective-permute-start(f32[2,2,16,128]{3,2,1,0:T(8,128)S(1)} %pad_maximum_fusion), channel_id=1, source_target_pairs={{0,8},{1,9},{2,10},{3,11},{4,12},{5,13},{6,14},{7,15},{8,16},{9,17... | collective-permute-start | bytes 98312 | tf_op jit(solution)/shard_map/ppermute | solution.py:70
  25.4 5.1 %collective-permute-start.11 = (f32[2,2,16,128]{3,2,1,0:T(8,128)S(1)}, f32[2,2,16,128]{3,2,1,0:T(8,128)S(1)}, u32[]{:S(2)}, u32[]{:S(2)}) collective-permute-start(f32[2,2,16,128]{3,2,1,0:T(8,128)S(1)} %pad_maximum_fusion.1), channel_id=1, source_target_pairs={{0,24},{1,25},{2,26},{3,27},{4,28},{5,29},{6,30},{7,31},{8,0},{9,1... | collective-permute-start | bytes 98312 | tf_op jit(solution)/shard_map/ppermute | solution.py:70

commit v4 on v3

--- a/solution.py
+++ b/solution.py
@@ -28,8 +28,10 @@
     return place - (place > 4)
 
 
-def outward():
-    return 2 * lax.rem(lax.axis_index("sub"), 2) - 1
+def directions():
+    outer, inner = lax.axis_index("dom"), lax.axis_index("sub")
+    past = (inner == lax.axis_size("sub") - 1).astype(jnp.int32)
+    return 2 * lax.rem(inner, 2) - 1, 1 - 2 * lax.rem(outer + past, 2), 1 - 2 * lax.rem(outer, 2)
 
 
 def columns(block_row):
@@ -40,46 +42,52 @@
     return jnp.concatenate([ref[place] for place in places], axis=axis)
 
 
-def sent(s):
+def sent(s, t, u):
     return (
-        ((0, -s), (1, -s), (-1, -s)),
+        ((0, -s), (u, -s), (-u, -s)),
+        ((-t, s),),
         ((0, s),),
-        ((s, s),),
-        ((-s, s),),
-        ((1, 0),),
-        ((-1, 0),),
-    )
-
-
-def received(s):
+        ((t, s),),
+        ((-u, 0),),
+        ((u, 0),),
+    )
+
+
+def received(s, t, u):
     return (
         ((0, s),),
+        ((t, -s),),
         ((0, -s),),
-        ((-s, -s),),
-        ((s, -s),),
-        ((1, 0), (1, s)),
-        ((-1, 0), (-1, s)),
-    )
-
-
-def exchange(pair, side, outer, inner, up, down):
+        ((-t, -s),),
+        ((u, 0), (u, s)),
+        ((-u, 0), (-u, s)),
+    )
+
+
+def exchange(pair, cross_far, side, cross_near, far, near):
     n_inner = lax.axis_size("sub")
     devices = lax.axis_size("dom") * n_inner
 
-    def move(array, odd, even):
-        return lax.ppermute(
-            array,
-            AXES,
-            [(d, (d + (odd if d % 2 else even)) % devices) for d in range(devices)],
-        )
-
-    pair = move(pair, -1, 1)
-    side = move(side, 1, -1)
-    outer = move(outer, n_inner + 1, -n_inner - 1)
-    inner = move(inner, 1 - n_inner, n_inner - 1)
-    up = move(jnp.concatenate([up, pair[1:2]], axis=0), n_inner, n_inner)
-    down = move(jnp.concatenate([down, pair[2:3]], axis=0), -n_inner, -n_inner)
-    return pair, side, outer, inner, up, down
+    def swap(array, target):
+        return lax.ppermute(array, AXES, [(d, target(d) % devices) for d in range(devices)])
+
+    def step(d):
+        return 1 if d % 2 else -1
+
+    def towards(d):
+        return n_inner if (d // n_inner) % 2 == 0 else -n_inner
+
+    def diagonal(d, sign):
+        past = (d + d % 2) % devices
+        return d + step(d) + sign * towards(past)
+
+    pair = swap(pair, lambda d: d - step(d))
+    cross_far = swap(cross_far, lambda d: diagonal(d, -1))
+    side = swap(side, lambda d: d + step(d))
+    cross_near = swap(cross_near, lambda d: diagonal(d, 1))
+    far = swap(jnp.concatenate([far, pair[2:3]], axis=0), lambda d: d - towards(d))
+    near = swap(jnp.concatenate([near, pair[1:2]], axis=0), lambda d: d + towards(d))
+    return pair, cross_far, side, cross_near, far, near
 
 
 def gather_kernel(send_hbm, vectors_hbm, ptr_hbm, col_hbm, blocks_hbm, vectors, ptr, col, send_out, *refs):
@@ -100,7 +108,7 @@
         copy.start()
     for copy in copies:
         copy.wait()
-    for ref, offsets in zip(outgoing, sent(outward())):
+    for ref, offsets in zip(outgoing, sent(*directions())):
         for i, (a, b) in enumerate(offsets):
             for g in range(ref.shape[1]):
                 ref[i, g] = vectors[:, columns(send[0, g, neighbour(a, b)])]
@@ -127,8 +135,8 @@
     ghosts, total, spread, long_rows = refs[13:]
     rows = image.shape[0]
     many = long_rows.shape[0] - 1
-    s = outward()
-    for ref, offsets in zip(arrived, received(s)):
+    way = directions()
+    for ref, offsets in zip(arrived, received(*way)):
         for i, (a, b) in enumerate(offsets):
             for g in range(ref.shape[1]):
                 ghosts[neighbour(a, b) * ref.shape[1] + g] = ref[i, g]
@@ -170,7 +178,7 @@
         backward(j, LOCAL, SHORT)
     for i in range(many):
         backward(long_rows[i], SHORT, LONG)
-    for ref, offsets in zip(outgoing, sent(s)):
+    for ref, offsets in zip(outgoing, sent(*way)):
         for i, (a, b) in enumerate(offsets):
             for g in range(ref.shape[1]):
                 slot = neighbour(-a, -b) * ref.shape[1] + g
@@ -205,9 +213,9 @@
 def gram_kernel(send, partial_adjoint, squares, *refs):
     arrived, adjoint, packed = refs[:6], refs[6], refs[7]
     k = adjoint.shape[0]
-    s = outward()
+    way = directions()
     adjoint[...] = partial_adjoint[...]
-    for ref, offsets in zip(arrived, received(s)):
+    for ref, offsets in zip(arrived, received(*way)):
         for i, (a, b) in enumerate(offsets):
             for g in range(ref.shape[1]):
                 place = columns(send[0, g, neighbour(-a, -b)])

time: 46.7 us -> 45.7 us (0.979)
  starting transfers between devices: 22.2 us -> 19.5 us
  waiting for transfers between devices: 0.86 us -> 3.47 us
  blocking collectives: 12 us -> 11.1 us
    ppermute x12, starting transfers between devices: 22.2 us -> 19.5 us  [swap(): lax.ppermute(array, AXES, [(d, target(d) % devices) for d in range(device...]
    ppermute x12, waiting for transfers between devices: 0.86 us -> 3.47 us  [swap(): lax.ppermute(array, AXES, [(d, target(d) % devices) for d in range(device...]
    all_to_all x1, blocking collectives: 12 us -> 11.1 us  [local(): everywhere = lax.all_to_all(packed, AXES, 0, 0)]
  transfers between devices with their start and end apart: 12 -> 12, of which waited for: 2 -> 3; matrix products, arithmetic and copies ran while one was open for 0% -> 0% of each run, Pallas kernels for 6% -> 6%
where the time goes in v4:
time: 45.7 us; the launch traced here: 45.5 us
  starting transfers between devices  19.5 us (43%)
  blocking collectives  11.1 us (24%)
  Pallas kernels  10.7 us (23%)
  waiting for transfers between devices  3.47 us (8%)
  between operations  0.72 us (2%)
    ppermute x12, starting transfers between devices, swap(): lax.ppermute(array, AXES, [(d, target(d) % devices) for d in range(device...  19.5 us
    all_to_all x1, blocking collectives, local(): everywhere = lax.all_to_all(packed, AXES, 0, 0)  11.1 us
    ppermute x12, waiting for transfers between devices, swap(): lax.ppermute(array, AXES, [(d, target(d) % devices) for d in range(device...  3.47 us
    pallas_call x1, Pallas kernels, local(): call(functools.partial(solve_kernel, unknowns * devices), 'solve', [((k,...  2.81 us
    pallas_call x1, Pallas kernels, local(): call(ghost_kernel, 'ghost', [((rows, k, B), BF16)] + [((n, ghost, k, B),...  2.56 us
    pallas_call x1, Pallas kernels, local(): call(local_forward_kernel, 'local_forward', [((rows, k, B), F32)], [SMEM,...  1.73 us
    pallas_call x1, Pallas kernels, local(): call(gram_kernel, 'gram', [((k, unknowns), F32), ((devices, 4, B), F32)],...  1.28 us
    pallas_call x1, Pallas kernels, local(): call(local_backward_kernel, 'local_backward', [((k, unknowns), F32), ((k,...  1.19 us
  transfers between devices with their start and end apart: 12, of which 3 were waited for; matrix products, arithmetic and copies ran while one was open for 0% of the time, Pallas kernels for 6%

profile of v4, /device:TPU:0, one launch (start us, length us, event | category | flops | bytes accessed | tf_op | source)
XLA Modules:
  0.0 45.5 jit_solution(6316643413397638880)
XLA Ops:
  0.6 1.1 %gather.1 = (bf16[16,4096]{1,0:T(8,128)(2,1)S(1)}, s32[1,33]{1,0:T(1,128)S(1)}, s32[1,224]{1,0:T(1,128)S(1)}, s32[1,2,8]{2,1,0:T(2,128)S(1)}, bf16[3,2,16,128]{3...) custom-call(s32[1,2,8]{2,1,0:T(2,128)} %bitcast.2, ...), custom_call_target="tpu_custom_call" | custom-call | tf_op jit(solution)/shard_map/gather/pallas_call | solution.py:289
  1.8 0.5 %collective-permute-start = (bf16[3,2,16,128]{3,2,1,0:T(8,128)(2,1)S(1)}, bf16[3,2,16,128]{3,2,1,0:T(8,128)(2,1)S(1)}, u32[]{:S(2)}, u32[]{:S(2)}) collective-permute-start(bf16[3,2,16,128]{3,2,1,0:T(8,128)(2,1)S(1)} %get-tuple-element.31), channel_id=1, source_target_pairs={{0,1},{1,0},{2,3},{3,2},{4,5},{5,4},{6,7},{7,6},{8,9},{9,8},{10,11... | collective-permute-start | bytes 73736 | tf_op jit(solution)/shard_map/ppermute | solution.py:72
  2.3 5.6 %collective-permute-start.1 = (bf16[2,2,16,128]{3,2,1,0:T(8,128)(2,1)S(1)}, bf16[2,2,16,128]{3,2,1,0:T(8,128)(2,1)S(1)}, u32[]{:S(2)}, u32[]{:S(2)}) collective-permute-start(bf16[2,2,16,128]{3,2,1,0:T(8,128)(2,1)S(1)} %get-tuple-element.32), channel_id=1, source_target_pairs={{0,23},{1,26},{2,25},{3,28},{4,27},{5,30},{6,29},{7,16},{8,15},{9,... | collective-permute-start | bytes 49160 | tf_op jit(solution)/shard_map/ppermute | solution.py:72
  7.9 1.2 %collective-permute-start.2 = (bf16[2,2,16,128]{3,2,1,0:T(8,128)(2,1)S(1)}, bf16[2,2,16,128]{3,2,1,0:T(8,128)(2,1)S(1)}, u32[]{:S(2)}, u32[]{:S(2)}) collective-permute-start(bf16[2,2,16,128]{3,2,1,0:T(8,128)(2,1)S(1)} %get-tuple-element.33), channel_id=1, source_target_pairs={{0,31},{1,2},{2,1},{3,4},{4,3},{5,6},{6,5},{7,8},{8,7},{9,10},{10,... | collective-permute-start | bytes 49160 | tf_op jit(solution)/shard_map/ppermute | solution.py:72
  9.1 0.5 %collective-permute-start.3 = (bf16[2,2,16,128]{3,2,1,0:T(8,128)(2,1)S(1)}, bf16[2,2,16,128]{3,2,1,0:T(8,128)(2,1)S(1)}, u32[]{:S(2)}, u32[]{:S(2)}) collective-permute-start(bf16[2,2,16,128]{3,2,1,0:T(8,128)(2,1)S(1)} %get-tuple-element.34), channel_id=1, source_target_pairs={{0,7},{1,10},{2,9},{3,12},{4,11},{5,14},{6,13},{7,0},{8,31},{9,2},... | collective-permute-start | bytes 49160 | tf_op jit(solution)/shard_map/ppermute | solution.py:72
  9.5 3.2 %collective-permute-start.4 = (bf16[2,2,16,128]{3,2,1,0:T(8,128)(2,1)S(1)}, bf16[2,2,16,128]{3,2,1,0:T(8,128)(2,1)S(1)}, u32[]{:S(2)}, u32[]{:S(2)}) collective-permute-start(bf16[2,2,16,128]{3,2,1,0:T(8,128)(2,1)S(1)} %pad_maximum_fusion.2), channel_id=1, source_target_pairs={{0,24},{1,25},{2,26},{3,27},{4,28},{5,29},{6,30},{7,31},{8,16},{9,... | collective-permute-start | bytes 49160 | tf_op jit(solution)/shard_map/ppermute | solution.py:72
  12.8 1.2 %collective-permute-start.5 = (bf16[2,2,16,128]{3,2,1,0:T(8,128)(2,1)S(1)}, bf16[2,2,16,128]{3,2,1,0:T(8,128)(2,1)S(1)}, u32[]{:S(2)}, u32[]{:S(2)}) collective-permute-start(bf16[2,2,16,128]{3,2,1,0:T(8,128)(2,1)S(1)} %pad_maximum_fusion.3), channel_id=1, source_target_pairs={{0,8},{1,9},{2,10},{3,11},{4,12},{5,13},{6,14},{7,15},{8,0},{9,1},... | collective-permute-start | bytes 49160 | tf_op jit(solution)/shard_map/ppermute | solution.py:72
  14.0 1.7 %local_forward.1.partial_image = f32[32,16,128]{2,1,0:T(8,128)S(1)} custom-call(s32[1,33]{1,0:T(1,128)S(1)} %get-tuple-element.28.ptr, bf16[16,4096]{1,0:T(8,128)(2,1)S(1)} %get-tuple-element.30.vectors, bf16[224,128,128]{2,1,0:T(8,128)(2,1)S(1)} %copy-done), custom_call_target="tpu_custom_call" | custom-call | flops 50331648 | bytes 3145728 | tf_op jit(solution)/shard_map/local_forward/pallas_call | solution.py:300
  15.7 0.0 collective-permute-done.3.refs_3_
  15.7 0.7 %collective-permute-done.5.refs_5_ = bf16[2,2,16,128]{3,2,1,0:T(8,128)(2,1)S(1)} collective-permute-done((bf16[2,2,16,128]{3,2,1,0:T(8,128)(2,1)S(1)}, bf16[2,2,16,128]{3,2,1,0:T(8,128)(2,1)S(1)}, u32[]{:S(2)}, u32[]{:S(2)}) %collective-permute-start.5) | collective-permute-done | bytes 16416 | tf_op jit(solution)/shard_map/ppermute | solution.py:72
  16.5 2.6 %ghost.1 = (bf16[32,16,128]{2,1,0:T(8,128)(2,1)S(1)}, f32[3,2,16,128]{3,2,1,0:T(8,128)S(1)}, f32[2,2,16,128]{3,2,1,0:T(8,128)S(1)}, f32[2,2,16,128]{3,2,1,0:T(8,...) custom-call(s32[1,33]{1,0:T(1,128)S(1)} %get-tuple-element.28.ptr, ...), custom_call_target="tpu_custom_call" | custom-call | flops 134217728 | bytes 8388608 | tf_op jit(solution)/shard_map/ghost/pallas_call | solution.py:308
  19.1 0.1 collective-permute-start.6
  19.1 1.0 %collective-permute-start.7 = (f32[2,2,16,128]{3,2,1,0:T(8,128)S(1)}, f32[2,2,16,128]{3,2,1,0:T(8,128)S(1)}, u32[]{:S(2)}, u32[]{:S(2)}) collective-permute-start(f32[2,2,16,128]{3,2,1,0:T(8,128)S(1)} %get-tuple-element.41), channel_id=1, source_target_pairs={{0,23},{1,26},{2,25},{3,28},{4,27},{5,30},{6,29},{7,16},{8,15},{9,... | collective-permute-start | bytes 98312 | tf_op jit(solution)/shard_map/ppermute | solution.py:72
  20.1 3.3 %collective-permute-start.8 = (f32[2,2,16,128]{3,2,1,0:T(8,128)S(1)}, f32[2,2,16,128]{3,2,1,0:T(8,128)S(1)}, u32[]{:S(2)}, u32[]{:S(2)}) collective-permute-start(f32[2,2,16,128]{3,2,1,0:T(8,128)S(1)} %get-tuple-element.42), channel_id=1, source_target_pairs={{0,31},{1,2},{2,1},{3,4},{4,3},{5,6},{6,5},{7,8},{8,7},{9,10},{10,... | collective-permute-start | bytes 98312 | tf_op jit(solution)/shard_map/ppermute | solution.py:72
  23.4 0.5 %collective-permute-start.9 = (f32[2,2,16,128]{3,2,1,0:T(8,128)S(1)}, f32[2,2,16,128]{3,2,1,0:T(8,128)S(1)}, u32[]{:S(2)}, u32[]{:S(2)}) collective-permute-start(f32[2,2,16,128]{3,2,1,0:T(8,128)S(1)} %get-tuple-element.43), channel_id=1, source_target_pairs={{0,7},{1,10},{2,9},{3,12},{4,11},{5,14},{6,13},{7,0},{8,31},{9,2},... | collective-permute-start | bytes 98312 | tf_op jit(solution)/shard_map/ppermute | solution.py:72
  23.9 2.5 %collective-permute-start.10 = (f32[2,2,16,128]{3,2,1,0:T(8,128)S(1)}, f32[2,2,16,128]{3,2,1,0:T(8,128)S(1)}, u32[]{:S(2)}, u32[]{:S(2)}) collective-permute-start(f32[2,2,16,128]{3,2,1,0:T(8,128)S(1)} %pad_maximum_fusion), channel_id=1, source_target_pairs={{0,24},{1,25},{2,26},{3,27},{4,28},{5,29},{6,30},{7,31},{8,16},{9,... | collective-permute-start | bytes 98312 | tf_op jit(solution)/shard_map/ppermute | solution.py:72
  26.4 1.2 %local_backward.1 = (f32[16,4096]{1,0:T(8,128)S(1)}, f32[16,128]{1,0:T(8,128)S(1)}) custom-call(s32[1,33]{1,0:T(1,128)S(1)} %get-tuple-element.28.ptr, bf16[224,128,128]{2,1,0:T(8,128)(2,1)S(1)} %copy-done, bf16[32,16,128]{2,1,0:T(8,128)(2,1)S(1)} %get-tuple-element.37.image), custom_call_target="tpu_custom_call" | custom-call | flops 50331648 | bytes 3145728 | tf_op jit(solution)/shard_map/local_backward/pallas_call | solution.py:323
  27.6 0.0 collective-permute-done.8.refs_2_
  27.6 0.0 collective-permute-done.9.refs_3_
  27.6 2.1 %collective-permute-done.10.refs_4_ = f32[2,2,16,128]{3,2,1,0:T(8,128)S(1)} collective-permute-done((f32[2,2,16,128]{3,2,1,0:T(8,128)S(1)}, f32[2,2,16,128]{3,2,1,0:T(8,128)S(1)}, u32[]{:S(2)}, u32[]{:S(2)}) %collective-permute-start.10) | collective-permute-done | bytes 32800 | tf_op jit(solution)/shard_map/ppermute | solution.py:72
  29.8 0.5 %collective-permute-done.11.refs_5_ = f32[2,2,16,128]{3,2,1,0:T(8,128)S(1)} collective-permute-done((f32[2,2,16,128]{3,2,1,0:T(8,128)S(1)}, f32[2,2,16,128]{3,2,1,0:T(8,128)S(1)}, u32[]{:S(2)}, u32[]{:S(2)}) %collective-permute-start.11) | collective-permute-done | bytes 32800 | tf_op jit(solution)/shard_map/ppermute | solution.py:72
  30.3 1.3 %gram.1 = (f32[16,4096]{1,0:T(8,128)S(1)}, f32[32,4,128]{2,1,0:T(4,128)S(1)}) custom-call(s32[1,2,8]{2,1,0:T(2,128)S(1)} %get-tuple-element.27.send, f32[16,4096]{1,0:T(8,128)S(1)} %get-tuple-element.38.partial_adjoint, f32[16,128]{1,0:T(8,128)S(1)} %get-tuple-element.39.squares, f32[3,2,16,128]{3,2,1,0:T(8,128)S(1)} %collective-permute-done.6.refs_0_, ...), custom_call_target="tpu_custom_call" | custom-call | tf_op jit(solution)/shard_map/gram/pallas_call | solution.py:331
  31.6 11.1 %all_to_all.5.packed = f32[32,4,128]{2,1,0:T(4,128)S(1)} all-to-all(f32[32,4,128]{2,1,0:T(4,128)S(1)} %get-tuple-element.46), channel_id=1, replica_groups=mesh['dom'=4,'sub'=8] {'dom','sub'}, dimensions={0} | all-to-all | bytes 131072 | tf_op jit(solution)/shard_map/all_to_all | solution.py:337
  42.7 2.8 %solve.1 = (f32[16,4096]{1,0:T(8,128)}, f32[16,16]{1,0:T(8,128)}, f32[1,16]{1,0:T(1,128)}) custom-call(f32[32,4,128]{2,1,0:T(4,128)S(1)} %all_to_all.5.packed, f32[16,4096]{1,0:T(8,128)S(1)} %get-tuple-element.47.adjoint), custom_call_target="tpu_custom_call" | custom-call | tf_op jit(solution)/shard_map/solve/pallas_call | solution.py:338
  (15 shorter events, 0.0 us)
Async XLA Ops:
  0.6 13.3 %copy-start = (bf16[224,128,128]{2,1,0:T(8,128)(2,1)S(1)}, bf16[224,128,128]{2,1,0:T(8,128)(2,1)}, u32[]{:S(2)}) copy-start(bf16[224,128,128]{2,1,0:T(8,128)(2,1)} %blocks.5) | copy-start | bytes 22020100
  1.8 7.7 %collective-permute-start = (bf16[3,2,16,128]{3,2,1,0:T(8,128)(2,1)S(1)}, bf16[3,2,16,128]{3,2,1,0:T(8,128)(2,1)S(1)}, u32[]{:S(2)}, u32[]{:S(2)}) collective-permute-start(bf16[3,2,16,128]{3,2,1,0:T(8,128)(2,1)S(1)} %get-tuple-element.31), channel_id=1, source_target_pairs={{0,1},{1,0},{2,3},{3,2},{4,5},{5,4},{6,7},{7,6},{8,9},{9,8},{10,11... | collective-permute-start | bytes 73736 | tf_op jit(solution)/shard_map/ppermute | solution.py:72
  2.3 13.4 %collective-permute-start.1 = (bf16[2,2,16,128]{3,2,1,0:T(8,128)(2,1)S(1)}, bf16[2,2,16,128]{3,2,1,0:T(8,128)(2,1)S(1)}, u32[]{:S(2)}, u32[]{:S(2)}) collective-permute-start(bf16[2,2,16,128]{3,2,1,0:T(8,128)(2,1)S(1)} %get-tuple-element.32), channel_id=1, source_target_pairs={{0,23},{1,26},{2,25},{3,28},{4,27},{5,30},{6,29},{7,16},{8,15},{9,... | collective-permute-start | bytes 49160 | tf_op jit(solution)/shard_map/ppermute | solution.py:72
  7.9 7.8 %collective-permute-start.2 = (bf16[2,2,16,128]{3,2,1,0:T(8,128)(2,1)S(1)}, bf16[2,2,16,128]{3,2,1,0:T(8,128)(2,1)S(1)}, u32[]{:S(2)}, u32[]{:S(2)}) collective-permute-start(bf16[2,2,16,128]{3,2,1,0:T(8,128)(2,1)S(1)} %get-tuple-element.33), channel_id=1, source_target_pairs={{0,31},{1,2},{2,1},{3,4},{4,3},{5,6},{6,5},{7,8},{8,7},{9,10},{10,... | collective-permute-start | bytes 49160 | tf_op jit(solution)/shard_map/ppermute | solution.py:72
  9.1 6.7 %collective-permute-start.3 = (bf16[2,2,16,128]{3,2,1,0:T(8,128)(2,1)S(1)}, bf16[2,2,16,128]{3,2,1,0:T(8,128)(2,1)S(1)}, u32[]{:S(2)}, u32[]{:S(2)}) collective-permute-start(bf16[2,2,16,128]{3,2,1,0:T(8,128)(2,1)S(1)} %get-tuple-element.34), channel_id=1, source_target_pairs={{0,7},{1,10},{2,9},{3,12},{4,11},{5,14},{6,13},{7,0},{8,31},{9,2},... | collective-permute-start | bytes 49160 | tf_op jit(solution)/shard_map/ppermute | solution.py:72
  9.5 6.2 %collective-permute-start.4 = (bf16[2,2,16,128]{3,2,1,0:T(8,128)(2,1)S(1)}, bf16[2,2,16,128]{3,2,1,0:T(8,128)(2,1)S(1)}, u32[]{:S(2)}, u32[]{:S(2)}) collective-permute-start(bf16[2,2,16,128]{3,2,1,0:T(8,128)(2,1)S(1)} %pad_maximum_fusion.2), channel_id=1, source_target_pairs={{0,24},{1,25},{2,26},{3,27},{4,28},{5,29},{6,30},{7,31},{8,16},{9,... | collective-permute-start | bytes 49160 | tf_op jit(solution)/shard_map/ppermute | solution.py:72
  12.8 3.7 %collective-permute-start.5 = (bf16[2,2,16,128]{3,2,1,0:T(8,128)(2,1)S(1)}, bf16[2,2,16,128]{3,2,1,0:T(8,128)(2,1)S(1)}, u32[]{:S(2)}, u32[]{:S(2)}) collective-permute-start(bf16[2,2,16,128]{3,2,1,0:T(8,128)(2,1)S(1)} %pad_maximum_fusion.3), channel_id=1, source_target_pairs={{0,8},{1,9},{2,10},{3,11},{4,12},{5,13},{6,14},{7,15},{8,0},{9,1},... | collective-permute-start | bytes 49160 | tf_op jit(solution)/shard_map/ppermute | solution.py:72
  19.1 4.8 %collective-permute-start.6 = (f32[3,2,16,128]{3,2,1,0:T(8,128)S(1)}, f32[3,2,16,128]{3,2,1,0:T(8,128)S(1)}, u32[]{:S(2)}, u32[]{:S(2)}) collective-permute-start(f32[3,2,16,128]{3,2,1,0:T(8,128)S(1)} %get-tuple-element.40), channel_id=1, source_target_pairs={{0,1},{1,0},{2,3},{3,2},{4,5},{5,4},{6,7},{7,6},{8,9},{9,8},{10,11... | collective-permute-start | bytes 147464 | tf_op jit(solution)/shard_map/ppermute | solution.py:72
  19.1 8.5 %collective-permute-start.7 = (f32[2,2,16,128]{3,2,1,0:T(8,128)S(1)}, f32[2,2,16,128]{3,2,1,0:T(8,128)S(1)}, u32[]{:S(2)}, u32[]{:S(2)}) collective-permute-start(f32[2,2,16,128]{3,2,1,0:T(8,128)S(1)} %get-tuple-element.41), channel_id=1, source_target_pairs={{0,23},{1,26},{2,25},{3,28},{4,27},{5,30},{6,29},{7,16},{8,15},{9,... | collective-permute-start | bytes 98312 | tf_op jit(solution)/shard_map/ppermute | solution.py:72
  20.1 7.5 %collective-permute-start.8 = (f32[2,2,16,128]{3,2,1,0:T(8,128)S(1)}, f32[2,2,16,128]{3,2,1,0:T(8,128)S(1)}, u32[]{:S(2)}, u32[]{:S(2)}) collective-permute-start(f32[2,2,16,128]{3,2,1,0:T(8,128)S(1)} %get-tuple-element.42), channel_id=1, source_target_pairs={{0,31},{1,2},{2,1},{3,4},{4,3},{5,6},{6,5},{7,8},{8,7},{9,10},{10,... | collective-permute-start | bytes 98312 | tf_op jit(solution)/shard_map/ppermute | solution.py:72
  23.4 4.2 %collective-permute-start.9 = (f32[2,2,16,128]{3,2,1,0:T(8,128)S(1)}, f32[2,2,16,128]{3,2,1,0:T(8,128)S(1)}, u32[]{:S(2)}, u32[]{:S(2)}) collective-permute-start(f32[2,2,16,128]{3,2,1,0:T(8,128)S(1)} %get-tuple-element.43), channel_id=1, source_target_pairs={{0,7},{1,10},{2,9},{3,12},{4,11},{5,14},{6,13},{7,0},{8,31},{9,2},... | collective-permute-start | bytes 98312 | tf_op jit(solution)/shard_map/ppermute | solution.py:72
  23.9 5.9 %collective-permute-start.10 = (f32[2,2,16,128]{3,2,1,0:T(8,128)S(1)}, f32[2,2,16,128]{3,2,1,0:T(8,128)S(1)}, u32[]{:S(2)}, u32[]{:S(2)}) collective-permute-start(f32[2,2,16,128]{3,2,1,0:T(8,128)S(1)} %pad_maximum_fusion), channel_id=1, source_target_pairs={{0,24},{1,25},{2,26},{3,27},{4,28},{5,29},{6,30},{7,31},{8,16},{9,... | collective-permute-start | bytes 98312 | tf_op jit(solution)/shard_map/ppermute | solution.py:72
  26.4 3.9 %collective-permute-start.11 = (f32[2,2,16,128]{3,2,1,0:T(8,128)S(1)}, f32[2,2,16,128]{3,2,1,0:T(8,128)S(1)}, u32[]{:S(2)}, u32[]{:S(2)}) collective-permute-start(f32[2,2,16,128]{3,2,1,0:T(8,128)S(1)} %pad_maximum_fusion.1), channel_id=1, source_target_pairs={{0,8},{1,9},{2,10},{3,11},{4,12},{5,13},{6,14},{7,15},{8,0},{9,1},... | collective-permute-start | bytes 98312 | tf_op jit(solution)/shard_map/ppermute | solution.py:72

commit v5 on v4

--- a/solution.py
+++ b/solution.py
@@ -90,8 +90,12 @@
     return pair, cross_far, side, cross_near, far, near
 
 
-def gather_kernel(send_hbm, vectors_hbm, ptr_hbm, col_hbm, blocks_hbm, vectors, ptr, col, send_out, *refs):
-    outgoing, (send, sems) = refs[:6], refs[6:]
+def rounded(size):
+    return -(-size // B) * B
+
+
+def gather_kernel(send_hbm, vectors_hbm, ptr_hbm, col_hbm, blocks_hbm, vectors, plan, send_lines, *refs):
+    outgoing, (send, ptr, col, sems) = refs[:6], refs[6:]
     copies = [
         pltpu.make_async_copy(source, target, sems.at[i])
         for i, (source, target) in enumerate(
@@ -100,7 +104,7 @@
                 (vectors_hbm, vectors),
                 (ptr_hbm, ptr),
                 (col_hbm, col),
-                (send_hbm, send_out),
+                (send_hbm, send_lines),
             )
         )
     ]
@@ -114,13 +118,15 @@
                 ref[i, g] = vectors[:, columns(send[0, g, neighbour(a, b)])]
         for i in range(len(offsets), ref.shape[0]):
             ref[i] = ref[0]
-
-
-def local_forward_kernel(ptr, vectors, blocks, *refs):
+    plan[:, : ptr.shape[1]] = ptr[...]
+    plan[:, rounded(ptr.shape[1]) : rounded(ptr.shape[1]) + col.shape[1]] = col[...]
+
+
+def local_forward_kernel(plan, vectors, blocks, *refs):
     image = refs[-1]
     rows = image.shape[0]
     for j in range(rows):
-        e = ptr[0, j]
+        e = plan[0, j]
         near = [vectors[:, c * B : c * B + B] for c in (j, (j + 1) % rows, (j - 1) % rows)]
         image[j] = lax.dot_general(
             jnp.concatenate(near, axis=1),
@@ -130,11 +136,12 @@
         )
 
 
-def ghost_kernel(ptr, col, blocks, partial_image, *refs):
+def ghost_kernel(plan, blocks, partial_image, *refs):
     arrived, image, outgoing = refs[:6], refs[6], refs[7:13]
     ghosts, total, spread, long_rows = refs[13:]
     rows = image.shape[0]
     many = long_rows.shape[0] - 1
+    first_column = rounded(rows + 1)
     way = directions()
     for ref, offsets in zip(arrived, received(*way)):
         for i, (a, b) in enumerate(offsets):
@@ -143,27 +150,27 @@
     found = 0
     for j in range(rows):
         long_rows[jnp.minimum(found, many)] = j
-        found = found + (ptr[0, j + 1] - ptr[0, j] > SHORT).astype(jnp.int32)
+        found = found + (plan[0, j + 1] - plan[0, j] > SHORT).astype(jnp.int32)
 
     def forward(e, first, last):
         return lax.dot_general(
-            joined(ghosts, [col[0, e + t] - rows for t in range(first, last)], 1),
+            joined(ghosts, [plan[0, first_column + e + t] - rows for t in range(first, last)], 1),
             joined(blocks, [e + t for t in range(first, last)], 1),
             BY_LAST,
             preferred_element_type=F32,
         )
 
     for j in range(rows):
-        total[j] = partial_image[j] + forward(ptr[0, j], LOCAL, SHORT)
+        total[j] = partial_image[j] + forward(plan[0, j], LOCAL, SHORT)
     for i in range(many):
         j = long_rows[i]
-        total[j] += forward(ptr[0, j], SHORT, LONG)
+        total[j] += forward(plan[0, j], SHORT, LONG)
     image[...] = total[...].astype(BF16)
     spread[...] = jnp.zeros_like(spread)
     banks = spread.shape[0]
 
     def backward(j, first, last):
-        e = ptr[0, j]
+        e = plan[0, j]
         terms = lax.dot_general(
             image[j],
             joined(blocks, [e + t for t in range(first, last)], 1),
@@ -172,7 +179,7 @@
         )
         for t in range(first, last):
             k = t - first
-            spread[k % banks, col[0, e + t] - rows] += terms[:, k * B : k * B + B]
+            spread[k % banks, plan[0, first_column + e + t] - rows] += terms[:, k * B : k * B + B]
 
     for j in range(rows):
         backward(j, LOCAL, SHORT)
@@ -187,20 +194,23 @@
             ref[i] = ref[0]
 
 
-def local_backward_kernel(ptr, blocks, image, adjoint, squares):
-    rows = image.shape[0]
-    total = jnp.zeros(squares.shape, F32)
+def local_backward_kernel(plan, blocks, image, adjoint, norms):
+    rows, k = image.shape[:2]
+    total = jnp.zeros((k, B), F32)
     for j in range(rows):
         before, after = (j - 1) % rows, (j + 1) % rows
         adjoint[:, j * B : j * B + B] = lax.dot_general(
             joined(image, [j, before, after], 1),
-            joined(blocks, [ptr[0, j], ptr[0, before] + 1, ptr[0, after] + 2], 0),
+            joined(blocks, [plan[0, j], plan[0, before] + 1, plan[0, after] + 2], 0),
             BY_FIRST,
             preferred_element_type=F32,
         )
         wide = image[j].astype(F32)
         total = total + wide * wide
-    squares[...] = total
+    row = lax.broadcasted_iota(jnp.int32, (k, B), 0)
+    lane = lax.broadcasted_iota(jnp.int32, (k, B), 1)
+    squares = jnp.sum(total, axis=1, keepdims=True)
+    norms[...] = jnp.sum(jnp.where(lane == row, squares, 0.0), axis=0, keepdims=True)
 
 
 def group_masks(k):
@@ -210,11 +220,10 @@
     return lax.rem(row, group) == lax.div(lane, k), row, lane
 
 
-def gram_kernel(send, partial_adjoint, squares, *refs):
+def gram_kernel(send, partial_adjoint, norms, *refs):
     arrived, adjoint, packed = refs[:6], refs[6], refs[7]
     k = adjoint.shape[0]
     way = directions()
-    adjoint[...] = partial_adjoint[...]
     for ref, offsets in zip(arrived, received(*way)):
         for i, (a, b) in enumerate(offsets):
             for g in range(ref.shape[1]):
@@ -222,55 +231,70 @@
                 adjoint[:, place] += ref[i, g]
     z = adjoint[...]
     gram = lax.dot_general(z, z, BY_LAST, precision=lax.Precision.HIGHEST, preferred_element_type=F32)
-    own, row, lane = group_masks(k)
-    tile = (lax.rem(lane, k) == row).astype(F32)
-    tiled = lax.dot_general(gram, tile, BY_FIRST, precision=lax.Precision.HIGHEST, preferred_element_type=F32)
-    tiled = jnp.where(own, tiled, 0.0)
+    wide = jnp.concatenate([gram, jnp.zeros((k, B - k), F32)], axis=1)
+    moved = pltpu.roll(wide, 0, 1, stride=k, stride_axis=0)
     group = B // k
-    lines = [jnp.sum(tiled[i : i + group], axis=0, keepdims=True) for i in range(0, k, group)]
-    norms = jnp.sum(squares[...], axis=1, keepdims=True)
-    lines.append(jnp.sum(jnp.where(lane == row, norms, 0.0), axis=0, keepdims=True))
+    lines = [jnp.sum(moved[i : i + group], axis=0, keepdims=True) for i in range(0, k, group)]
+    lines.append(norms[...])
     lines.append(jnp.zeros(((-len(lines)) % 4, B), F32))
     packed[...] = jnp.broadcast_to(jnp.concatenate(lines, axis=0)[None], packed.shape)
 
 
-def solve_kernel(count, packed, adjoint, basis, factor, gain):
-    k = adjoint.shape[0]
+def solve_kernel(count, packed, adjoint, basis_hbm, factor_hbm, gain_hbm, basis, factor, gain, sems):
+    k, unknowns = adjoint.shape
     group = B // k
     own, row, lane = group_masks(k)
     sums = jnp.sum(packed[...], axis=0) / count
+    gain[...] = sums[k // group : k // group + 1, :k]
+    small = [pltpu.make_async_copy(gain, gain_hbm, sems.at[0])]
+    small[0].start()
     spread = jnp.concatenate(
         [jnp.broadcast_to(sums[i : i + 1], (group, B)) for i in range(k // group)], axis=0
     )
-    line = lax.broadcasted_iota(jnp.int32, (B, B), 0)
-    column = lax.broadcasted_iota(jnp.int32, (B, B), 1)
-    fold = (lax.rem(line, k) == column).astype(F32)
-    both = lax.dot_general(
-        jnp.where(own, spread, 0.0), fold, BY_FIRST, precision=lax.Precision.HIGHEST, preferred_element_type=F32
-    )
-    both = both + (lane == row + k).astype(F32)
+    gram = jnp.where(own, spread, 0.0)
+    shift = k
+    while shift < B:
+        gram = gram + pltpu.roll(gram, shift, 1)
+        shift *= 2
+    lines = [jnp.broadcast_to(gram[:, i : i + 1], (k, B)) for i in range(k)]
+    both = jnp.where(lane < k, gram, (lane == row + k).astype(F32))
     for i in range(k):
-        pivots = jnp.broadcast_to(both[:, i : i + 1], (k, B))
-        scale = lax.rsqrt(pivots[i : i + 1])
+        scale = lax.rsqrt(lines[i][i : i + 1])
+        left = lines[i] * scale
         top = both[i : i + 1] * scale
-        lower = both - pivots * scale * top
-        both = jnp.where(row > i, lower, jnp.where(row == i, top, both))
+        for j in range(i + 1, k):
+            lines[j] = lines[j] - left * left[j : j + 1]
+        both = jnp.where(row > i, both - left * top, jnp.where(row == i, top, both))
     factor[...] = jnp.where(lane >= row, both, 0.0)[:, :k]
-    gain[...] = sums[k // group : k // group + 1, :k]
+    small.append(pltpu.make_async_copy(factor, factor_hbm, sems.at[1]))
+    small[1].start()
     inverse = both[:, k : 2 * k]
-    basis[...] = lax.dot_general(
-        inverse, adjoint[...], BY_FIRST, precision=lax.Precision.HIGHEST, preferred_element_type=F32
-    )
-
-
-def call(kernel, name, shapes, in_specs, scratch=(), flops=0, bytes_accessed=0):
+    parts = sems.shape[0] - 2
+    copies = []
+    for i in range(parts):
+        place = pl.ds(i * (unknowns // parts), unknowns // parts)
+        basis[:, place] = lax.dot_general(
+            inverse,
+            adjoint[:, place],
+            BY_FIRST,
+            precision=lax.Precision.HIGHEST,
+            preferred_element_type=F32,
+        )
+        copies.append(pltpu.make_async_copy(basis.at[:, place], basis_hbm.at[:, place], sems.at[2 + i]))
+        copies[-1].start()
+    for copy in small + copies:
+        copy.wait()
+
+
+def call(kernel, name, shapes, in_specs, scratch=(), out=VMEM, alias={}, flops=0, bytes_accessed=0):
     return pl.pallas_call(
         kernel,
         name=name,
-        out_shape=[jax.ShapeDtypeStruct(*s) if isinstance(s, tuple) else s for s in shapes],
+        out_shape=[jax.ShapeDtypeStruct(shape, dtype) for shape, dtype in shapes],
         in_specs=in_specs,
-        out_specs=[VMEM] * len(shapes),
+        out_specs=[out] * len(shapes),
         scratch_shapes=scratch,
+        input_output_aliases=alias,
         compiler_params=pltpu.CompilerParams(vmem_limit_bytes=LIMIT),
         cost_estimate=pl.CostEstimate(flops=flops, bytes_accessed=bytes_accessed, transcendentals=0),
     )
@@ -286,30 +310,34 @@
     many = (stored - SHORT * rows) // (LONG - SHORT)
     sizes = (3, 2, 2, 2, 1, 1)
     send_lines = jnp.transpose(send_list, (0, 2, 1))
-    here, ptr, col, send, *outgoing = call(
+    inputs = (send_lines, vectors, row_ptr, col_index, blocks)
+    here, plan, send, *outgoing = call(
         gather_kernel,
         "gather",
-        [(vectors.shape, BF16)]
-        + [(a.shape, jnp.int32) for a in (row_ptr, col_index, send_lines)]
+        [(vectors.shape, BF16), ((1, rounded(rows + 1) + rounded(stored)), jnp.int32), (send_lines.shape, jnp.int32)]
         + [((n, ghost, k, B), BF16) for n in sizes],
         [HBM] * 5,
-        scratch=[pltpu.SMEM(send_lines.shape, jnp.int32), pltpu.SemaphoreType.DMA((5,))],
-        bytes_accessed=0,
-    )(*[pltpu.with_memory_space_constraint(a, pltpu.HBM) for a in (send_lines, vectors, row_ptr, col_index, blocks)])
+        scratch=[
+            pltpu.SMEM(send_lines.shape, jnp.int32),
+            pltpu.VMEM(row_ptr.shape, jnp.int32),
+            pltpu.VMEM(col_index.shape, jnp.int32),
+            pltpu.SemaphoreType.DMA((5,)),
+        ],
+    )(*[pltpu.with_memory_space_constraint(a, pltpu.HBM) for a in inputs])
     arrived = exchange(*outgoing)
     (partial_image,) = call(
         local_forward_kernel,
         "local_forward",
         [((rows, k, B), F32)],
-        [SMEM, VMEM, VMEM] + [ANY] * len(arrived[:0]),
+        [SMEM, VMEM, VMEM],
         flops=2 * rows * LOCAL * B * B * k,
         bytes_accessed=2 * rows * LOCAL * B * B,
-    )(ptr, here, blocks, *arrived[:0])
+    )(plan, here, blocks)
     image, *returns = call(
         ghost_kernel,
         "ghost",
         [((rows, k, B), BF16)] + [((n, ghost, k, B), F32) for n in sizes],
-        [SMEM, SMEM] + [VMEM] * 8,
+        [SMEM] + [VMEM] * 8,
         scratch=[
             pltpu.VMEM((slots, k, B), BF16),
             pltpu.VMEM((rows, k, B), F32),
@@ -318,28 +346,37 @@
         ],
         flops=4 * (stored - rows * LOCAL) * B * B * k,
         bytes_accessed=4 * (stored - rows * LOCAL) * B * B,
-    )(ptr, col, blocks, partial_image, *arrived)
+    )(plan, blocks, partial_image, *arrived)
     returned = exchange(*returns)
-    partial_adjoint, squares = call(
+    partial_adjoint, norms = call(
         local_backward_kernel,
         "local_backward",
-        [((k, unknowns), F32), ((k, B), F32)],
+        [((k, unknowns), F32), ((1, B), F32)],
         [SMEM, VMEM, VMEM],
         flops=2 * rows * LOCAL * B * B * k,
         bytes_accessed=2 * rows * LOCAL * B * B,
-    )(ptr, blocks, image)
+    )(plan, blocks, image)
     adjoint, packed = call(
         gram_kernel,
         "gram",
         [((k, unknowns), F32), ((devices, 4, B), F32)],
         [SMEM] + [VMEM] * 8,
-    )(send, partial_adjoint, squares, *returned)
+        alias={1: 0},
+    )(send, partial_adjoint, norms, *returned)
     everywhere = lax.all_to_all(packed, AXES, 0, 0)
+    parts = 4
     basis, factor, gain = call(
         functools.partial(solve_kernel, unknowns * devices),
         "solve",
         [((k, unknowns), F32), ((k, k), F32), ((1, k), F32)],
         [VMEM, VMEM],
+        scratch=[
+            pltpu.VMEM((k, unknowns), F32),
+            pltpu.VMEM((k, k), F32),
+            pltpu.VMEM((1, k), F32),
+            pltpu.SemaphoreType.DMA((parts + 2,)),
+        ],
+        out=HBM,
     )(everywhere, adjoint)
     return basis, factor, gain[0]
 

time: 45.7 us -> 44.5 us (0.974)
  Pallas kernels: 10.7 us -> 9.54 us
    pallas_call x1, Pallas kernels: 2.81 us -> 1.66 us  [local(): call(functools.partial(solve_kernel, unknowns * devices), 'solve', [((k,...]
  transfers between devices with their start and end apart: 12 -> 12, of which waited for: 3 -> 3; matrix products, arithmetic and copies ran while one was open for 0% -> 0% of each run, Pallas kernels for 6% -> 7%
where the time goes in v5:
time: 44.5 us; the launch traced here: 44.3 us
  starting transfers between devices  19.5 us (44%)
  blocking collectives  11.1 us (25%)
  Pallas kernels  9.54 us (21%)
  waiting for transfers between devices  3.44 us (8%)
  between operations  0.72 us (2%)
    ppermute x12, starting transfers between devices, swap(): lax.ppermute(array, AXES, [(d, target(d) % devices) for d in range(device...  19.5 us
    all_to_all x1, blocking collectives, local(): everywhere = lax.all_to_all(packed, AXES, 0, 0)  11.1 us
    ppermute x12, waiting for transfers between devices, swap(): lax.ppermute(array, AXES, [(d, target(d) % devices) for d in range(device...  3.44 us
    pallas_call x1, Pallas kernels, local(): call(ghost_kernel, 'ghost', [((rows, k, B), BF16)] + [((n, ghost, k, B),...  2.56 us
    pallas_call x1, Pallas kernels, local(): call(local_forward_kernel, 'local_forward', [((rows, k, B), F32)], [SMEM,...  1.75 us
    pallas_call x1, Pallas kernels, local(): call(functools.partial(solve_kernel, unknowns * devices), 'solve', [((k,...  1.66 us
    pallas_call x1, Pallas kernels, local(): call(local_backward_kernel, 'local_backward', [((k, unknowns), F32), ((1,...  1.21 us
    pallas_call x1, Pallas kernels, local(): call(gram_kernel, 'gram', [((k, unknowns), F32), ((devices, 4, B), F32)],...  1.21 us
  transfers between devices with their start and end apart: 12, of which 3 were waited for; matrix products, arithmetic and copies ran while one was open for 0% of the time, Pallas kernels for 7%

profile of v5, /device:TPU:0, one launch (start us, length us, event | category | flops | bytes accessed | tf_op | source)
XLA Modules:
  0.0 44.3 jit_solution(16634946609388109917)
XLA Ops:
  0.6 1.1 %gather.1 = (bf16[16,4096]{1,0:T(8,128)(2,1)S(1)}, s32[1,384]{1,0:T(1,128)S(1)}, s32[1,2,8]{2,1,0:T(2,128)S(1)}, bf16[3,2,16,128]{3,2,1,0:T(8,128)(2,1)S(1)}, bf...) custom-call(s32[1,2,8]{2,1,0:T(2,128)} %bitcast.2, ...), custom_call_target="tpu_custom_call" | custom-call | tf_op jit(solution)/shard_map/gather/pallas_call | solution.py:314
  1.8 0.5 %collective-permute-start = (bf16[3,2,16,128]{3,2,1,0:T(8,128)(2,1)S(1)}, bf16[3,2,16,128]{3,2,1,0:T(8,128)(2,1)S(1)}, u32[]{:S(2)}, u32[]{:S(2)}) collective-permute-start(bf16[3,2,16,128]{3,2,1,0:T(8,128)(2,1)S(1)} %get-tuple-element.29), channel_id=1, source_target_pairs={{0,1},{1,0},{2,3},{3,2},{4,5},{5,4},{6,7},{7,6},{8,9},{9,8},{10,11... | collective-permute-start | bytes 73736 | tf_op jit(solution)/shard_map/ppermute | solution.py:72
  2.3 5.6 %collective-permute-start.1 = (bf16[2,2,16,128]{3,2,1,0:T(8,128)(2,1)S(1)}, bf16[2,2,16,128]{3,2,1,0:T(8,128)(2,1)S(1)}, u32[]{:S(2)}, u32[]{:S(2)}) collective-permute-start(bf16[2,2,16,128]{3,2,1,0:T(8,128)(2,1)S(1)} %get-tuple-element.30), channel_id=1, source_target_pairs={{0,23},{1,26},{2,25},{3,28},{4,27},{5,30},{6,29},{7,16},{8,15},{9,... | collective-permute-start | bytes 49160 | tf_op jit(solution)/shard_map/ppermute | solution.py:72
  7.9 1.2 %collective-permute-start.2 = (bf16[2,2,16,128]{3,2,1,0:T(8,128)(2,1)S(1)}, bf16[2,2,16,128]{3,2,1,0:T(8,128)(2,1)S(1)}, u32[]{:S(2)}, u32[]{:S(2)}) collective-permute-start(bf16[2,2,16,128]{3,2,1,0:T(8,128)(2,1)S(1)} %get-tuple-element.31), channel_id=1, source_target_pairs={{0,31},{1,2},{2,1},{3,4},{4,3},{5,6},{6,5},{7,8},{8,7},{9,10},{10,... | collective-permute-start | bytes 49160 | tf_op jit(solution)/shard_map/ppermute | solution.py:72
  9.1 0.5 %collective-permute-start.3 = (bf16[2,2,16,128]{3,2,1,0:T(8,128)(2,1)S(1)}, bf16[2,2,16,128]{3,2,1,0:T(8,128)(2,1)S(1)}, u32[]{:S(2)}, u32[]{:S(2)}) collective-permute-start(bf16[2,2,16,128]{3,2,1,0:T(8,128)(2,1)S(1)} %get-tuple-element.32), channel_id=1, source_target_pairs={{0,7},{1,10},{2,9},{3,12},{4,11},{5,14},{6,13},{7,0},{8,31},{9,2},... | collective-permute-start | bytes 49160 | tf_op jit(solution)/shard_map/ppermute | solution.py:72
  9.5 3.2 %collective-permute-start.4 = (bf16[2,2,16,128]{3,2,1,0:T(8,128)(2,1)S(1)}, bf16[2,2,16,128]{3,2,1,0:T(8,128)(2,1)S(1)}, u32[]{:S(2)}, u32[]{:S(2)}) collective-permute-start(bf16[2,2,16,128]{3,2,1,0:T(8,128)(2,1)S(1)} %pad_maximum_fusion.2), channel_id=1, source_target_pairs={{0,24},{1,25},{2,26},{3,27},{4,28},{5,29},{6,30},{7,31},{8,16},{9,... | collective-permute-start | bytes 49160 | tf_op jit(solution)/shard_map/ppermute | solution.py:72
  12.8 1.2 %collective-permute-start.5 = (bf16[2,2,16,128]{3,2,1,0:T(8,128)(2,1)S(1)}, bf16[2,2,16,128]{3,2,1,0:T(8,128)(2,1)S(1)}, u32[]{:S(2)}, u32[]{:S(2)}) collective-permute-start(bf16[2,2,16,128]{3,2,1,0:T(8,128)(2,1)S(1)} %pad_maximum_fusion.3), channel_id=1, source_target_pairs={{0,8},{1,9},{2,10},{3,11},{4,12},{5,13},{6,14},{7,15},{8,0},{9,1},... | collective-permute-start | bytes 49160 | tf_op jit(solution)/shard_map/ppermute | solution.py:72
  14.0 1.7 %local_forward.1.partial_image = f32[32,16,128]{2,1,0:T(8,128)S(1)} custom-call(s32[1,384]{1,0:T(1,128)S(1)} %get-tuple-element.27.plan, bf16[16,4096]{1,0:T(8,128)(2,1)S(1)} %get-tuple-element.28.vectors, bf16[224,128,128]{2,1,0:T(8,128)(2,1)S(1)} %copy-done), custom_call_target="tpu_custom_call" | custom-call | flops 50331648 | bytes 3145728 | tf_op jit(solution)/shard_map/local_forward/pallas_call | solution.py:328
  15.7 0.0 collective-permute-done.3.refs_3_
  15.8 0.7 %collective-permute-done.5.refs_5_ = bf16[2,2,16,128]{3,2,1,0:T(8,128)(2,1)S(1)} collective-permute-done((bf16[2,2,16,128]{3,2,1,0:T(8,128)(2,1)S(1)}, bf16[2,2,16,128]{3,2,1,0:T(8,128)(2,1)S(1)}, u32[]{:S(2)}, u32[]{:S(2)}) %collective-permute-start.5) | collective-permute-done | bytes 16416 | tf_op jit(solution)/shard_map/ppermute | solution.py:72
  16.5 2.6 %ghost.1 = (bf16[32,16,128]{2,1,0:T(8,128)(2,1)S(1)}, f32[3,2,16,128]{3,2,1,0:T(8,128)S(1)}, f32[2,2,16,128]{3,2,1,0:T(8,128)S(1)}, f32[2,2,16,128]{3,2,1,0:T(8,...) custom-call(s32[1,384]{1,0:T(1,128)S(1)} %get-tuple-element.27.plan, ...), custom_call_target="tpu_custom_call" | custom-call | flops 134217728 | bytes 8388608 | tf_op jit(solution)/shard_map/ghost/pallas_call | solution.py:336
  19.1 0.1 collective-permute-start.6
  19.1 1.0 %collective-permute-start.7 = (f32[2,2,16,128]{3,2,1,0:T(8,128)S(1)}, f32[2,2,16,128]{3,2,1,0:T(8,128)S(1)}, u32[]{:S(2)}, u32[]{:S(2)}) collective-permute-start(f32[2,2,16,128]{3,2,1,0:T(8,128)S(1)} %get-tuple-element.39), channel_id=1, source_target_pairs={{0,23},{1,26},{2,25},{3,28},{4,27},{5,30},{6,29},{7,16},{8,15},{9,... | collective-permute-start | bytes 98312 | tf_op jit(solution)/shard_map/ppermute | solution.py:72
  20.1 3.3 %collective-permute-start.8 = (f32[2,2,16,128]{3,2,1,0:T(8,128)S(1)}, f32[2,2,16,128]{3,2,1,0:T(8,128)S(1)}, u32[]{:S(2)}, u32[]{:S(2)}) collective-permute-start(f32[2,2,16,128]{3,2,1,0:T(8,128)S(1)} %get-tuple-element.40), channel_id=1, source_target_pairs={{0,31},{1,2},{2,1},{3,4},{4,3},{5,6},{6,5},{7,8},{8,7},{9,10},{10,... | collective-permute-start | bytes 98312 | tf_op jit(solution)/shard_map/ppermute | solution.py:72
  23.4 0.5 %collective-permute-start.9 = (f32[2,2,16,128]{3,2,1,0:T(8,128)S(1)}, f32[2,2,16,128]{3,2,1,0:T(8,128)S(1)}, u32[]{:S(2)}, u32[]{:S(2)}) collective-permute-start(f32[2,2,16,128]{3,2,1,0:T(8,128)S(1)} %get-tuple-element.41), channel_id=1, source_target_pairs={{0,7},{1,10},{2,9},{3,12},{4,11},{5,14},{6,13},{7,0},{8,31},{9,2},... | collective-permute-start | bytes 98312 | tf_op jit(solution)/shard_map/ppermute | solution.py:72
  23.9 2.5 %collective-permute-start.10 = (f32[2,2,16,128]{3,2,1,0:T(8,128)S(1)}, f32[2,2,16,128]{3,2,1,0:T(8,128)S(1)}, u32[]{:S(2)}, u32[]{:S(2)}) collective-permute-start(f32[2,2,16,128]{3,2,1,0:T(8,128)S(1)} %pad_maximum_fusion), channel_id=1, source_target_pairs={{0,24},{1,25},{2,26},{3,27},{4,28},{5,29},{6,30},{7,31},{8,16},{9,... | collective-permute-start | bytes 98312 | tf_op jit(solution)/shard_map/ppermute | solution.py:72
  26.4 1.2 %local_backward.1 = (f32[16,4096]{1,0:T(8,128)S(1)}, f32[1,128]{1,0:T(1,128)S(1)}) custom-call(s32[1,384]{1,0:T(1,128)S(1)} %get-tuple-element.27.plan, bf16[224,128,128]{2,1,0:T(8,128)(2,1)S(1)} %copy-done, bf16[32,16,128]{2,1,0:T(8,128)(2,1)S(1)} %get-tuple-element.35.image), custom_call_target="tpu_custom_call" | custom-call | flops 50331648 | bytes 3145728 | tf_op jit(solution)/shard_map/local_backward/pallas_call | solution.py:351
  27.6 0.0 collective-permute-done.8.refs_2_
  27.6 0.0 collective-permute-done.9.refs_3_
  27.7 2.1 %collective-permute-done.10.refs_4_ = f32[2,2,16,128]{3,2,1,0:T(8,128)S(1)} collective-permute-done((f32[2,2,16,128]{3,2,1,0:T(8,128)S(1)}, f32[2,2,16,128]{3,2,1,0:T(8,128)S(1)}, u32[]{:S(2)}, u32[]{:S(2)}) %collective-permute-start.10) | collective-permute-done | bytes 32800 | tf_op jit(solution)/shard_map/ppermute | solution.py:72
  29.8 0.5 %collective-permute-done.11.refs_5_ = f32[2,2,16,128]{3,2,1,0:T(8,128)S(1)} collective-permute-done((f32[2,2,16,128]{3,2,1,0:T(8,128)S(1)}, f32[2,2,16,128]{3,2,1,0:T(8,128)S(1)}, u32[]{:S(2)}, u32[]{:S(2)}) %collective-permute-start.11) | collective-permute-done | bytes 32800 | tf_op jit(solution)/shard_map/ppermute | solution.py:72
  30.3 1.2 %gram.1 = (f32[16,4096]{1,0:T(8,128)S(1)}, f32[32,4,128]{2,1,0:T(4,128)S(1)}) custom-call(s32[1,2,8]{2,1,0:T(2,128)S(1)} %get-tuple-element.26.send, f32[16,4096]{1,0:T(8,128)S(1)} %get-tuple-element.36.partial_adjoint, f32[1,128]{1,0:T(1,128)S(1)} %get-tuple-element.37.norms, ...), custom_call_target="tpu_custom_call", output_to_operand_aliasing={{0}: (1, {})} | custom-call | tf_op jit(solution)/shard_map/gram/pallas_call | solution.py:359
  31.5 11.1 %all_to_all.5.packed = f32[32,4,128]{2,1,0:T(4,128)S(1)} all-to-all(f32[32,4,128]{2,1,0:T(4,128)S(1)} %get-tuple-element.44), channel_id=1, replica_groups=mesh['dom'=4,'sub'=8] {'dom','sub'}, dimensions={0} | all-to-all | bytes 131072 | tf_op jit(solution)/shard_map/all_to_all | solution.py:366
  42.7 1.7 %solve.1 = (f32[16,4096]{1,0:T(8,128)}, f32[16,16]{1,0:T(8,128)}, f32[1,16]{1,0:T(1,128)}) custom-call(f32[32,4,128]{2,1,0:T(4,128)S(1)} %all_to_all.5.packed, f32[16,4096]{1,0:T(8,128)S(1)} %get-tuple-element.45.adjoint), custom_call_target="tpu_custom_call" | custom-call | tf_op jit(solution)/shard_map/solve/pallas_call | solution.py:368
  (15 shorter events, 0.0 us)
Async XLA Ops:
  0.6 13.3 %copy-start = (bf16[224,128,128]{2,1,0:T(8,128)(2,1)S(1)}, bf16[224,128,128]{2,1,0:T(8,128)(2,1)}, u32[]{:S(2)}) copy-start(bf16[224,128,128]{2,1,0:T(8,128)(2,1)} %blocks.5) | copy-start | bytes 22020100
  1.8 7.7 %collective-permute-start = (bf16[3,2,16,128]{3,2,1,0:T(8,128)(2,1)S(1)}, bf16[3,2,16,128]{3,2,1,0:T(8,128)(2,1)S(1)}, u32[]{:S(2)}, u32[]{:S(2)}) collective-permute-start(bf16[3,2,16,128]{3,2,1,0:T(8,128)(2,1)S(1)} %get-tuple-element.29), channel_id=1, source_target_pairs={{0,1},{1,0},{2,3},{3,2},{4,5},{5,4},{6,7},{7,6},{8,9},{9,8},{10,11... | collective-permute-start | bytes 73736 | tf_op jit(solution)/shard_map/ppermute | solution.py:72
  2.3 13.4 %collective-permute-start.1 = (bf16[2,2,16,128]{3,2,1,0:T(8,128)(2,1)S(1)}, bf16[2,2,16,128]{3,2,1,0:T(8,128)(2,1)S(1)}, u32[]{:S(2)}, u32[]{:S(2)}) collective-permute-start(bf16[2,2,16,128]{3,2,1,0:T(8,128)(2,1)S(1)} %get-tuple-element.30), channel_id=1, source_target_pairs={{0,23},{1,26},{2,25},{3,28},{4,27},{5,30},{6,29},{7,16},{8,15},{9,... | collective-permute-start | bytes 49160 | tf_op jit(solution)/shard_map/ppermute | solution.py:72
  7.9 7.8 %collective-permute-start.2 = (bf16[2,2,16,128]{3,2,1,0:T(8,128)(2,1)S(1)}, bf16[2,2,16,128]{3,2,1,0:T(8,128)(2,1)S(1)}, u32[]{:S(2)}, u32[]{:S(2)}) collective-permute-start(bf16[2,2,16,128]{3,2,1,0:T(8,128)(2,1)S(1)} %get-tuple-element.31), channel_id=1, source_target_pairs={{0,31},{1,2},{2,1},{3,4},{4,3},{5,6},{6,5},{7,8},{8,7},{9,10},{10,... | collective-permute-start | bytes 49160 | tf_op jit(solution)/shard_map/ppermute | solution.py:72
  9.1 6.7 %collective-permute-start.3 = (bf16[2,2,16,128]{3,2,1,0:T(8,128)(2,1)S(1)}, bf16[2,2,16,128]{3,2,1,0:T(8,128)(2,1)S(1)}, u32[]{:S(2)}, u32[]{:S(2)}) collective-permute-start(bf16[2,2,16,128]{3,2,1,0:T(8,128)(2,1)S(1)} %get-tuple-element.32), channel_id=1, source_target_pairs={{0,7},{1,10},{2,9},{3,12},{4,11},{5,14},{6,13},{7,0},{8,31},{9,2},... | collective-permute-start | bytes 49160 | tf_op jit(solution)/shard_map/ppermute | solution.py:72
  9.5 6.2 %collective-permute-start.4 = (bf16[2,2,16,128]{3,2,1,0:T(8,128)(2,1)S(1)}, bf16[2,2,16,128]{3,2,1,0:T(8,128)(2,1)S(1)}, u32[]{:S(2)}, u32[]{:S(2)}) collective-permute-start(bf16[2,2,16,128]{3,2,1,0:T(8,128)(2,1)S(1)} %pad_maximum_fusion.2), channel_id=1, source_target_pairs={{0,24},{1,25},{2,26},{3,27},{4,28},{5,29},{6,30},{7,31},{8,16},{9,... | collective-permute-start | bytes 49160 | tf_op jit(solution)/shard_map/ppermute | solution.py:72
  12.8 3.7 %collective-permute-start.5 = (bf16[2,2,16,128]{3,2,1,0:T(8,128)(2,1)S(1)}, bf16[2,2,16,128]{3,2,1,0:T(8,128)(2,1)S(1)}, u32[]{:S(2)}, u32[]{:S(2)}) collective-permute-start(bf16[2,2,16,128]{3,2,1,0:T(8,128)(2,1)S(1)} %pad_maximum_fusion.3), channel_id=1, source_target_pairs={{0,8},{1,9},{2,10},{3,11},{4,12},{5,13},{6,14},{7,15},{8,0},{9,1},... | collective-permute-start | bytes 49160 | tf_op jit(solution)/shard_map/ppermute | solution.py:72
  19.1 4.8 %collective-permute-start.6 = (f32[3,2,16,128]{3,2,1,0:T(8,128)S(1)}, f32[3,2,16,128]{3,2,1,0:T(8,128)S(1)}, u32[]{:S(2)}, u32[]{:S(2)}) collective-permute-start(f32[3,2,16,128]{3,2,1,0:T(8,128)S(1)} %get-tuple-element.38), channel_id=1, source_target_pairs={{0,1},{1,0},{2,3},{3,2},{4,5},{5,4},{6,7},{7,6},{8,9},{9,8},{10,11... | collective-permute-start | bytes 147464 | tf_op jit(solution)/shard_map/ppermute | solution.py:72
  19.1 8.5 %collective-permute-start.7 = (f32[2,2,16,128]{3,2,1,0:T(8,128)S(1)}, f32[2,2,16,128]{3,2,1,0:T(8,128)S(1)}, u32[]{:S(2)}, u32[]{:S(2)}) collective-permute-start(f32[2,2,16,128]{3,2,1,0:T(8,128)S(1)} %get-tuple-element.39), channel_id=1, source_target_pairs={{0,23},{1,26},{2,25},{3,28},{4,27},{5,30},{6,29},{7,16},{8,15},{9,... | collective-permute-start | bytes 98312 | tf_op jit(solution)/shard_map/ppermute | solution.py:72
  20.1 7.5 %collective-permute-start.8 = (f32[2,2,16,128]{3,2,1,0:T(8,128)S(1)}, f32[2,2,16,128]{3,2,1,0:T(8,128)S(1)}, u32[]{:S(2)}, u32[]{:S(2)}) collective-permute-start(f32[2,2,16,128]{3,2,1,0:T(8,128)S(1)} %get-tuple-element.40), channel_id=1, source_target_pairs={{0,31},{1,2},{2,1},{3,4},{4,3},{5,6},{6,5},{7,8},{8,7},{9,10},{10,... | collective-permute-start | bytes 98312 | tf_op jit(solution)/shard_map/ppermute | solution.py:72
  23.4 4.2 %collective-permute-start.9 = (f32[2,2,16,128]{3,2,1,0:T(8,128)S(1)}, f32[2,2,16,128]{3,2,1,0:T(8,128)S(1)}, u32[]{:S(2)}, u32[]{:S(2)}) collective-permute-start(f32[2,2,16,128]{3,2,1,0:T(8,128)S(1)} %get-tuple-element.41), channel_id=1, source_target_pairs={{0,7},{1,10},{2,9},{3,12},{4,11},{5,14},{6,13},{7,0},{8,31},{9,2},... | collective-permute-start | bytes 98312 | tf_op jit(solution)/shard_map/ppermute | solution.py:72
  23.9 5.9 %collective-permute-start.10 = (f32[2,2,16,128]{3,2,1,0:T(8,128)S(1)}, f32[2,2,16,128]{3,2,1,0:T(8,128)S(1)}, u32[]{:S(2)}, u32[]{:S(2)}) collective-permute-start(f32[2,2,16,128]{3,2,1,0:T(8,128)S(1)} %pad_maximum_fusion), channel_id=1, source_target_pairs={{0,24},{1,25},{2,26},{3,27},{4,28},{5,29},{6,30},{7,31},{8,16},{9,... | collective-permute-start | bytes 98312 | tf_op jit(solution)/shard_map/ppermute | solution.py:72
  26.4 3.9 %collective-permute-start.11 = (f32[2,2,16,128]{3,2,1,0:T(8,128)S(1)}, f32[2,2,16,128]{3,2,1,0:T(8,128)S(1)}, u32[]{:S(2)}, u32[]{:S(2)}) collective-permute-start(f32[2,2,16,128]{3,2,1,0:T(8,128)S(1)} %pad_maximum_fusion.1), channel_id=1, source_target_pairs={{0,8},{1,9},{2,10},{3,11},{4,12},{5,13},{6,14},{7,15},{8,0},{9,1},... | collective-permute-start | bytes 98312 | tf_op jit(solution)/shard_map/ppermute | solution.py:72

commit v6 on v5

--- a/solution.py
+++ b/solution.py
@@ -45,8 +45,8 @@
 def sent(s, t, u):
     return (
         ((0, -s), (u, -s), (-u, -s)),
+        ((0, s),),
         ((-t, s),),
-        ((0, s),),
         ((t, s),),
         ((-u, 0),),
         ((u, 0),),
@@ -56,15 +56,15 @@
 def received(s, t, u):
     return (
         ((0, s),),
+        ((0, -s),),
         ((t, -s),),
-        ((0, -s),),
         ((-t, -s),),
         ((u, 0), (u, s)),
         ((-u, 0), (-u, s)),
     )
 
 
-def exchange(pair, cross_far, side, cross_near, far, near):
+def exchange(pair, side, cross_far, cross_near, far, near):
     n_inner = lax.axis_size("sub")
     devices = lax.axis_size("dom") * n_inner
 
@@ -82,12 +82,12 @@
         return d + step(d) + sign * towards(past)
 
     pair = swap(pair, lambda d: d - step(d))
+    side = swap(side, lambda d: d + step(d))
     cross_far = swap(cross_far, lambda d: diagonal(d, -1))
-    side = swap(side, lambda d: d + step(d))
     cross_near = swap(cross_near, lambda d: diagonal(d, 1))
     far = swap(jnp.concatenate([far, pair[2:3]], axis=0), lambda d: d - towards(d))
     near = swap(jnp.concatenate([near, pair[1:2]], axis=0), lambda d: d + towards(d))
-    return pair, cross_far, side, cross_near, far, near
+    return pair, side, cross_far, cross_near, far, near
 
 
 def rounded(size):

time: 44.5 us -> 42.5 us (0.955)
  waiting for transfers between devices: 3.44 us -> 2.06 us
  blocking collectives: 11.1 us -> 9.94 us
  starting transfers between devices: 19.5 us -> 20 us
    ppermute x12, waiting for transfers between devices: 3.44 us -> 2.06 us  [swap(): lax.ppermute(array, AXES, [(d, target(d) % devices) for d in range(device...]
    all_to_all x1, blocking collectives: 11.1 us -> 9.94 us  [local(): everywhere = lax.all_to_all(packed, AXES, 0, 0)]
    ppermute x12, starting transfers between devices: 19.5 us -> 20 us  [swap(): lax.ppermute(array, AXES, [(d, target(d) % devices) for d in range(device...]
  transfers between devices with their start and end apart: 12 -> 12, of which waited for: 3 -> 2; matrix products, arithmetic and copies ran while one was open for 0% -> 0% of each run, Pallas kernels for 7% -> 7%
where the time goes in v6:
time: 42.5 us; the launch traced here: 42.3 us
  starting transfers between devices  20 us (47%)
  blocking collectives  9.94 us (23%)
  Pallas kernels  9.52 us (22%)
  waiting for transfers between devices  2.06 us (5%)
  between operations  0.74 us (2%)
    ppermute x12, starting transfers between devices, swap(): lax.ppermute(array, AXES, [(d, target(d) % devices) for d in range(device...  20 us
    all_to_all x1, blocking collectives, local(): everywhere = lax.all_to_all(packed, AXES, 0, 0)  9.94 us
    pallas_call x1, Pallas kernels, local(): call(ghost_kernel, 'ghost', [((rows, k, B), BF16)] + [((n, ghost, k, B),...  2.57 us
    ppermute x12, waiting for transfers between devices, swap(): lax.ppermute(array, AXES, [(d, target(d) % devices) for d in range(device...  2.06 us
    pallas_call x1, Pallas kernels, local(): call(local_forward_kernel, 'local_forward', [((rows, k, B), F32)], [SMEM,...  1.75 us
    pallas_call x1, Pallas kernels, local(): call(functools.partial(solve_kernel, unknowns * devices), 'solve', [((k,...  1.67 us
    pallas_call x1, Pallas kernels, local(): call(local_backward_kernel, 'local_backward', [((k, unknowns), F32), ((1,...  1.21 us
    pallas_call x1, Pallas kernels, local(): call(gram_kernel, 'gram', [((k, unknowns), F32), ((devices, 4, B), F32)],...  1.17 us
  transfers between devices with their start and end apart: 12, of which 2 were waited for; matrix products, arithmetic and copies ran while one was open for 0% of the time, Pallas kernels for 7%

profile of v6, /device:TPU:0, one launch (start us, length us, event | category | flops | bytes accessed | tf_op | source)
XLA Modules:
  0.0 42.3 jit_solution(15996692654499491460)
XLA Ops:
  0.6 1.1 %gather.1 = (bf16[16,4096]{1,0:T(8,128)(2,1)S(1)}, s32[1,384]{1,0:T(1,128)S(1)}, s32[1,2,8]{2,1,0:T(2,128)S(1)}, bf16[3,2,16,128]{3,2,1,0:T(8,128)(2,1)S(1)}, bf...) custom-call(s32[1,2,8]{2,1,0:T(2,128)} %bitcast.2, ...), custom_call_target="tpu_custom_call" | custom-call | tf_op jit(solution)/shard_map/gather/pallas_call | solution.py:314
  1.8 0.5 %collective-permute-start = (bf16[3,2,16,128]{3,2,1,0:T(8,128)(2,1)S(1)}, bf16[3,2,16,128]{3,2,1,0:T(8,128)(2,1)S(1)}, u32[]{:S(2)}, u32[]{:S(2)}) collective-permute-start(bf16[3,2,16,128]{3,2,1,0:T(8,128)(2,1)S(1)} %get-tuple-element.29), channel_id=1, source_target_pairs={{0,1},{1,0},{2,3},{3,2},{4,5},{5,4},{6,7},{7,6},{8,9},{9,8},{10,11... | collective-permute-start | bytes 73736 | tf_op jit(solution)/shard_map/ppermute | solution.py:72
  2.3 6.6 %collective-permute-start.1 = (bf16[2,2,16,128]{3,2,1,0:T(8,128)(2,1)S(1)}, bf16[2,2,16,128]{3,2,1,0:T(8,128)(2,1)S(1)}, u32[]{:S(2)}, u32[]{:S(2)}) collective-permute-start(bf16[2,2,16,128]{3,2,1,0:T(8,128)(2,1)S(1)} %get-tuple-element.30), channel_id=1, source_target_pairs={{0,31},{1,2},{2,1},{3,4},{4,3},{5,6},{6,5},{7,8},{8,7},{9,10},{10,... | collective-permute-start | bytes 49160 | tf_op jit(solution)/shard_map/ppermute | solution.py:72
  8.9 0.2 collective-permute-start.2
  9.1 1.4 %collective-permute-start.3 = (bf16[2,2,16,128]{3,2,1,0:T(8,128)(2,1)S(1)}, bf16[2,2,16,128]{3,2,1,0:T(8,128)(2,1)S(1)}, u32[]{:S(2)}, u32[]{:S(2)}) collective-permute-start(bf16[2,2,16,128]{3,2,1,0:T(8,128)(2,1)S(1)} %get-tuple-element.32), channel_id=1, source_target_pairs={{0,7},{1,10},{2,9},{3,12},{4,11},{5,14},{6,13},{7,0},{8,31},{9,2},... | collective-permute-start | bytes 49160 | tf_op jit(solution)/shard_map/ppermute | solution.py:72
  10.4 1.4 %collective-permute-start.4 = (bf16[2,2,16,128]{3,2,1,0:T(8,128)(2,1)S(1)}, bf16[2,2,16,128]{3,2,1,0:T(8,128)(2,1)S(1)}, u32[]{:S(2)}, u32[]{:S(2)}) collective-permute-start(bf16[2,2,16,128]{3,2,1,0:T(8,128)(2,1)S(1)} %pad_maximum_fusion.2), channel_id=1, source_target_pairs={{0,24},{1,25},{2,26},{3,27},{4,28},{5,29},{6,30},{7,31},{8,16},{9,... | collective-permute-start | bytes 49160 | tf_op jit(solution)/shard_map/ppermute | solution.py:72
  11.9 2.7 %collective-permute-start.5 = (bf16[2,2,16,128]{3,2,1,0:T(8,128)(2,1)S(1)}, bf16[2,2,16,128]{3,2,1,0:T(8,128)(2,1)S(1)}, u32[]{:S(2)}, u32[]{:S(2)}) collective-permute-start(bf16[2,2,16,128]{3,2,1,0:T(8,128)(2,1)S(1)} %pad_maximum_fusion.3), channel_id=1, source_target_pairs={{0,8},{1,9},{2,10},{3,11},{4,12},{5,13},{6,14},{7,15},{8,0},{9,1},... | collective-permute-start | bytes 49160 | tf_op jit(solution)/shard_map/ppermute | solution.py:72
  14.6 1.7 %local_forward.1.partial_image = f32[32,16,128]{2,1,0:T(8,128)S(1)} custom-call(s32[1,384]{1,0:T(1,128)S(1)} %get-tuple-element.27.plan, bf16[16,4096]{1,0:T(8,128)(2,1)S(1)} %get-tuple-element.28.vectors, bf16[224,128,128]{2,1,0:T(8,128)(2,1)S(1)} %copy-done), custom_call_target="tpu_custom_call" | custom-call | flops 50331648 | bytes 3145728 | tf_op jit(solution)/shard_map/local_forward/pallas_call | solution.py:328
  16.3 0.0 collective-permute-done.1.refs_1_
  16.3 0.0 collective-permute-done.3.refs_3_
  16.4 2.6 %ghost.1 = (bf16[32,16,128]{2,1,0:T(8,128)(2,1)S(1)}, f32[3,2,16,128]{3,2,1,0:T(8,128)S(1)}, f32[2,2,16,128]{3,2,1,0:T(8,128)S(1)}, f32[2,2,16,128]{3,2,1,0:T(8,...) custom-call(s32[1,384]{1,0:T(1,128)S(1)} %get-tuple-element.27.plan, ...), custom_call_target="tpu_custom_call" | custom-call | flops 134217728 | bytes 8388608 | tf_op jit(solution)/shard_map/ghost/pallas_call | solution.py:336
  18.9 0.1 collective-permute-start.6
  19.0 1.6 %collective-permute-start.7 = (f32[2,2,16,128]{3,2,1,0:T(8,128)S(1)}, f32[2,2,16,128]{3,2,1,0:T(8,128)S(1)}, u32[]{:S(2)}, u32[]{:S(2)}) collective-permute-start(f32[2,2,16,128]{3,2,1,0:T(8,128)S(1)} %get-tuple-element.39), channel_id=1, source_target_pairs={{0,31},{1,2},{2,1},{3,4},{4,3},{5,6},{6,5},{7,8},{8,7},{9,10},{10,... | collective-permute-start | bytes 98312 | tf_op jit(solution)/shard_map/ppermute | solution.py:72
  20.6 2.3 %collective-permute-start.8 = (f32[2,2,16,128]{3,2,1,0:T(8,128)S(1)}, f32[2,2,16,128]{3,2,1,0:T(8,128)S(1)}, u32[]{:S(2)}, u32[]{:S(2)}) collective-permute-start(f32[2,2,16,128]{3,2,1,0:T(8,128)S(1)} %get-tuple-element.40), channel_id=1, source_target_pairs={{0,23},{1,26},{2,25},{3,28},{4,27},{5,30},{6,29},{7,16},{8,15},{9,... | collective-permute-start | bytes 98312 | tf_op jit(solution)/shard_map/ppermute | solution.py:72
  22.9 0.2 collective-permute-start.9
  23.1 2.5 %collective-permute-start.10 = (f32[2,2,16,128]{3,2,1,0:T(8,128)S(1)}, f32[2,2,16,128]{3,2,1,0:T(8,128)S(1)}, u32[]{:S(2)}, u32[]{:S(2)}) collective-permute-start(f32[2,2,16,128]{3,2,1,0:T(8,128)S(1)} %pad_maximum_fusion), channel_id=1, source_target_pairs={{0,24},{1,25},{2,26},{3,27},{4,28},{5,29},{6,30},{7,31},{8,16},{9,... | collective-permute-start | bytes 98312 | tf_op jit(solution)/shard_map/ppermute | solution.py:72
  25.6 0.6 %collective-permute-start.11 = (f32[2,2,16,128]{3,2,1,0:T(8,128)S(1)}, f32[2,2,16,128]{3,2,1,0:T(8,128)S(1)}, u32[]{:S(2)}, u32[]{:S(2)}) collective-permute-start(f32[2,2,16,128]{3,2,1,0:T(8,128)S(1)} %pad_maximum_fusion.1), channel_id=1, source_target_pairs={{0,8},{1,9},{2,10},{3,11},{4,12},{5,13},{6,14},{7,15},{8,0},{9,1},... | collective-permute-start | bytes 98312 | tf_op jit(solution)/shard_map/ppermute | solution.py:72
  26.3 1.2 %local_backward.1 = (f32[16,4096]{1,0:T(8,128)S(1)}, f32[1,128]{1,0:T(1,128)S(1)}) custom-call(s32[1,384]{1,0:T(1,128)S(1)} %get-tuple-element.27.plan, bf16[224,128,128]{2,1,0:T(8,128)(2,1)S(1)} %copy-done, bf16[32,16,128]{2,1,0:T(8,128)(2,1)S(1)} %get-tuple-element.35.image), custom_call_target="tpu_custom_call" | custom-call | flops 50331648 | bytes 3145728 | tf_op jit(solution)/shard_map/local_backward/pallas_call | solution.py:351
  27.5 0.0 collective-permute-done.8.refs_2_
  27.5 1.4 %collective-permute-done.10.refs_4_ = f32[2,2,16,128]{3,2,1,0:T(8,128)S(1)} collective-permute-done((f32[2,2,16,128]{3,2,1,0:T(8,128)S(1)}, f32[2,2,16,128]{3,2,1,0:T(8,128)S(1)}, u32[]{:S(2)}, u32[]{:S(2)}) %collective-permute-start.10) | collective-permute-done | bytes 32800 | tf_op jit(solution)/shard_map/ppermute | solution.py:72
  28.9 0.6 %collective-permute-done.11.refs_5_ = f32[2,2,16,128]{3,2,1,0:T(8,128)S(1)} collective-permute-done((f32[2,2,16,128]{3,2,1,0:T(8,128)S(1)}, f32[2,2,16,128]{3,2,1,0:T(8,128)S(1)}, u32[]{:S(2)}, u32[]{:S(2)}) %collective-permute-start.11) | collective-permute-done | bytes 32800 | tf_op jit(solution)/shard_map/ppermute | solution.py:72
  29.5 1.2 %gram.1 = (f32[16,4096]{1,0:T(8,128)S(1)}, f32[32,4,128]{2,1,0:T(4,128)S(1)}) custom-call(s32[1,2,8]{2,1,0:T(2,128)S(1)} %get-tuple-element.26.send, f32[16,4096]{1,0:T(8,128)S(1)} %get-tuple-element.36.partial_adjoint, f32[1,128]{1,0:T(1,128)S(1)} %get-tuple-element.37.norms, ...), custom_call_target="tpu_custom_call", output_to_operand_aliasing={{0}: (1, {})} | custom-call | tf_op jit(solution)/shard_map/gram/pallas_call | solution.py:359
  30.7 9.9 %all_to_all.5.packed = f32[32,4,128]{2,1,0:T(4,128)S(1)} all-to-all(f32[32,4,128]{2,1,0:T(4,128)S(1)} %get-tuple-element.44), channel_id=1, replica_groups=mesh['dom'=4,'sub'=8] {'dom','sub'}, dimensions={0} | all-to-all | bytes 131072 | tf_op jit(solution)/shard_map/all_to_all | solution.py:366
  40.6 1.7 %solve.1 = (f32[16,4096]{1,0:T(8,128)}, f32[16,16]{1,0:T(8,128)}, f32[1,16]{1,0:T(1,128)}) custom-call(f32[32,4,128]{2,1,0:T(4,128)S(1)} %all_to_all.5.packed, f32[16,4096]{1,0:T(8,128)S(1)} %get-tuple-element.45.adjoint), custom_call_target="tpu_custom_call" | custom-call | tf_op jit(solution)/shard_map/solve/pallas_call | solution.py:368
  (15 shorter events, 0.0 us)
Async XLA Ops:
  0.6 13.9 %copy-start = (bf16[224,128,128]{2,1,0:T(8,128)(2,1)S(1)}, bf16[224,128,128]{2,1,0:T(8,128)(2,1)}, u32[]{:S(2)}) copy-start(bf16[224,128,128]{2,1,0:T(8,128)(2,1)} %blocks.5) | copy-start | bytes 22020100
  1.8 8.6 %collective-permute-start = (bf16[3,2,16,128]{3,2,1,0:T(8,128)(2,1)S(1)}, bf16[3,2,16,128]{3,2,1,0:T(8,128)(2,1)S(1)}, u32[]{:S(2)}, u32[]{:S(2)}) collective-permute-start(bf16[3,2,16,128]{3,2,1,0:T(8,128)(2,1)S(1)} %get-tuple-element.29), channel_id=1, source_target_pairs={{0,1},{1,0},{2,3},{3,2},{4,5},{5,4},{6,7},{7,6},{8,9},{9,8},{10,11... | collective-permute-start | bytes 73736 | tf_op jit(solution)/shard_map/ppermute | solution.py:72
  2.3 14.0 %collective-permute-start.1 = (bf16[2,2,16,128]{3,2,1,0:T(8,128)(2,1)S(1)}, bf16[2,2,16,128]{3,2,1,0:T(8,128)(2,1)S(1)}, u32[]{:S(2)}, u32[]{:S(2)}) collective-permute-start(bf16[2,2,16,128]{3,2,1,0:T(8,128)(2,1)S(1)} %get-tuple-element.30), channel_id=1, source_target_pairs={{0,31},{1,2},{2,1},{3,4},{4,3},{5,6},{6,5},{7,8},{8,7},{9,10},{10,... | collective-permute-start | bytes 49160 | tf_op jit(solution)/shard_map/ppermute | solution.py:72
  8.9 7.4 %collective-permute-start.2 = (bf16[2,2,16,128]{3,2,1,0:T(8,128)(2,1)S(1)}, bf16[2,2,16,128]{3,2,1,0:T(8,128)(2,1)S(1)}, u32[]{:S(2)}, u32[]{:S(2)}) collective-permute-start(bf16[2,2,16,128]{3,2,1,0:T(8,128)(2,1)S(1)} %get-tuple-element.31), channel_id=1, source_target_pairs={{0,23},{1,26},{2,25},{3,28},{4,27},{5,30},{6,29},{7,16},{8,15},{9,... | collective-permute-start | bytes 49160 | tf_op jit(solution)/shard_map/ppermute | solution.py:72
  9.1 7.3 %collective-permute-start.3 = (bf16[2,2,16,128]{3,2,1,0:T(8,128)(2,1)S(1)}, bf16[2,2,16,128]{3,2,1,0:T(8,128)(2,1)S(1)}, u32[]{:S(2)}, u32[]{:S(2)}) collective-permute-start(bf16[2,2,16,128]{3,2,1,0:T(8,128)(2,1)S(1)} %get-tuple-element.32), channel_id=1, source_target_pairs={{0,7},{1,10},{2,9},{3,12},{4,11},{5,14},{6,13},{7,0},{8,31},{9,2},... | collective-permute-start | bytes 49160 | tf_op jit(solution)/shard_map/ppermute | solution.py:72
  10.4 5.9 %collective-permute-start.4 = (bf16[2,2,16,128]{3,2,1,0:T(8,128)(2,1)S(1)}, bf16[2,2,16,128]{3,2,1,0:T(8,128)(2,1)S(1)}, u32[]{:S(2)}, u32[]{:S(2)}) collective-permute-start(bf16[2,2,16,128]{3,2,1,0:T(8,128)(2,1)S(1)} %pad_maximum_fusion.2), channel_id=1, source_target_pairs={{0,24},{1,25},{2,26},{3,27},{4,28},{5,29},{6,30},{7,31},{8,16},{9,... | collective-permute-start | bytes 49160 | tf_op jit(solution)/shard_map/ppermute | solution.py:72
  11.9 4.5 %collective-permute-start.5 = (bf16[2,2,16,128]{3,2,1,0:T(8,128)(2,1)S(1)}, bf16[2,2,16,128]{3,2,1,0:T(8,128)(2,1)S(1)}, u32[]{:S(2)}, u32[]{:S(2)}) collective-permute-start(bf16[2,2,16,128]{3,2,1,0:T(8,128)(2,1)S(1)} %pad_maximum_fusion.3), channel_id=1, source_target_pairs={{0,8},{1,9},{2,10},{3,11},{4,12},{5,13},{6,14},{7,15},{8,0},{9,1},... | collective-permute-start | bytes 49160 | tf_op jit(solution)/shard_map/ppermute | solution.py:72
  18.9 4.2 %collective-permute-start.6 = (f32[3,2,16,128]{3,2,1,0:T(8,128)S(1)}, f32[3,2,16,128]{3,2,1,0:T(8,128)S(1)}, u32[]{:S(2)}, u32[]{:S(2)}) collective-permute-start(f32[3,2,16,128]{3,2,1,0:T(8,128)S(1)} %get-tuple-element.38), channel_id=1, source_target_pairs={{0,1},{1,0},{2,3},{3,2},{4,5},{5,4},{6,7},{7,6},{8,9},{9,8},{10,11... | collective-permute-start | bytes 147464 | tf_op jit(solution)/shard_map/ppermute | solution.py:72
  19.0 8.5 %collective-permute-start.7 = (f32[2,2,16,128]{3,2,1,0:T(8,128)S(1)}, f32[2,2,16,128]{3,2,1,0:T(8,128)S(1)}, u32[]{:S(2)}, u32[]{:S(2)}) collective-permute-start(f32[2,2,16,128]{3,2,1,0:T(8,128)S(1)} %get-tuple-element.39), channel_id=1, source_target_pairs={{0,31},{1,2},{2,1},{3,4},{4,3},{5,6},{6,5},{7,8},{8,7},{9,10},{10,... | collective-permute-start | bytes 98312 | tf_op jit(solution)/shard_map/ppermute | solution.py:72
  20.6 6.9 %collective-permute-start.8 = (f32[2,2,16,128]{3,2,1,0:T(8,128)S(1)}, f32[2,2,16,128]{3,2,1,0:T(8,128)S(1)}, u32[]{:S(2)}, u32[]{:S(2)}) collective-permute-start(f32[2,2,16,128]{3,2,1,0:T(8,128)S(1)} %get-tuple-element.40), channel_id=1, source_target_pairs={{0,23},{1,26},{2,25},{3,28},{4,27},{5,30},{6,29},{7,16},{8,15},{9,... | collective-permute-start | bytes 98312 | tf_op jit(solution)/shard_map/ppermute | solution.py:72
  22.9 4.6 %collective-permute-start.9 = (f32[2,2,16,128]{3,2,1,0:T(8,128)S(1)}, f32[2,2,16,128]{3,2,1,0:T(8,128)S(1)}, u32[]{:S(2)}, u32[]{:S(2)}) collective-permute-start(f32[2,2,16,128]{3,2,1,0:T(8,128)S(1)} %get-tuple-element.41), channel_id=1, source_target_pairs={{0,7},{1,10},{2,9},{3,12},{4,11},{5,14},{6,13},{7,0},{8,31},{9,2},... | collective-permute-start | bytes 98312 | tf_op jit(solution)/shard_map/ppermute | solution.py:72
  23.1 5.8 %collective-permute-start.10 = (f32[2,2,16,128]{3,2,1,0:T(8,128)S(1)}, f32[2,2,16,128]{3,2,1,0:T(8,128)S(1)}, u32[]{:S(2)}, u32[]{:S(2)}) collective-permute-start(f32[2,2,16,128]{3,2,1,0:T(8,128)S(1)} %pad_maximum_fusion), channel_id=1, source_target_pairs={{0,24},{1,25},{2,26},{3,27},{4,28},{5,29},{6,30},{7,31},{8,16},{9,... | collective-permute-start | bytes 98312 | tf_op jit(solution)/shard_map/ppermute | solution.py:72
  25.6 3.9 %collective-permute-start.11 = (f32[2,2,16,128]{3,2,1,0:T(8,128)S(1)}, f32[2,2,16,128]{3,2,1,0:T(8,128)S(1)}, u32[]{:S(2)}, u32[]{:S(2)}) collective-permute-start(f32[2,2,16,128]{3,2,1,0:T(8,128)S(1)} %pad_maximum_fusion.1), channel_id=1, source_target_pairs={{0,8},{1,9},{2,10},{3,11},{4,12},{5,13},{6,14},{7,15},{8,0},{9,1},... | collective-permute-start | bytes 98312 | tf_op jit(solution)/shard_map/ppermute | solution.py:72

commit v7 on v6

--- a/solution.py
+++ b/solution.py
@@ -30,8 +30,10 @@
 
 def directions():
     outer, inner = lax.axis_index("dom"), lax.axis_index("sub")
-    past = (inner == lax.axis_size("sub") - 1).astype(jnp.int32)
-    return 2 * lax.rem(inner, 2) - 1, 1 - 2 * lax.rem(outer + past, 2), 1 - 2 * lax.rem(outer, 2)
+    edge = (inner == 0) | (inner == lax.axis_size("sub") - 1)
+    s = 2 * lax.rem(inner, 2) - 1
+    u = 1 - 2 * lax.rem(outer, 2)
+    return s, u, jnp.where(edge, -u, u)
 
 
 def columns(block_row):
@@ -42,33 +44,31 @@
     return jnp.concatenate([ref[place] for place in places], axis=axis)
 
 
-def sent(s, t, u):
+def sent(s, u, p):
     return (
         ((0, -s), (u, -s), (-u, -s)),
-        ((0, s),),
-        ((-t, s),),
-        ((t, s),),
+        ((0, s), (p, s)),
+        ((-p, s),),
         ((-u, 0),),
         ((u, 0),),
     )
 
 
-def received(s, t, u):
+def received(s, u, p):
     return (
         ((0, s),),
         ((0, -s),),
-        ((t, -s),),
-        ((-t, -s),),
+        ((u, -s),),
         ((u, 0), (u, s)),
-        ((-u, 0), (-u, s)),
-    )
-
-
-def exchange(pair, side, cross_far, cross_near, far, near):
+        ((-u, 0), (-u, s), (-u, -s)),
+    )
+
+
+def exchange(pair, side, cross, far, near):
     n_inner = lax.axis_size("sub")
     devices = lax.axis_size("dom") * n_inner
 
-    def swap(array, target):
+    def move(array, target):
         return lax.ppermute(array, AXES, [(d, target(d) % devices) for d in range(devices)])
 
     def step(d):
@@ -77,17 +77,15 @@
     def towards(d):
         return n_inner if (d // n_inner) % 2 == 0 else -n_inner
 
-    def diagonal(d, sign):
-        past = (d + d % 2) % devices
-        return d + step(d) + sign * towards(past)
-
-    pair = swap(pair, lambda d: d - step(d))
-    side = swap(side, lambda d: d + step(d))
-    cross_far = swap(cross_far, lambda d: diagonal(d, -1))
-    cross_near = swap(cross_near, lambda d: diagonal(d, 1))
-    far = swap(jnp.concatenate([far, pair[2:3]], axis=0), lambda d: d - towards(d))
-    near = swap(jnp.concatenate([near, pair[1:2]], axis=0), lambda d: d + towards(d))
-    return pair, side, cross_far, cross_near, far, near
+    def beside(d):
+        return (d + step(d)) % devices
+
+    pair = move(pair, lambda d: d - step(d))
+    side = move(side, beside)
+    cross = move(cross, lambda d: beside(d) - towards(beside(d)))
+    far = move(jnp.concatenate([far, pair[2:3], far], axis=0), lambda d: d - towards(d))
+    near = move(jnp.concatenate([near, pair[1:2], side[1:2]], axis=0), lambda d: d + towards(d))
+    return pair, side, cross, far, near
 
 
 def rounded(size):
@@ -95,7 +93,7 @@
 
 
 def gather_kernel(send_hbm, vectors_hbm, ptr_hbm, col_hbm, blocks_hbm, vectors, plan, send_lines, *refs):
-    outgoing, (send, ptr, col, sems) = refs[:6], refs[6:]
+    outgoing, (send, ptr, col, sems) = refs[:5], refs[5:]
     copies = [
         pltpu.make_async_copy(source, target, sems.at[i])
         for i, (source, target) in enumerate(
@@ -137,8 +135,8 @@
 
 
 def ghost_kernel(plan, blocks, partial_image, *refs):
-    arrived, image, outgoing = refs[:6], refs[6], refs[7:13]
-    ghosts, total, spread, long_rows = refs[13:]
+    arrived, image, outgoing = refs[:5], refs[5], refs[6:11]
+    ghosts, total, spread, long_rows = refs[11:]
     rows = image.shape[0]
     many = long_rows.shape[0] - 1
     first_column = rounded(rows + 1)
@@ -221,7 +219,7 @@
 
 
 def gram_kernel(send, partial_adjoint, norms, *refs):
-    arrived, adjoint, packed = refs[:6], refs[6], refs[7]
+    arrived, adjoint, packed = refs[:5], refs[5], refs[6]
     k = adjoint.shape[0]
     way = directions()
     for ref, offsets in zip(arrived, received(*way)):
@@ -308,7 +306,7 @@
     ghost = send_list.shape[2]
     slots = send_list.shape[1] * ghost
     many = (stored - SHORT * rows) // (LONG - SHORT)
-    sizes = (3, 2, 2, 2, 1, 1)
+    sizes = (3, 3, 4, 1, 1)
     send_lines = jnp.transpose(send_list, (0, 2, 1))
     inputs = (send_lines, vectors, row_ptr, col_index, blocks)
     here, plan, send, *outgoing = call(
@@ -337,7 +335,7 @@
         ghost_kernel,
         "ghost",
         [((rows, k, B), BF16)] + [((n, ghost, k, B), F32) for n in sizes],
-        [SMEM] + [VMEM] * 8,
+        [SMEM] + [VMEM] * 7,
         scratch=[
             pltpu.VMEM((slots, k, B), BF16),
             pltpu.VMEM((rows, k, B), F32),
@@ -360,7 +358,7 @@
         gram_kernel,
         "gram",
         [((k, unknowns), F32), ((devices, 4, B), F32)],
-        [SMEM] + [VMEM] * 8,
+        [SMEM] + [VMEM] * 7,
         alias={1: 0},
     )(send, partial_adjoint, norms, *returned)
     everywhere = lax.all_to_all(packed, AXES, 0, 0)

time: 42.5 us -> 42 us (0.988)
  starting transfers between devices: 20 us -> 13.7 us
  waiting for transfers between devices: 2.06 us -> 8.24 us
    ppermute x12 -> x10, starting transfers between devices: 20 us -> 13.7 us  [move(): lax.ppermute(array, AXES, [(d, target(d) % devices) for d in range(device...]
    ppermute x12 -> x10, waiting for transfers between devices: 2.06 us -> 8.24 us  [move(): lax.ppermute(array, AXES, [(d, target(d) % devices) for d in range(device...]
  transfers between devices with their start and end apart: 12 -> 10, of which waited for: 2 -> 4; matrix products, arithmetic and copies ran while one was open for 0% -> 0% of each run, Pallas kernels for 7% -> 7%
where the time goes in v7:
time: 42 us; the launch traced here: 41.8 us
  starting transfers between devices  13.7 us (33%)
  blocking collectives  9.62 us (23%)
  Pallas kernels  9.54 us (23%)
  waiting for transfers between devices  8.24 us (20%)
  between operations  0.73 us (2%)
    ppermute x10, starting transfers between devices, move(): lax.ppermute(array, AXES, [(d, target(d) % devices) for d in range(device...  13.7 us
    all_to_all x1, blocking collectives, local(): everywhere = lax.all_to_all(packed, AXES, 0, 0)  9.62 us
    ppermute x10, waiting for transfers between devices, move(): lax.ppermute(array, AXES, [(d, target(d) % devices) for d in range(device...  8.24 us
    pallas_call x1, Pallas kernels, local(): call(ghost_kernel, 'ghost', [((rows, k, B), BF16)] + [((n, ghost, k, B),...  2.56 us
    pallas_call x1, Pallas kernels, local(): call(local_forward_kernel, 'local_forward', [((rows, k, B), F32)], [SMEM,...  1.75 us
    pallas_call x1, Pallas kernels, local(): call(functools.partial(solve_kernel, unknowns * devices), 'solve', [((k,...  1.66 us
    pallas_call x1, Pallas kernels, local(): call(local_backward_kernel, 'local_backward', [((k, unknowns), F32), ((1,...  1.21 us
    pallas_call x1, Pallas kernels, local(): call(gram_kernel, 'gram', [((k, unknowns), F32), ((devices, 4, B), F32)],...  1.21 us
  transfers between devices with their start and end apart: 10, of which 4 were waited for; matrix products, arithmetic and copies ran while one was open for 0% of the time, Pallas kernels for 7%

profile of v7, /device:TPU:0, one launch (start us, length us, event | category | flops | bytes accessed | tf_op | source)
XLA Modules:
  0.0 41.8 jit_solution(12096182012224625739)
XLA Ops:
  0.6 1.1 %gather.1 = (bf16[16,4096]{1,0:T(8,128)(2,1)S(1)}, s32[1,384]{1,0:T(1,128)S(1)}, s32[1,2,8]{2,1,0:T(2,128)S(1)}, bf16[3,2,16,128]{3,2,1,0:T(8,128)(2,1)S(1)}, bf...) custom-call(s32[1,2,8]{2,1,0:T(2,128)} %bitcast.2, ...), custom_call_target="tpu_custom_call" | custom-call | tf_op jit(solution)/shard_map/gather/pallas_call | solution.py:312
  1.8 0.5 %collective-permute-start = (bf16[3,2,16,128]{3,2,1,0:T(8,128)(2,1)S(1)}, bf16[3,2,16,128]{3,2,1,0:T(8,128)(2,1)S(1)}, u32[]{:S(2)}, u32[]{:S(2)}) collective-permute-start(bf16[3,2,16,128]{3,2,1,0:T(8,128)(2,1)S(1)} %get-tuple-element.27), channel_id=1, source_target_pairs={{0,1},{1,0},{2,3},{3,2},{4,5},{5,4},{6,7},{7,6},{8,9},{9,8},{10,11... | collective-permute-start | bytes 73736 | tf_op jit(solution)/shard_map/ppermute | solution.py:72
  2.3 6.6 %collective-permute-start.1 = (bf16[3,2,16,128]{3,2,1,0:T(8,128)(2,1)S(1)}, bf16[3,2,16,128]{3,2,1,0:T(8,128)(2,1)S(1)}, u32[]{:S(2)}, u32[]{:S(2)}) collective-permute-start(bf16[3,2,16,128]{3,2,1,0:T(8,128)(2,1)S(1)} %get-tuple-element.28), channel_id=1, source_target_pairs={{0,31},{1,2},{2,1},{3,4},{4,3},{5,6},{6,5},{7,8},{8,7},{9,10},{10,... | collective-permute-start | bytes 73736 | tf_op jit(solution)/shard_map/ppermute | solution.py:72
  8.9 0.0 collective-permute-start.2
  8.9 0.0 collective-permute-done.refs_0_
  8.9 1.6 %collective-permute-start.3 = (bf16[3,2,16,128]{3,2,1,0:T(8,128)(2,1)S(1)}, bf16[3,2,16,128]{3,2,1,0:T(8,128)(2,1)S(1)}, u32[]{:S(2)}, u32[]{:S(2)}) collective-permute-start(bf16[3,2,16,128]{3,2,1,0:T(8,128)(2,1)S(1)} %pad_maximum_fusion.2), channel_id=1, source_target_pairs={{0,24},{1,25},{2,26},{3,27},{4,28},{5,29},{6,30},{7,31},{8,16},{9,... | collective-permute-start | bytes 73736 | tf_op jit(solution)/shard_map/ppermute | solution.py:72
  10.5 0.1 collective-permute-start.4
  10.6 1.8 %local_forward.1.partial_image = f32[32,16,128]{2,1,0:T(8,128)S(1)} custom-call(s32[1,384]{1,0:T(1,128)S(1)} %get-tuple-element.25.plan, bf16[16,4096]{1,0:T(8,128)(2,1)S(1)} %get-tuple-element.26.vectors, bf16[224,128,128]{2,1,0:T(8,128)(2,1)S(1)} %copy-done), custom_call_target="tpu_custom_call" | custom-call | flops 50331648 | bytes 3145728 | tf_op jit(solution)/shard_map/local_forward/pallas_call | solution.py:326
  12.4 2.9 %collective-permute-done.2.refs_2_ = bf16[4,2,16,128]{3,2,1,0:T(8,128)(2,1)S(1)} collective-permute-done((bf16[4,2,16,128]{3,2,1,0:T(8,128)(2,1)S(1)}, bf16[4,2,16,128]{3,2,1,0:T(8,128)(2,1)S(1)}, u32[]{:S(2)}, u32[]{:S(2)}) %collective-permute-start.2) | collective-permute-done | bytes 32800 | tf_op jit(solution)/shard_map/ppermute | solution.py:72
  15.2 0.0 collective-permute-done.3.refs_3_
  15.2 0.0 collective-permute-done.4.refs_4_
  15.2 2.6 %ghost.1 = (bf16[32,16,128]{2,1,0:T(8,128)(2,1)S(1)}, f32[3,2,16,128]{3,2,1,0:T(8,128)S(1)}, f32[3,2,16,128]{3,2,1,0:T(8,128)S(1)}, f32[4,2,16,128]{3,2,1,0:T(8,...) custom-call(s32[1,384]{1,0:T(1,128)S(1)} %get-tuple-element.25.plan, ...), custom_call_target="tpu_custom_call" | custom-call | flops 134217728 | bytes 8388608 | tf_op jit(solution)/shard_map/ghost/pallas_call | solution.py:334
  17.8 0.1 collective-permute-start.5
  17.9 3.4 %collective-permute-start.6 = (f32[3,2,16,128]{3,2,1,0:T(8,128)S(1)}, f32[3,2,16,128]{3,2,1,0:T(8,128)S(1)}, u32[]{:S(2)}, u32[]{:S(2)}) collective-permute-start(f32[3,2,16,128]{3,2,1,0:T(8,128)S(1)} %get-tuple-element.36), channel_id=1, source_target_pairs={{0,31},{1,2},{2,1},{3,4},{4,3},{5,6},{6,5},{7,8},{8,7},{9,10},{10,... | collective-permute-start | bytes 147464 | tf_op jit(solution)/shard_map/ppermute | solution.py:72
  21.3 1.4 %collective-permute-start.8 = (f32[3,2,16,128]{3,2,1,0:T(8,128)S(1)}, f32[3,2,16,128]{3,2,1,0:T(8,128)S(1)}, u32[]{:S(2)}, u32[]{:S(2)}) collective-permute-start(f32[3,2,16,128]{3,2,1,0:T(8,128)S(1)} %pad_maximum_fusion), channel_id=1, source_target_pairs={{0,24},{1,25},{2,26},{3,27},{4,28},{5,29},{6,30},{7,31},{8,16},{9,... | collective-permute-start | bytes 147464 | tf_op jit(solution)/shard_map/ppermute | solution.py:72
  22.7 2.5 %collective-permute-done.6.refs_1_ = f32[3,2,16,128]{3,2,1,0:T(8,128)S(1)} collective-permute-done((f32[3,2,16,128]{3,2,1,0:T(8,128)S(1)}, f32[3,2,16,128]{3,2,1,0:T(8,128)S(1)}, u32[]{:S(2)}, u32[]{:S(2)}) %collective-permute-start.6) | collective-permute-done | bytes 49184 | tf_op jit(solution)/shard_map/ppermute | solution.py:72
  25.2 0.1 collective-permute-start.9
  25.3 1.2 %local_backward.1 = (f32[16,4096]{1,0:T(8,128)S(1)}, f32[1,128]{1,0:T(1,128)S(1)}) custom-call(s32[1,384]{1,0:T(1,128)S(1)} %get-tuple-element.25.plan, bf16[224,128,128]{2,1,0:T(8,128)(2,1)S(1)} %copy-done, bf16[32,16,128]{2,1,0:T(8,128)(2,1)S(1)} %get-tuple-element.32.image), custom_call_target="tpu_custom_call" | custom-call | flops 50331648 | bytes 3145728 | tf_op jit(solution)/shard_map/local_backward/pallas_call | solution.py:349
  26.5 1.8 %collective-permute-done.7.refs_2_ = f32[4,2,16,128]{3,2,1,0:T(8,128)S(1)} collective-permute-done((f32[4,2,16,128]{3,2,1,0:T(8,128)S(1)}, f32[4,2,16,128]{3,2,1,0:T(8,128)S(1)}, u32[]{:S(2)}, u32[]{:S(2)}) %collective-permute-start.7) | collective-permute-done | bytes 65568 | tf_op jit(solution)/shard_map/ppermute | solution.py:72
  28.3 0.0 collective-permute-done.8.refs_3_
  28.3 1.1 %collective-permute-done.9.refs_4_ = f32[3,2,16,128]{3,2,1,0:T(8,128)S(1)} collective-permute-done((f32[3,2,16,128]{3,2,1,0:T(8,128)S(1)}, f32[3,2,16,128]{3,2,1,0:T(8,128)S(1)}, u32[]{:S(2)}, u32[]{:S(2)}) %collective-permute-start.9) | collective-permute-done | bytes 49184 | tf_op jit(solution)/shard_map/ppermute | solution.py:72
  29.3 1.2 %gram.1 = (f32[16,4096]{1,0:T(8,128)S(1)}, f32[32,4,128]{2,1,0:T(4,128)S(1)}) custom-call(s32[1,2,8]{2,1,0:T(2,128)S(1)} %get-tuple-element.24.send, f32[16,4096]{1,0:T(8,128)S(1)} %get-tuple-element.33.partial_adjoint, f32[1,128]{1,0:T(1,128)S(1)} %get-tuple-element.34.norms, ...), custom_call_target="tpu_custom_call", output_to_operand_aliasing={{0}: (1, {})} | custom-call | tf_op jit(solution)/shard_map/gram/pallas_call | solution.py:357
  30.5 9.6 %all_to_all.5.packed = f32[32,4,128]{2,1,0:T(4,128)S(1)} all-to-all(f32[32,4,128]{2,1,0:T(4,128)S(1)} %get-tuple-element.40), channel_id=1, replica_groups=mesh['dom'=4,'sub'=8] {'dom','sub'}, dimensions={0} | all-to-all | bytes 131072 | tf_op jit(solution)/shard_map/all_to_all | solution.py:364
  40.2 1.7 %solve.1 = (f32[16,4096]{1,0:T(8,128)}, f32[16,16]{1,0:T(8,128)}, f32[1,16]{1,0:T(1,128)}) custom-call(f32[32,4,128]{2,1,0:T(4,128)S(1)} %all_to_all.5.packed, f32[16,4096]{1,0:T(8,128)S(1)} %get-tuple-element.41.adjoint), custom_call_target="tpu_custom_call" | custom-call | tf_op jit(solution)/shard_map/solve/pallas_call | solution.py:366
  (13 shorter events, 0.0 us)
Async XLA Ops:
  0.6 10.0 %copy-start = (bf16[224,128,128]{2,1,0:T(8,128)(2,1)S(1)}, bf16[224,128,128]{2,1,0:T(8,128)(2,1)}, u32[]{:S(2)}) copy-start(bf16[224,128,128]{2,1,0:T(8,128)(2,1)} %blocks.5) | copy-start | bytes 22020100
  1.8 7.1 %collective-permute-start = (bf16[3,2,16,128]{3,2,1,0:T(8,128)(2,1)S(1)}, bf16[3,2,16,128]{3,2,1,0:T(8,128)(2,1)S(1)}, u32[]{:S(2)}, u32[]{:S(2)}) collective-permute-start(bf16[3,2,16,128]{3,2,1,0:T(8,128)(2,1)S(1)} %get-tuple-element.27), channel_id=1, source_target_pairs={{0,1},{1,0},{2,3},{3,2},{4,5},{5,4},{6,7},{7,6},{8,9},{9,8},{10,11... | collective-permute-start | bytes 73736 | tf_op jit(solution)/shard_map/ppermute | solution.py:72
  2.3 8.2 %collective-permute-start.1 = (bf16[3,2,16,128]{3,2,1,0:T(8,128)(2,1)S(1)}, bf16[3,2,16,128]{3,2,1,0:T(8,128)(2,1)S(1)}, u32[]{:S(2)}, u32[]{:S(2)}) collective-permute-start(bf16[3,2,16,128]{3,2,1,0:T(8,128)(2,1)S(1)} %get-tuple-element.28), channel_id=1, source_target_pairs={{0,31},{1,2},{2,1},{3,4},{4,3},{5,6},{6,5},{7,8},{8,7},{9,10},{10,... | collective-permute-start | bytes 73736 | tf_op jit(solution)/shard_map/ppermute | solution.py:72
  8.9 6.3 %collective-permute-start.2 = (bf16[4,2,16,128]{3,2,1,0:T(8,128)(2,1)S(1)}, bf16[4,2,16,128]{3,2,1,0:T(8,128)(2,1)S(1)}, u32[]{:S(2)}, u32[]{:S(2)}) collective-permute-start(bf16[4,2,16,128]{3,2,1,0:T(8,128)(2,1)S(1)} %get-tuple-element.29), channel_id=1, source_target_pairs={{0,7},{1,26},{2,25},{3,28},{4,27},{5,30},{6,29},{7,16},{8,31},{9,1... | collective-permute-start | bytes 98312 | tf_op jit(solution)/shard_map/ppermute | solution.py:72
  8.9 6.3 %collective-permute-start.3 = (bf16[3,2,16,128]{3,2,1,0:T(8,128)(2,1)S(1)}, bf16[3,2,16,128]{3,2,1,0:T(8,128)(2,1)S(1)}, u32[]{:S(2)}, u32[]{:S(2)}) collective-permute-start(bf16[3,2,16,128]{3,2,1,0:T(8,128)(2,1)S(1)} %pad_maximum_fusion.2), channel_id=1, source_target_pairs={{0,24},{1,25},{2,26},{3,27},{4,28},{5,29},{6,30},{7,31},{8,16},{9,... | collective-permute-start | bytes 73736 | tf_op jit(solution)/shard_map/ppermute | solution.py:72
  10.5 4.7 %collective-permute-start.4 = (bf16[3,2,16,128]{3,2,1,0:T(8,128)(2,1)S(1)}, bf16[3,2,16,128]{3,2,1,0:T(8,128)(2,1)S(1)}, u32[]{:S(2)}, u32[]{:S(2)}) collective-permute-start(bf16[3,2,16,128]{3,2,1,0:T(8,128)(2,1)S(1)} %pad_maximum_fusion.3), channel_id=1, source_target_pairs={{0,8},{1,9},{2,10},{3,11},{4,12},{5,13},{6,14},{7,15},{8,0},{9,1},... | collective-permute-start | bytes 73736 | tf_op jit(solution)/shard_map/ppermute | solution.py:72
  17.8 3.5 %collective-permute-start.5 = (f32[3,2,16,128]{3,2,1,0:T(8,128)S(1)}, f32[3,2,16,128]{3,2,1,0:T(8,128)S(1)}, u32[]{:S(2)}, u32[]{:S(2)}) collective-permute-start(f32[3,2,16,128]{3,2,1,0:T(8,128)S(1)} %get-tuple-element.35), channel_id=1, source_target_pairs={{0,1},{1,0},{2,3},{3,2},{4,5},{5,4},{6,7},{7,6},{8,9},{9,8},{10,11... | collective-permute-start | bytes 147464 | tf_op jit(solution)/shard_map/ppermute | solution.py:72
  17.9 7.3 %collective-permute-start.6 = (f32[3,2,16,128]{3,2,1,0:T(8,128)S(1)}, f32[3,2,16,128]{3,2,1,0:T(8,128)S(1)}, u32[]{:S(2)}, u32[]{:S(2)}) collective-permute-start(f32[3,2,16,128]{3,2,1,0:T(8,128)S(1)} %get-tuple-element.36), channel_id=1, source_target_pairs={{0,31},{1,2},{2,1},{3,4},{4,3},{5,6},{6,5},{7,8},{8,7},{9,10},{10,... | collective-permute-start | bytes 147464 | tf_op jit(solution)/shard_map/ppermute | solution.py:72
  21.2 7.0 %collective-permute-start.7 = (f32[4,2,16,128]{3,2,1,0:T(8,128)S(1)}, f32[4,2,16,128]{3,2,1,0:T(8,128)S(1)}, u32[]{:S(2)}, u32[]{:S(2)}) collective-permute-start(f32[4,2,16,128]{3,2,1,0:T(8,128)S(1)} %get-tuple-element.37), channel_id=1, source_target_pairs={{0,7},{1,26},{2,25},{3,28},{4,27},{5,30},{6,29},{7,16},{8,31},{9,1... | collective-permute-start | bytes 196616 | tf_op jit(solution)/shard_map/ppermute | solution.py:72
  21.3 7.0 %collective-permute-start.8 = (f32[3,2,16,128]{3,2,1,0:T(8,128)S(1)}, f32[3,2,16,128]{3,2,1,0:T(8,128)S(1)}, u32[]{:S(2)}, u32[]{:S(2)}) collective-permute-start(f32[3,2,16,128]{3,2,1,0:T(8,128)S(1)} %pad_maximum_fusion), channel_id=1, source_target_pairs={{0,24},{1,25},{2,26},{3,27},{4,28},{5,29},{6,30},{7,31},{8,16},{9,... | collective-permute-start | bytes 147464 | tf_op jit(solution)/shard_map/ppermute | solution.py:72
  25.2 4.1 %collective-permute-start.9 = (f32[3,2,16,128]{3,2,1,0:T(8,128)S(1)}, f32[3,2,16,128]{3,2,1,0:T(8,128)S(1)}, u32[]{:S(2)}, u32[]{:S(2)}) collective-permute-start(f32[3,2,16,128]{3,2,1,0:T(8,128)S(1)} %pad_maximum_fusion.1), channel_id=1, source_target_pairs={{0,8},{1,9},{2,10},{3,11},{4,12},{5,13},{6,14},{7,15},{8,0},{9,1},... | collective-permute-start | bytes 147464 | tf_op jit(solution)/shard_map/ppermute | solution.py:72

commit v8 on v7

--- a/solution.py
+++ b/solution.py
@@ -306,7 +306,7 @@
     ghost = send_list.shape[2]
     slots = send_list.shape[1] * ghost
     many = (stored - SHORT * rows) // (LONG - SHORT)
-    sizes = (3, 3, 4, 1, 1)
+    sizes = (3, 3, 3, 1, 1)
     send_lines = jnp.transpose(send_list, (0, 2, 1))
     inputs = (send_lines, vectors, row_ptr, col_index, blocks)
     here, plan, send, *outgoing = call(

time: 42 us -> 42 us (level)
  no operation moved by 1% of the time
where the time goes in v8:
time: 42 us; the launch traced here: 41.8 us
  starting transfers between devices  13.8 us (33%)
  blocking collectives  9.88 us (24%)
  Pallas kernels  9.5 us (23%)
  waiting for transfers between devices  7.92 us (19%)
  between operations  0.73 us (2%)
    ppermute x10, starting transfers between devices, move(): lax.ppermute(array, AXES, [(d, target(d) % devices) for d in range(device...  13.8 us
    all_to_all x1, blocking collectives, local(): everywhere = lax.all_to_all(packed, AXES, 0, 0)  9.88 us
    ppermute x10, waiting for transfers between devices, move(): lax.ppermute(array, AXES, [(d, target(d) % devices) for d in range(device...  7.92 us
    pallas_call x1, Pallas kernels, local(): call(ghost_kernel, 'ghost', [((rows, k, B), BF16)] + [((n, ghost, k, B),...  2.56 us
    pallas_call x1, Pallas kernels, local(): call(local_forward_kernel, 'local_forward', [((rows, k, B), F32)], [SMEM,...  1.75 us
    pallas_call x1, Pallas kernels, local(): call(functools.partial(solve_kernel, unknowns * devices), 'solve', [((k,...  1.67 us
    pallas_call x1, Pallas kernels, local(): call(local_backward_kernel, 'local_backward', [((k, unknowns), F32), ((1,...  1.21 us
    pallas_call x1, Pallas kernels, local(): call(gram_kernel, 'gram', [((k, unknowns), F32), ((devices, 4, B), F32)],...  1.16 us
  transfers between devices with their start and end apart: 10, of which 4 were waited for; matrix products, arithmetic and copies ran while one was open for 0% of the time, Pallas kernels for 7%

profile of v8, /device:TPU:0, one launch (start us, length us, event | category | flops | bytes accessed | tf_op | source)
XLA Modules:
  0.0 41.8 jit_solution(7532276427753252022)
XLA Ops:
  0.6 1.1 %gather.1 = (bf16[16,4096]{1,0:T(8,128)(2,1)S(1)}, s32[1,384]{1,0:T(1,128)S(1)}, s32[1,2,8]{2,1,0:T(2,128)S(1)}, bf16[3,2,16,128]{3,2,1,0:T(8,128)(2,1)S(1)}, bf...) custom-call(s32[1,2,8]{2,1,0:T(2,128)} %bitcast.2, ...), custom_call_target="tpu_custom_call" | custom-call | tf_op jit(solution)/shard_map/gather/pallas_call | solution.py:312
  1.8 0.5 %collective-permute-start = (bf16[3,2,16,128]{3,2,1,0:T(8,128)(2,1)S(1)}, bf16[3,2,16,128]{3,2,1,0:T(8,128)(2,1)S(1)}, u32[]{:S(2)}, u32[]{:S(2)}) collective-permute-start(bf16[3,2,16,128]{3,2,1,0:T(8,128)(2,1)S(1)} %get-tuple-element.27), channel_id=1, source_target_pairs={{0,1},{1,0},{2,3},{3,2},{4,5},{5,4},{6,7},{7,6},{8,9},{9,8},{10,11... | collective-permute-start | bytes 73736 | tf_op jit(solution)/shard_map/ppermute | solution.py:72
  2.3 6.6 %collective-permute-start.1 = (bf16[3,2,16,128]{3,2,1,0:T(8,128)(2,1)S(1)}, bf16[3,2,16,128]{3,2,1,0:T(8,128)(2,1)S(1)}, u32[]{:S(2)}, u32[]{:S(2)}) collective-permute-start(bf16[3,2,16,128]{3,2,1,0:T(8,128)(2,1)S(1)} %get-tuple-element.28), channel_id=1, source_target_pairs={{0,31},{1,2},{2,1},{3,4},{4,3},{5,6},{6,5},{7,8},{8,7},{9,10},{10,... | collective-permute-start | bytes 73736 | tf_op jit(solution)/shard_map/ppermute | solution.py:72
  8.9 0.0 collective-permute-start.2
  8.9 0.0 collective-permute-done.refs_0_
  8.9 1.6 %collective-permute-start.3 = (bf16[3,2,16,128]{3,2,1,0:T(8,128)(2,1)S(1)}, bf16[3,2,16,128]{3,2,1,0:T(8,128)(2,1)S(1)}, u32[]{:S(2)}, u32[]{:S(2)}) collective-permute-start(bf16[3,2,16,128]{3,2,1,0:T(8,128)(2,1)S(1)} %pad_maximum_fusion.2), channel_id=1, source_target_pairs={{0,24},{1,25},{2,26},{3,27},{4,28},{5,29},{6,30},{7,31},{8,16},{9,... | collective-permute-start | bytes 73736 | tf_op jit(solution)/shard_map/ppermute | solution.py:72
  10.5 0.1 collective-permute-start.4
  10.6 1.8 %local_forward.1.partial_image = f32[32,16,128]{2,1,0:T(8,128)S(1)} custom-call(s32[1,384]{1,0:T(1,128)S(1)} %get-tuple-element.25.plan, bf16[16,4096]{1,0:T(8,128)(2,1)S(1)} %get-tuple-element.26.vectors, bf16[224,128,128]{2,1,0:T(8,128)(2,1)S(1)} %copy-done), custom_call_target="tpu_custom_call" | custom-call | flops 50331648 | bytes 3145728 | tf_op jit(solution)/shard_map/local_forward/pallas_call | solution.py:326
  12.4 2.8 %collective-permute-done.2.refs_2_ = bf16[3,2,16,128]{3,2,1,0:T(8,128)(2,1)S(1)} collective-permute-done((bf16[3,2,16,128]{3,2,1,0:T(8,128)(2,1)S(1)}, bf16[3,2,16,128]{3,2,1,0:T(8,128)(2,1)S(1)}, u32[]{:S(2)}, u32[]{:S(2)}) %collective-permute-start.2) | collective-permute-done | bytes 24608 | tf_op jit(solution)/shard_map/ppermute | solution.py:72
  15.1 0.0 collective-permute-done.3.refs_3_
  15.1 0.0 collective-permute-done.4.refs_4_
  15.1 2.6 %ghost.1 = (bf16[32,16,128]{2,1,0:T(8,128)(2,1)S(1)}, f32[3,2,16,128]{3,2,1,0:T(8,128)S(1)}, f32[3,2,16,128]{3,2,1,0:T(8,128)S(1)}, f32[3,2,16,128]{3,2,1,0:T(8,...) custom-call(s32[1,384]{1,0:T(1,128)S(1)} %get-tuple-element.25.plan, ...), custom_call_target="tpu_custom_call" | custom-call | flops 134217728 | bytes 8388608 | tf_op jit(solution)/shard_map/ghost/pallas_call | solution.py:334
  17.7 0.1 collective-permute-start.5
  17.8 3.5 %collective-permute-start.6 = (f32[3,2,16,128]{3,2,1,0:T(8,128)S(1)}, f32[3,2,16,128]{3,2,1,0:T(8,128)S(1)}, u32[]{:S(2)}, u32[]{:S(2)}) collective-permute-start(f32[3,2,16,128]{3,2,1,0:T(8,128)S(1)} %get-tuple-element.36), channel_id=1, source_target_pairs={{0,31},{1,2},{2,1},{3,4},{4,3},{5,6},{6,5},{7,8},{8,7},{9,10},{10,... | collective-permute-start | bytes 147464 | tf_op jit(solution)/shard_map/ppermute | solution.py:72
  21.2 0.0 collective-permute-start.7
  21.3 1.4 %collective-permute-start.8 = (f32[3,2,16,128]{3,2,1,0:T(8,128)S(1)}, f32[3,2,16,128]{3,2,1,0:T(8,128)S(1)}, u32[]{:S(2)}, u32[]{:S(2)}) collective-permute-start(f32[3,2,16,128]{3,2,1,0:T(8,128)S(1)} %pad_maximum_fusion), channel_id=1, source_target_pairs={{0,24},{1,25},{2,26},{3,27},{4,28},{5,29},{6,30},{7,31},{8,16},{9,... | collective-permute-start | bytes 147464 | tf_op jit(solution)/shard_map/ppermute | solution.py:72
  22.7 2.3 %collective-permute-done.6.refs_1_ = f32[3,2,16,128]{3,2,1,0:T(8,128)S(1)} collective-permute-done((f32[3,2,16,128]{3,2,1,0:T(8,128)S(1)}, f32[3,2,16,128]{3,2,1,0:T(8,128)S(1)}, u32[]{:S(2)}, u32[]{:S(2)}) %collective-permute-start.6) | collective-permute-done | bytes 49184 | tf_op jit(solution)/shard_map/ppermute | solution.py:72
  25.0 0.1 collective-permute-start.9
  25.0 1.2 %local_backward.1 = (f32[16,4096]{1,0:T(8,128)S(1)}, f32[1,128]{1,0:T(1,128)S(1)}) custom-call(s32[1,384]{1,0:T(1,128)S(1)} %get-tuple-element.25.plan, bf16[224,128,128]{2,1,0:T(8,128)(2,1)S(1)} %copy-done, bf16[32,16,128]{2,1,0:T(8,128)(2,1)S(1)} %get-tuple-element.32.image), custom_call_target="tpu_custom_call" | custom-call | flops 50331648 | bytes 3145728 | tf_op jit(solution)/shard_map/local_backward/pallas_call | solution.py:349
  26.2 1.8 %collective-permute-done.7.refs_2_ = f32[3,2,16,128]{3,2,1,0:T(8,128)S(1)} collective-permute-done((f32[3,2,16,128]{3,2,1,0:T(8,128)S(1)}, f32[3,2,16,128]{3,2,1,0:T(8,128)S(1)}, u32[]{:S(2)}, u32[]{:S(2)}) %collective-permute-start.7) | collective-permute-done | bytes 49184 | tf_op jit(solution)/shard_map/ppermute | solution.py:72
  28.1 1.0 %collective-permute-done.9.refs_4_ = f32[3,2,16,128]{3,2,1,0:T(8,128)S(1)} collective-permute-done((f32[3,2,16,128]{3,2,1,0:T(8,128)S(1)}, f32[3,2,16,128]{3,2,1,0:T(8,128)S(1)}, u32[]{:S(2)}, u32[]{:S(2)}) %collective-permute-start.9) | collective-permute-done | bytes 49184 | tf_op jit(solution)/shard_map/ppermute | solution.py:72
  29.1 1.2 %gram.1 = (f32[16,4096]{1,0:T(8,128)S(1)}, f32[32,4,128]{2,1,0:T(4,128)S(1)}) custom-call(s32[1,2,8]{2,1,0:T(2,128)S(1)} %get-tuple-element.24.send, f32[16,4096]{1,0:T(8,128)S(1)} %get-tuple-element.33.partial_adjoint, f32[1,128]{1,0:T(1,128)S(1)} %get-tuple-element.34.norms, ...), custom_call_target="tpu_custom_call", output_to_operand_aliasing={{0}: (1, {})} | custom-call | tf_op jit(solution)/shard_map/gram/pallas_call | solution.py:357
  30.3 9.9 %all_to_all.5.packed = f32[32,4,128]{2,1,0:T(4,128)S(1)} all-to-all(f32[32,4,128]{2,1,0:T(4,128)S(1)} %get-tuple-element.40), channel_id=1, replica_groups=mesh['dom'=4,'sub'=8] {'dom','sub'}, dimensions={0} | all-to-all | bytes 131072 | tf_op jit(solution)/shard_map/all_to_all | solution.py:364
  40.2 1.7 %solve.1 = (f32[16,4096]{1,0:T(8,128)}, f32[16,16]{1,0:T(8,128)}, f32[1,16]{1,0:T(1,128)}) custom-call(f32[32,4,128]{2,1,0:T(4,128)S(1)} %all_to_all.5.packed, f32[16,4096]{1,0:T(8,128)S(1)} %get-tuple-element.41.adjoint), custom_call_target="tpu_custom_call" | custom-call | tf_op jit(solution)/shard_map/solve/pallas_call | solution.py:366
  (13 shorter events, 0.0 us)
Async XLA Ops:
  0.6 10.0 %copy-start = (bf16[224,128,128]{2,1,0:T(8,128)(2,1)S(1)}, bf16[224,128,128]{2,1,0:T(8,128)(2,1)}, u32[]{:S(2)}) copy-start(bf16[224,128,128]{2,1,0:T(8,128)(2,1)} %blocks.5) | copy-start | bytes 22020100
  1.8 7.1 %collective-permute-start = (bf16[3,2,16,128]{3,2,1,0:T(8,128)(2,1)S(1)}, bf16[3,2,16,128]{3,2,1,0:T(8,128)(2,1)S(1)}, u32[]{:S(2)}, u32[]{:S(2)}) collective-permute-start(bf16[3,2,16,128]{3,2,1,0:T(8,128)(2,1)S(1)} %get-tuple-element.27), channel_id=1, source_target_pairs={{0,1},{1,0},{2,3},{3,2},{4,5},{5,4},{6,7},{7,6},{8,9},{9,8},{10,11... | collective-permute-start | bytes 73736 | tf_op jit(solution)/shard_map/ppermute | solution.py:72
  2.3 8.2 %collective-permute-start.1 = (bf16[3,2,16,128]{3,2,1,0:T(8,128)(2,1)S(1)}, bf16[3,2,16,128]{3,2,1,0:T(8,128)(2,1)S(1)}, u32[]{:S(2)}, u32[]{:S(2)}) collective-permute-start(bf16[3,2,16,128]{3,2,1,0:T(8,128)(2,1)S(1)} %get-tuple-element.28), channel_id=1, source_target_pairs={{0,31},{1,2},{2,1},{3,4},{4,3},{5,6},{6,5},{7,8},{8,7},{9,10},{10,... | collective-permute-start | bytes 73736 | tf_op jit(solution)/shard_map/ppermute | solution.py:72
  8.9 6.2 %collective-permute-start.2 = (bf16[3,2,16,128]{3,2,1,0:T(8,128)(2,1)S(1)}, bf16[3,2,16,128]{3,2,1,0:T(8,128)(2,1)S(1)}, u32[]{:S(2)}, u32[]{:S(2)}) collective-permute-start(bf16[3,2,16,128]{3,2,1,0:T(8,128)(2,1)S(1)} %get-tuple-element.29), channel_id=1, source_target_pairs={{0,7},{1,26},{2,25},{3,28},{4,27},{5,30},{6,29},{7,16},{8,31},{9,1... | collective-permute-start | bytes 73736 | tf_op jit(solution)/shard_map/ppermute | solution.py:72
  8.9 6.2 %collective-permute-start.3 = (bf16[3,2,16,128]{3,2,1,0:T(8,128)(2,1)S(1)}, bf16[3,2,16,128]{3,2,1,0:T(8,128)(2,1)S(1)}, u32[]{:S(2)}, u32[]{:S(2)}) collective-permute-start(bf16[3,2,16,128]{3,2,1,0:T(8,128)(2,1)S(1)} %pad_maximum_fusion.2), channel_id=1, source_target_pairs={{0,24},{1,25},{2,26},{3,27},{4,28},{5,29},{6,30},{7,31},{8,16},{9,... | collective-permute-start | bytes 73736 | tf_op jit(solution)/shard_map/ppermute | solution.py:72
  10.5 4.6 %collective-permute-start.4 = (bf16[3,2,16,128]{3,2,1,0:T(8,128)(2,1)S(1)}, bf16[3,2,16,128]{3,2,1,0:T(8,128)(2,1)S(1)}, u32[]{:S(2)}, u32[]{:S(2)}) collective-permute-start(bf16[3,2,16,128]{3,2,1,0:T(8,128)(2,1)S(1)} %pad_maximum_fusion.3), channel_id=1, source_target_pairs={{0,8},{1,9},{2,10},{3,11},{4,12},{5,13},{6,14},{7,15},{8,0},{9,1},... | collective-permute-start | bytes 73736 | tf_op jit(solution)/shard_map/ppermute | solution.py:72
  17.7 3.6 %collective-permute-start.5 = (f32[3,2,16,128]{3,2,1,0:T(8,128)S(1)}, f32[3,2,16,128]{3,2,1,0:T(8,128)S(1)}, u32[]{:S(2)}, u32[]{:S(2)}) collective-permute-start(f32[3,2,16,128]{3,2,1,0:T(8,128)S(1)} %get-tuple-element.35), channel_id=1, source_target_pairs={{0,1},{1,0},{2,3},{3,2},{4,5},{5,4},{6,7},{7,6},{8,9},{9,8},{10,11... | collective-permute-start | bytes 147464 | tf_op jit(solution)/shard_map/ppermute | solution.py:72
  17.8 7.2 %collective-permute-start.6 = (f32[3,2,16,128]{3,2,1,0:T(8,128)S(1)}, f32[3,2,16,128]{3,2,1,0:T(8,128)S(1)}, u32[]{:S(2)}, u32[]{:S(2)}) collective-permute-start(f32[3,2,16,128]{3,2,1,0:T(8,128)S(1)} %get-tuple-element.36), channel_id=1, source_target_pairs={{0,31},{1,2},{2,1},{3,4},{4,3},{5,6},{6,5},{7,8},{8,7},{9,10},{10,... | collective-permute-start | bytes 147464 | tf_op jit(solution)/shard_map/ppermute | solution.py:72
  21.2 6.8 %collective-permute-start.7 = (f32[3,2,16,128]{3,2,1,0:T(8,128)S(1)}, f32[3,2,16,128]{3,2,1,0:T(8,128)S(1)}, u32[]{:S(2)}, u32[]{:S(2)}) collective-permute-start(f32[3,2,16,128]{3,2,1,0:T(8,128)S(1)} %get-tuple-element.37), channel_id=1, source_target_pairs={{0,7},{1,26},{2,25},{3,28},{4,27},{5,30},{6,29},{7,16},{8,31},{9,1... | collective-permute-start | bytes 147464 | tf_op jit(solution)/shard_map/ppermute | solution.py:72
  21.3 6.8 %collective-permute-start.8 = (f32[3,2,16,128]{3,2,1,0:T(8,128)S(1)}, f32[3,2,16,128]{3,2,1,0:T(8,128)S(1)}, u32[]{:S(2)}, u32[]{:S(2)}) collective-permute-start(f32[3,2,16,128]{3,2,1,0:T(8,128)S(1)} %pad_maximum_fusion), channel_id=1, source_target_pairs={{0,24},{1,25},{2,26},{3,27},{4,28},{5,29},{6,30},{7,31},{8,16},{9,... | collective-permute-start | bytes 147464 | tf_op jit(solution)/shard_map/ppermute | solution.py:72
  25.0 4.1 %collective-permute-start.9 = (f32[3,2,16,128]{3,2,1,0:T(8,128)S(1)}, f32[3,2,16,128]{3,2,1,0:T(8,128)S(1)}, u32[]{:S(2)}, u32[]{:S(2)}) collective-permute-start(f32[3,2,16,128]{3,2,1,0:T(8,128)S(1)} %pad_maximum_fusion.1), channel_id=1, source_target_pairs={{0,8},{1,9},{2,10},{3,11},{4,12},{5,13},{6,14},{7,15},{8,0},{9,1},... | collective-permute-start | bytes 147464 | tf_op jit(solution)/shard_map/ppermute | solution.py:72

commit v9 on v8

--- a/solution.py
+++ b/solution.py
@@ -134,9 +134,12 @@
         )
 
 
-def ghost_kernel(plan, blocks, partial_image, *refs):
+def ghost_kernel(plan_lines, blocks, partial_image, *refs):
     arrived, image, outgoing = refs[:5], refs[5], refs[6:11]
-    ghosts, total, spread, long_rows = refs[11:]
+    ghosts, total, spread, long_rows, plan, sem = refs[11:]
+    load = pltpu.make_async_copy(plan_lines, plan, sem)
+    load.start()
+    spread[...] = jnp.zeros_like(spread)
     rows = image.shape[0]
     many = long_rows.shape[0] - 1
     first_column = rounded(rows + 1)
@@ -145,6 +148,7 @@
         for i, (a, b) in enumerate(offsets):
             for g in range(ref.shape[1]):
                 ghosts[neighbour(a, b) * ref.shape[1] + g] = ref[i, g]
+    load.wait()
     found = 0
     for j in range(rows):
         long_rows[jnp.minimum(found, many)] = j
@@ -164,7 +168,6 @@
         j = long_rows[i]
         total[j] += forward(plan[0, j], SHORT, LONG)
     image[...] = total[...].astype(BF16)
-    spread[...] = jnp.zeros_like(spread)
     banks = spread.shape[0]
 
     def backward(j, first, last):
@@ -335,12 +338,14 @@
         ghost_kernel,
         "ghost",
         [((rows, k, B), BF16)] + [((n, ghost, k, B), F32) for n in sizes],
-        [SMEM] + [VMEM] * 7,
+        [VMEM] * 8,
         scratch=[
             pltpu.VMEM((slots, k, B), BF16),
             pltpu.VMEM((rows, k, B), F32),
-            pltpu.VMEM((4, slots, k, B), F32),
+            pltpu.VMEM((1, slots, k, B), F32),
             pltpu.SMEM((many + 1,), jnp.int32),
+            pltpu.SMEM(plan.shape, jnp.int32),
+            pltpu.SemaphoreType.DMA,
         ],
         flops=4 * (stored - rows * LOCAL) * B * B * k,
         bytes_accessed=4 * (stored - rows * LOCAL) * B * B,

time: 42 us -> 42 us (level)
  no operation moved by 1% of the time
where the time goes in v9:
time: 42 us; the launch traced here: 41.8 us
  starting transfers between devices  13.8 us (33%)
  blocking collectives  9.84 us (23%)
  Pallas kernels  9.52 us (23%)
  waiting for transfers between devices  7.92 us (19%)
  between operations  0.73 us (2%)
    ppermute x10, starting transfers between devices, move(): lax.ppermute(array, AXES, [(d, target(d) % devices) for d in range(device...  13.8 us
    all_to_all x1, blocking collectives, local(): everywhere = lax.all_to_all(packed, AXES, 0, 0)  9.84 us
    ppermute x10, waiting for transfers between devices, move(): lax.ppermute(array, AXES, [(d, target(d) % devices) for d in range(device...  7.92 us
    pallas_call x1, Pallas kernels, local(): call(ghost_kernel, 'ghost', [((rows, k, B), BF16)] + [((n, ghost, k, B),...  2.54 us
    pallas_call x1, Pallas kernels, local(): call(local_forward_kernel, 'local_forward', [((rows, k, B), F32)], [SMEM,...  1.75 us
    pallas_call x1, Pallas kernels, local(): call(functools.partial(solve_kernel, unknowns * devices), 'solve', [((k,...  1.66 us
    pallas_call x1, Pallas kernels, local(): call(local_backward_kernel, 'local_backward', [((k, unknowns), F32), ((1,...  1.21 us
    pallas_call x1, Pallas kernels, local(): call(gram_kernel, 'gram', [((k, unknowns), F32), ((devices, 4, B), F32)],...  1.21 us
  transfers between devices with their start and end apart: 10, of which 4 were waited for; matrix products, arithmetic and copies ran while one was open for 0% of the time, Pallas kernels for 7%

profile of v9, /device:TPU:0, one launch (start us, length us, event | category | flops | bytes accessed | tf_op | source)
XLA Modules:
  0.0 41.8 jit_solution(8955599225525158157)
XLA Ops:
  0.6 1.1 %gather.1 = (bf16[16,4096]{1,0:T(8,128)(2,1)S(1)}, s32[1,384]{1,0:T(1,128)S(1)}, s32[1,2,8]{2,1,0:T(2,128)S(1)}, bf16[3,2,16,128]{3,2,1,0:T(8,128)(2,1)S(1)}, bf...) custom-call(s32[1,2,8]{2,1,0:T(2,128)} %bitcast.2, ...), custom_call_target="tpu_custom_call" | custom-call | tf_op jit(solution)/shard_map/gather/pallas_call | solution.py:315
  1.8 0.5 %collective-permute-start = (bf16[3,2,16,128]{3,2,1,0:T(8,128)(2,1)S(1)}, bf16[3,2,16,128]{3,2,1,0:T(8,128)(2,1)S(1)}, u32[]{:S(2)}, u32[]{:S(2)}) collective-permute-start(bf16[3,2,16,128]{3,2,1,0:T(8,128)(2,1)S(1)} %get-tuple-element.27), channel_id=1, source_target_pairs={{0,1},{1,0},{2,3},{3,2},{4,5},{5,4},{6,7},{7,6},{8,9},{9,8},{10,11... | collective-permute-start | bytes 73736 | tf_op jit(solution)/shard_map/ppermute | solution.py:72
  2.3 6.6 %collective-permute-start.1 = (bf16[3,2,16,128]{3,2,1,0:T(8,128)(2,1)S(1)}, bf16[3,2,16,128]{3,2,1,0:T(8,128)(2,1)S(1)}, u32[]{:S(2)}, u32[]{:S(2)}) collective-permute-start(bf16[3,2,16,128]{3,2,1,0:T(8,128)(2,1)S(1)} %get-tuple-element.28), channel_id=1, source_target_pairs={{0,31},{1,2},{2,1},{3,4},{4,3},{5,6},{6,5},{7,8},{8,7},{9,10},{10,... | collective-permute-start | bytes 73736 | tf_op jit(solution)/shard_map/ppermute | solution.py:72
  8.9 0.0 collective-permute-start.2
  8.9 0.0 collective-permute-done.refs_0_
  8.9 1.6 %collective-permute-start.3 = (bf16[3,2,16,128]{3,2,1,0:T(8,128)(2,1)S(1)}, bf16[3,2,16,128]{3,2,1,0:T(8,128)(2,1)S(1)}, u32[]{:S(2)}, u32[]{:S(2)}) collective-permute-start(bf16[3,2,16,128]{3,2,1,0:T(8,128)(2,1)S(1)} %pad_maximum_fusion.2), channel_id=1, source_target_pairs={{0,24},{1,25},{2,26},{3,27},{4,28},{5,29},{6,30},{7,31},{8,16},{9,... | collective-permute-start | bytes 73736 | tf_op jit(solution)/shard_map/ppermute | solution.py:72
  10.5 0.1 collective-permute-start.4
  10.6 1.8 %local_forward.1.partial_image = f32[32,16,128]{2,1,0:T(8,128)S(1)} custom-call(s32[1,384]{1,0:T(1,128)S(1)} %get-tuple-element.25.plan.plan_lines, bf16[16,4096]{1,0:T(8,128)(2,1)S(1)} %get-tuple-element.26.vectors, bf16[224,128,128]{2,1,0:T(8,128)(2,1)S(1)} %copy-done), custom_call_target="tpu_custom_call" | custom-call | flops 50331648 | bytes 3145728 | tf_op jit(solution)/shard_map/local_forward/pallas_call | solution.py:329
  12.4 2.8 %collective-permute-done.2.refs_2_ = bf16[3,2,16,128]{3,2,1,0:T(8,128)(2,1)S(1)} collective-permute-done((bf16[3,2,16,128]{3,2,1,0:T(8,128)(2,1)S(1)}, bf16[3,2,16,128]{3,2,1,0:T(8,128)(2,1)S(1)}, u32[]{:S(2)}, u32[]{:S(2)}) %collective-permute-start.2) | collective-permute-done | bytes 24608 | tf_op jit(solution)/shard_map/ppermute | solution.py:72
  15.1 0.0 collective-permute-done.3.refs_3_
  15.1 0.0 collective-permute-done.4.refs_4_
  15.1 2.5 %ghost.1 = (bf16[32,16,128]{2,1,0:T(8,128)(2,1)S(1)}, f32[3,2,16,128]{3,2,1,0:T(8,128)S(1)}, f32[3,2,16,128]{3,2,1,0:T(8,128)S(1)}, f32[3,2,16,128]{3,2,1,0:T(8,...) custom-call(s32[1,384]{1,0:T(1,128)S(1)} %get-tuple-element.25.plan.plan_lines, ...), custom_call_target="tpu_custom_call" | custom-call | flops 134217728 | bytes 8388608 | tf_op jit(solution)/shard_map/ghost/pallas_call | solution.py:337
  17.7 0.1 collective-permute-start.5
  17.8 3.5 %collective-permute-start.6 = (f32[3,2,16,128]{3,2,1,0:T(8,128)S(1)}, f32[3,2,16,128]{3,2,1,0:T(8,128)S(1)}, u32[]{:S(2)}, u32[]{:S(2)}) collective-permute-start(f32[3,2,16,128]{3,2,1,0:T(8,128)S(1)} %get-tuple-element.36), channel_id=1, source_target_pairs={{0,31},{1,2},{2,1},{3,4},{4,3},{5,6},{6,5},{7,8},{8,7},{9,10},{10,... | collective-permute-start | bytes 147464 | tf_op jit(solution)/shard_map/ppermute | solution.py:72
  21.2 0.0 collective-permute-start.7
  21.3 1.4 %collective-permute-start.8 = (f32[3,2,16,128]{3,2,1,0:T(8,128)S(1)}, f32[3,2,16,128]{3,2,1,0:T(8,128)S(1)}, u32[]{:S(2)}, u32[]{:S(2)}) collective-permute-start(f32[3,2,16,128]{3,2,1,0:T(8,128)S(1)} %pad_maximum_fusion), channel_id=1, source_target_pairs={{0,24},{1,25},{2,26},{3,27},{4,28},{5,29},{6,30},{7,31},{8,16},{9,... | collective-permute-start | bytes 147464 | tf_op jit(solution)/shard_map/ppermute | solution.py:72
  22.7 2.3 %collective-permute-done.6.refs_1_ = f32[3,2,16,128]{3,2,1,0:T(8,128)S(1)} collective-permute-done((f32[3,2,16,128]{3,2,1,0:T(8,128)S(1)}, f32[3,2,16,128]{3,2,1,0:T(8,128)S(1)}, u32[]{:S(2)}, u32[]{:S(2)}) %collective-permute-start.6) | collective-permute-done | bytes 49184 | tf_op jit(solution)/shard_map/ppermute | solution.py:72
  24.9 0.1 collective-permute-start.9
  25.0 1.2 %local_backward.1 = (f32[16,4096]{1,0:T(8,128)S(1)}, f32[1,128]{1,0:T(1,128)S(1)}) custom-call(s32[1,384]{1,0:T(1,128)S(1)} %get-tuple-element.25.plan.plan_lines, bf16[224,128,128]{2,1,0:T(8,128)(2,1)S(1)} %copy-done, bf16[32,16,128]{2,1,0:T(8,128)(2,1)S(1)} %get-tuple-element.32.image), custom_call_target="tpu_custom_call" | custom-call | flops 50331648 | bytes 3145728 | tf_op jit(solution)/shard_map/local_backward/pallas_call | solution.py:354
  26.2 1.8 %collective-permute-done.7.refs_2_ = f32[3,2,16,128]{3,2,1,0:T(8,128)S(1)} collective-permute-done((f32[3,2,16,128]{3,2,1,0:T(8,128)S(1)}, f32[3,2,16,128]{3,2,1,0:T(8,128)S(1)}, u32[]{:S(2)}, u32[]{:S(2)}) %collective-permute-start.7) | collective-permute-done | bytes 49184 | tf_op jit(solution)/shard_map/ppermute | solution.py:72
  28.1 1.0 %collective-permute-done.9.refs_4_ = f32[3,2,16,128]{3,2,1,0:T(8,128)S(1)} collective-permute-done((f32[3,2,16,128]{3,2,1,0:T(8,128)S(1)}, f32[3,2,16,128]{3,2,1,0:T(8,128)S(1)}, u32[]{:S(2)}, u32[]{:S(2)}) %collective-permute-start.9) | collective-permute-done | bytes 49184 | tf_op jit(solution)/shard_map/ppermute | solution.py:72
  29.1 1.2 %gram.1 = (f32[16,4096]{1,0:T(8,128)S(1)}, f32[32,4,128]{2,1,0:T(4,128)S(1)}) custom-call(s32[1,2,8]{2,1,0:T(2,128)S(1)} %get-tuple-element.24.send, f32[16,4096]{1,0:T(8,128)S(1)} %get-tuple-element.33.partial_adjoint, f32[1,128]{1,0:T(1,128)S(1)} %get-tuple-element.34.norms, ...), custom_call_target="tpu_custom_call", output_to_operand_aliasing={{0}: (1, {})} | custom-call | tf_op jit(solution)/shard_map/gram/pallas_call | solution.py:362
  30.3 9.8 %all_to_all.5.packed = f32[32,4,128]{2,1,0:T(4,128)S(1)} all-to-all(f32[32,4,128]{2,1,0:T(4,128)S(1)} %get-tuple-element.40), channel_id=1, replica_groups=mesh['dom'=4,'sub'=8] {'dom','sub'}, dimensions={0} | all-to-all | bytes 131072 | tf_op jit(solution)/shard_map/all_to_all | solution.py:369
  40.1 1.7 %solve.1 = (f32[16,4096]{1,0:T(8,128)}, f32[16,16]{1,0:T(8,128)}, f32[1,16]{1,0:T(1,128)}) custom-call(f32[32,4,128]{2,1,0:T(4,128)S(1)} %all_to_all.5.packed, f32[16,4096]{1,0:T(8,128)S(1)} %get-tuple-element.41.adjoint), custom_call_target="tpu_custom_call" | custom-call | tf_op jit(solution)/shard_map/solve/pallas_call | solution.py:371
  (13 shorter events, 0.0 us)
Async XLA Ops:
  0.6 10.0 %copy-start = (bf16[224,128,128]{2,1,0:T(8,128)(2,1)S(1)}, bf16[224,128,128]{2,1,0:T(8,128)(2,1)}, u32[]{:S(2)}) copy-start(bf16[224,128,128]{2,1,0:T(8,128)(2,1)} %blocks.5) | copy-start | bytes 22020100
  1.8 7.1 %collective-permute-start = (bf16[3,2,16,128]{3,2,1,0:T(8,128)(2,1)S(1)}, bf16[3,2,16,128]{3,2,1,0:T(8,128)(2,1)S(1)}, u32[]{:S(2)}, u32[]{:S(2)}) collective-permute-start(bf16[3,2,16,128]{3,2,1,0:T(8,128)(2,1)S(1)} %get-tuple-element.27), channel_id=1, source_target_pairs={{0,1},{1,0},{2,3},{3,2},{4,5},{5,4},{6,7},{7,6},{8,9},{9,8},{10,11... | collective-permute-start | bytes 73736 | tf_op jit(solution)/shard_map/ppermute | solution.py:72
  2.3 8.2 %collective-permute-start.1 = (bf16[3,2,16,128]{3,2,1,0:T(8,128)(2,1)S(1)}, bf16[3,2,16,128]{3,2,1,0:T(8,128)(2,1)S(1)}, u32[]{:S(2)}, u32[]{:S(2)}) collective-permute-start(bf16[3,2,16,128]{3,2,1,0:T(8,128)(2,1)S(1)} %get-tuple-element.28), channel_id=1, source_target_pairs={{0,31},{1,2},{2,1},{3,4},{4,3},{5,6},{6,5},{7,8},{8,7},{9,10},{10,... | collective-permute-start | bytes 73736 | tf_op jit(solution)/shard_map/ppermute | solution.py:72
  8.9 6.2 %collective-permute-start.2 = (bf16[3,2,16,128]{3,2,1,0:T(8,128)(2,1)S(1)}, bf16[3,2,16,128]{3,2,1,0:T(8,128)(2,1)S(1)}, u32[]{:S(2)}, u32[]{:S(2)}) collective-permute-start(bf16[3,2,16,128]{3,2,1,0:T(8,128)(2,1)S(1)} %get-tuple-element.29), channel_id=1, source_target_pairs={{0,7},{1,26},{2,25},{3,28},{4,27},{5,30},{6,29},{7,16},{8,31},{9,1... | collective-permute-start | bytes 73736 | tf_op jit(solution)/shard_map/ppermute | solution.py:72
  8.9 6.2 %collective-permute-start.3 = (bf16[3,2,16,128]{3,2,1,0:T(8,128)(2,1)S(1)}, bf16[3,2,16,128]{3,2,1,0:T(8,128)(2,1)S(1)}, u32[]{:S(2)}, u32[]{:S(2)}) collective-permute-start(bf16[3,2,16,128]{3,2,1,0:T(8,128)(2,1)S(1)} %pad_maximum_fusion.2), channel_id=1, source_target_pairs={{0,24},{1,25},{2,26},{3,27},{4,28},{5,29},{6,30},{7,31},{8,16},{9,... | collective-permute-start | bytes 73736 | tf_op jit(solution)/shard_map/ppermute | solution.py:72
  10.5 4.6 %collective-permute-start.4 = (bf16[3,2,16,128]{3,2,1,0:T(8,128)(2,1)S(1)}, bf16[3,2,16,128]{3,2,1,0:T(8,128)(2,1)S(1)}, u32[]{:S(2)}, u32[]{:S(2)}) collective-permute-start(bf16[3,2,16,128]{3,2,1,0:T(8,128)(2,1)S(1)} %pad_maximum_fusion.3), channel_id=1, source_target_pairs={{0,8},{1,9},{2,10},{3,11},{4,12},{5,13},{6,14},{7,15},{8,0},{9,1},... | collective-permute-start | bytes 73736 | tf_op jit(solution)/shard_map/ppermute | solution.py:72
  17.7 3.6 %collective-permute-start.5 = (f32[3,2,16,128]{3,2,1,0:T(8,128)S(1)}, f32[3,2,16,128]{3,2,1,0:T(8,128)S(1)}, u32[]{:S(2)}, u32[]{:S(2)}) collective-permute-start(f32[3,2,16,128]{3,2,1,0:T(8,128)S(1)} %get-tuple-element.35), channel_id=1, source_target_pairs={{0,1},{1,0},{2,3},{3,2},{4,5},{5,4},{6,7},{7,6},{8,9},{9,8},{10,11... | collective-permute-start | bytes 147464 | tf_op jit(solution)/shard_map/ppermute | solution.py:72
  17.8 7.2 %collective-permute-start.6 = (f32[3,2,16,128]{3,2,1,0:T(8,128)S(1)}, f32[3,2,16,128]{3,2,1,0:T(8,128)S(1)}, u32[]{:S(2)}, u32[]{:S(2)}) collective-permute-start(f32[3,2,16,128]{3,2,1,0:T(8,128)S(1)} %get-tuple-element.36), channel_id=1, source_target_pairs={{0,31},{1,2},{2,1},{3,4},{4,3},{5,6},{6,5},{7,8},{8,7},{9,10},{10,... | collective-permute-start | bytes 147464 | tf_op jit(solution)/shard_map/ppermute | solution.py:72
  21.2 6.8 %collective-permute-start.7 = (f32[3,2,16,128]{3,2,1,0:T(8,128)S(1)}, f32[3,2,16,128]{3,2,1,0:T(8,128)S(1)}, u32[]{:S(2)}, u32[]{:S(2)}) collective-permute-start(f32[3,2,16,128]{3,2,1,0:T(8,128)S(1)} %get-tuple-element.37), channel_id=1, source_target_pairs={{0,7},{1,26},{2,25},{3,28},{4,27},{5,30},{6,29},{7,16},{8,31},{9,1... | collective-permute-start | bytes 147464 | tf_op jit(solution)/shard_map/ppermute | solution.py:72
  21.3 6.8 %collective-permute-start.8 = (f32[3,2,16,128]{3,2,1,0:T(8,128)S(1)}, f32[3,2,16,128]{3,2,1,0:T(8,128)S(1)}, u32[]{:S(2)}, u32[]{:S(2)}) collective-permute-start(f32[3,2,16,128]{3,2,1,0:T(8,128)S(1)} %pad_maximum_fusion), channel_id=1, source_target_pairs={{0,24},{1,25},{2,26},{3,27},{4,28},{5,29},{6,30},{7,31},{8,16},{9,... | collective-permute-start | bytes 147464 | tf_op jit(solution)/shard_map/ppermute | solution.py:72
  24.9 4.1 %collective-permute-start.9 = (f32[3,2,16,128]{3,2,1,0:T(8,128)S(1)}, f32[3,2,16,128]{3,2,1,0:T(8,128)S(1)}, u32[]{:S(2)}, u32[]{:S(2)}) collective-permute-start(f32[3,2,16,128]{3,2,1,0:T(8,128)S(1)} %pad_maximum_fusion.1), channel_id=1, source_target_pairs={{0,8},{1,9},{2,10},{3,11},{4,12},{5,13},{6,14},{7,15},{8,0},{9,1},... | collective-permute-start | bytes 147464 | tf_op jit(solution)/shard_map/ppermute | solution.py:72
